TPU v7x, 32 devices: a whole 2x2x4 slice. The times are simulated.
32 devices in a mesh: dp: 8 (over z, y), pair: 4 (over x, core).
Axes of the slice: x: 2, y: 2, z: 4, core: 2. Of those that a mesh axis runs over, the one named last changes fastest.
Arguments:
- student_image: bfloat16 [8192, 512], P(('dp', 'pair')), may hold values from -60 to 60
- student_text: bfloat16 [8192, 512], P(('dp', 'pair')), may hold values from -6 to 6
- teacher_image: bfloat16 [8192, 1280], P(('dp', 'pair')), may hold values from -60 to 60
- teacher_text: bfloat16 [8192, 1280], P(('dp', 'pair')), may hold values from -6 to 6
Outputs:
- grad_image: float32 [8192, 512], P(('dp', 'pair'))
- grad_text: float32 [8192, 512], P(('dp', 'pair'))
All inputs are finite; a program needn't handle non-finite values.
Results may differ from a plain program's by a relative error of at most 0.0025.
Values may be sent and summed in bfloat16 or wider, within the bound.
No kernel may reach another device: no remote copies, remote signals or barrier semaphores. Data moves between devices by JAX's collectives and lax.ppermute only.
A program may use at most 128 MiB of HBM per device.

v0:
```python
import math

import jax
import jax.numpy as jnp
from jax import lax
from jax.sharding import PartitionSpec as P

WINDOW = 4


def from_behind(value, axis, steps):
    count = lax.axis_size(axis)
    pairs = [(source, (source + steps) % count) for source in range(count)]
    return lax.ppermute(value, axis, pairs)


def combined_all(value, axis, join):
    pieces = jax.tree.map(lambda part: lax.all_gather(part, axis), value)
    head = jax.tree.map(lambda part: part[0], pieces)
    tail = jax.tree.map(lambda part: part[1:], pieces)
    subtotal, _ = lax.scan(lambda subtotal, section: (join(subtotal, section), None), head, tail)
    return subtotal


def stats_of(scores, axis):
    top = jnp.max(scores, axis=axis)
    total = jnp.sum(jnp.exp(scores - jnp.expand_dims(top, axis)), axis=axis)
    return (top, total)


def combine_stats(first, second):
    result = []
    for offset in (0, 2):
        top = jnp.maximum(first[offset], second[offset])
        total = first[offset + 1] * jnp.exp(first[offset] - top) + second[offset + 1] * jnp.exp(
            second[offset] - top
        )
        result += [top, total]
    return tuple(result)


def as_tuple(stacked):
    return (stacked[0], stacked[1], stacked[2], stacked[3])


def weight_tile(s_tile, t_tile, row_stats, col_stats):
    rm_s, rz_s, rm_t, rz_t = row_stats
    cm_s, cz_s, cm_t, cz_t = col_stats
    return (
        jnp.exp(s_tile - rm_s[:, None]) / rz_s[:, None]
        - jnp.exp(t_tile - rm_t[:, None]) / rz_t[:, None]
        + jnp.exp(s_tile - cm_s[None, :]) / cz_s[None, :]
        - jnp.exp(t_tile - cm_t[None, :]) / cz_t[None, :]
    ).astype(jnp.bfloat16)


def on_device(student_image, student_text, teacher_image, teacher_text):
    width_s = student_image.shape[1]
    scale_s = 2.0 / math.sqrt(width_s)
    scale_t = 2.0 / math.sqrt(teacher_image.shape[1])
    shard_len = student_image.shape[0]
    block_len = shard_len * lax.axis_size("pair")
    both_text = jnp.concatenate([student_text, teacher_text], axis=1)
    image_s, image_t = (student_image, teacher_image)
    own_block = lax.all_gather(both_text, "pair", axis=0, tiled=True)
    blocks = [own_block]
    for step in range(1, WINDOW):
        blocks.append(from_behind(own_block, "dp", -step))
    partners = jnp.concatenate(blocks, axis=0)
    part_s = partners[:, :width_s]
    part_t = partners[:, width_s:]
    dims = (((1,), (1,)), ((), ()))
    s_tile = lax.dot_general(image_s, part_s, dims, preferred_element_type=jnp.float32) * scale_s
    t_tile = lax.dot_general(image_t, part_t, dims, preferred_element_type=jnp.float32) * scale_t
    row_stats = stats_of(s_tile, 1) + stats_of(t_tile, 1)
    col_local = stats_of(s_tile, 0) + stats_of(t_tile, 0)
    col_block = combined_all(col_local, "pair", combine_stats)
    stacked = jnp.stack(col_block, axis=0).reshape(4, WINDOW, block_len)
    home = as_tuple(stacked[:, 0])
    for step in range(1, WINDOW):
        arrived = from_behind(stacked[:, step], "dp", step)
        home = combine_stats(home, as_tuple(arrived))
    home_all = jnp.stack(home, axis=0)
    pieces = [home_all]
    for step in range(1, WINDOW):
        pieces.append(from_behind(home_all, "dp", -step))
    band_stats = jnp.concatenate(pieces, axis=1)
    col_stats = as_tuple(band_stats)
    weights = weight_tile(s_tile, t_tile, row_stats, col_stats)
    image_terms = jnp.dot(weights, part_s, preferred_element_type=jnp.float32)
    text_part = lax.dot_general(
        weights, image_s, (((0,), (0,)), ((), ())), preferred_element_type=jnp.float32
    )
    grad_image = image_terms * scale_s
    text_home = text_part[:block_len]
    for step in range(1, WINDOW):
        text_home = text_home + from_behind(
            text_part[step * block_len : (step + 1) * block_len], "dp", step
        )
    grad_text = lax.psum_scatter(text_home, "pair", scatter_dimension=0, tiled=True) * scale_s
    return (grad_image, grad_text)


def solution(mesh):
    return jax.shard_map(
        on_device,
        mesh=mesh,
        in_specs=(
            P(("dp", "pair"), None),
            P(("dp", "pair"), None),
            P(("dp", "pair"), None),
            P(("dp", "pair"), None),
        ),
        out_specs=(P(("dp", "pair"), None), P(("dp", "pair"), None)),
        check_vma=False,
    )
```

profile of v0, /device:TPU:0, one launch (start us, length us, event | category | flops | bytes accessed | tf_op | source)
XLA Modules:
  0.0 644.6 jit_solution(3145536718647154412)
XLA Ops:
  7.2 0.0 all-gather.6.cloned.1.call-start
  7.2 2.2 pad_maximum_fusion
  9.4 0.0 all-gather.6.cloned.1.call-update
  9.5 0.0 reduce-scatter.2.cloned.1.call-start
  9.5 34.3 %all-gather.6.cloned.1.call-done = bf16[1024,1792]{1,0:T(8,128)(2,1)} async-done(((bf16[256,1792]{1,0:T(8,128)(2,1)}), bf16[1024,1792]{1,0:T(8,128)(2,1)}) %all-gather.6.cloned.1.call-update) | async-done | bytes 3670032 | tf_op jit(solution)/shard_map/all_gather | solution.py:65
  43.8 4.2 collective-permute-start
  48.1 0.5 collective-permute-start.1
  48.6 2.3 constant_dynamic-update-slice_fusion.3
  50.9 77.2 %collective-permute-done = bf16[1024,1792]{1,0:T(8,128)(2,1)} collective-permute-done((bf16[1024,1792]{1,0:T(8,128)(2,1)}, bf16[1024,1792]{1,0:T(8,128)(2,1)}, u32[]{:S(2)}, u32[]{:S(2)}) %collective-permute-start) | collective-permute-done | bytes 3670048 | tf_op jit(solution)/shard_map/ppermute | solution.py:14
  128.1 2.3 constant_dynamic-update-slice_fusion.2
  130.4 76.4 %collective-permute-done.1 = bf16[1024,1792]{1,0:T(8,128)(2,1)} collective-permute-done((bf16[1024,1792]{1,0:T(8,128)(2,1)}, bf16[1024,1792]{1,0:T(8,128)(2,1)}, u32[]{:S(2)}, u32[]{:S(2)}) %collective-permute-start.1) | collective-permute-done | bytes 3670048 | tf_op jit(solution)/shard_map/ppermute | solution.py:14
  206.8 2.3 constant_dynamic-update-slice_fusion.1
  209.0 75.7 %collective-permute-done.2 = bf16[1024,1792]{1,0:T(8,128)(2,1)} collective-permute-done((bf16[1024,1792]{1,0:T(8,128)(2,1)}, bf16[1024,1792]{1,0:T(8,128)(2,1)}, u32[]{:S(2)}, u32[]{:S(2)}) %collective-permute-start.2) | collective-permute-done | bytes 3670048 | tf_op jit(solution)/shard_map/ppermute | solution.py:14
  284.7 2.3 constant_dynamic-update-slice_fusion
  287.0 3.0 fusion.30
  290.0 1.8 fusion.5
  291.8 5.2 all-gather.3
  297.1 1.4 fusion.29
  298.5 2.0 copy-done.3
  300.5 1.9 fusion.6
  302.4 5.2 all-gather.1
  307.6 5.2 all-gather
  312.8 5.2 all-gather.2
  318.2 0.5 while.16
  318.9 80.2 %collective-permute-start.3 = (f32[4,1024]{1,0:T(4,128)S(1)}, f32[4,1024]{1,0:T(4,128)S(1)}, u32[]{:S(2)}, u32[]{:S(2)}) collective-permute-start(f32[4,1024]{1,0:T(4,128)S(1)} %bitcast.72), channel_id=1, source_target_pairs={{0,4},{4,8},{8,12},{12,16},{16,20},{20,24},{24,28},{28,0},{1,5},{5... | collective-permute-start | bytes 49160 | tf_op jit(solution)/shard_map/ppermute | solution.py:14
  399.1 0.1 collective-permute-start.5
  399.2 5.4 collective-permute-done.3
  404.5 0.5 collective-permute-done.4
  405.0 0.1 collective-permute-done.5
  405.1 0.1 fusion.21
  405.3 3.3 collective-permute-start.6
  408.5 1.1 collective-permute-start.7
  409.6 1.4 collective-permute-start.8
  411.0 1.2 collective-permute-done.7
  412.3 2.0 collective-permute-done.8
  414.4 7.4 %subtract_convert_fusion = bf16[4096,256]{1,0:T(8,128)(2,1)S(1)} fusion(f32[4096,256]{1,0:T(8,128)} %copy-done.2, f32[4096,256]{1,0:T(8,128)} %copy-done.3, f32[4096]{0:T(1024)S(1)} %bitcast.69, f32[4096]{0:T(1024)S(1)} %bitcast.70, f32[4096]{0:T(1024)S(1)} %bitcast.71, f32[4096]{0:T(1024)S(1)} %bitcast.68, f32[256]{0:T(256)S(1)} %get-tuple-element.60, ...), kind=kLoop, calls=%fused_computation.10 | loop fusion | flops 12582912 | bytes 10555392 | tf_op jit(solution)/shard_map/convert_element_type | solution.py:54
  421.8 1.2 fusion.34
  423.0 0.7 fusion.31
  423.8 1.0 collective-permute-start.10
  424.7 1.9 collective-permute-start.11
  426.7 2.4 collective-permute-start.9
  429.1 45.1 %collective-permute-done.10 = f32[1024,512]{1,0:T(8,128)S(1)} collective-permute-done((f32[1024,512]{1,0:T(8,128)S(1)}, f32[1024,512]{1,0:T(8,128)S(1)}, u32[]{:S(2)}, u32[]{:S(2)}) %collective-permute-start.10) | collective-permute-done | bytes 2097184 | tf_op jit(solution)/shard_map/ppermute | solution.py:14
  474.2 131.4 %collective-permute-done.11 = f32[1024,512]{1,0:T(8,128)S(1)} collective-permute-done((f32[1024,512]{1,0:T(8,128)S(1)}, f32[1024,512]{1,0:T(8,128)S(1)}, u32[]{:S(2)}, u32[]{:S(2)}) %collective-permute-start.11) | collective-permute-done | bytes 2097184 | tf_op jit(solution)/shard_map/ppermute | solution.py:14
  605.6 2.3 fusion.11
  607.9 0.0 reduce-scatter.2.cloned.1.call-update
  607.9 4.6 fusion.12
  612.6 23.3 %reduce-scatter.2.cloned.1.call-done = f32[256,512]{1,0:T(8,128)} async-done(((f32[1024,512]{1,0:T(8,128)}), f32[256,512]{1,0:T(8,128)}) %reduce-scatter.2.cloned.1.call-update) | async-done | bytes 524304 | tf_op jit(solution)/shard_map/reduce_scatter | solution.py:100
  635.8 1.9 broadcast_multiply_fusion
  (61 shorter events, 0.7 us)
Async XLA Ops:
  7.2 279.8 %copy-start = (bf16[256,1280]{1,0:T(8,128)(2,1)S(1)}, bf16[256,1280]{1,0:T(8,128)(2,1)}, u32[]{:S(2)}) copy-start(bf16[256,1280]{1,0:T(8,128)(2,1)} %param.8) | copy-start | bytes 1966084
  7.2 36.6 %all-gather.6.cloned.1.call-start = ((), (), s32[]{:S(2)}) async-start(), calls=%async_computation.1 | async-start | bytes 4587520 | tf_op jit(solution)/shard_map/all_gather | solution.py:65
  9.5 626.4 %reduce-scatter.2.cloned.1.call-start = ((), (), s32[]{:S(2)}) async-start(), calls=%async_computation.2 | async-start | bytes 2621440 | tf_op jit(solution)/shard_map/reduce_scatter | solution.py:100
  43.8 84.3 %collective-permute-start = (bf16[1024,1792]{1,0:T(8,128)(2,1)}, bf16[1024,1792]{1,0:T(8,128)(2,1)}, u32[]{:S(2)}, u32[]{:S(2)}) collective-permute-start(bf16[1024,1792]{1,0:T(8,128)(2,1)} %all-gather.6.cloned.1.call-done), channel_id=1, source_target_pairs={{0,28},{4,0},{8,4},{12,8},{16,12},{20,16},{24,20},{28,24},{1,29},{... | collective-permute-start | bytes 11010056 | tf_op jit(solution)/shard_map/ppermute | solution.py:14
  48.1 158.7 %collective-permute-start.1 = (bf16[1024,1792]{1,0:T(8,128)(2,1)}, bf16[1024,1792]{1,0:T(8,128)(2,1)}, u32[]{:S(2)}, u32[]{:S(2)}) collective-permute-start(bf16[1024,1792]{1,0:T(8,128)(2,1)} %all-gather.6.cloned.1.call-done), channel_id=1, source_target_pairs={{0,24},{4,28},{8,0},{12,4},{16,8},{20,12},{24,16},{28,20},{1,25},{... | collective-permute-start | bytes 11010056 | tf_op jit(solution)/shard_map/ppermute | solution.py:14
  48.6 236.1 %collective-permute-start.2 = (bf16[1024,1792]{1,0:T(8,128)(2,1)}, bf16[1024,1792]{1,0:T(8,128)(2,1)}, u32[]{:S(2)}, u32[]{:S(2)}) collective-permute-start(bf16[1024,1792]{1,0:T(8,128)(2,1)} %all-gather.6.cloned.1.call-done), channel_id=1, source_target_pairs={{0,20},{4,24},{8,28},{12,0},{16,4},{20,8},{24,12},{28,16},{1,21},{... | collective-permute-start | bytes 11010056 | tf_op jit(solution)/shard_map/ppermute | solution.py:14
  287.0 10.1 %copy-start.4 = (bf16[4096,1792]{1,0:T(8,128)(2,1)}, bf16[4096,1792]{1,0:T(8,128)(2,1)S(1)}, u32[]{:S(2)}) copy-start(bf16[4096,1792]{1,0:T(8,128)(2,1)S(1)} %constant_dynamic-update-slice_fusion) | copy-start | bytes 44040196
  290.0 8.4 %copy-start.2 = (f32[4096,256]{1,0:T(8,128)}, f32[4096,256]{1,0:T(8,128)S(1)}, u32[]{:S(2)}) copy-start(f32[4096,256]{1,0:T(8,128)S(1)} %get-tuple-element.105) | copy-start | bytes 12582916
  290.0 7.1 %copy-start.6 = (bf16[256,512]{1,0:T(8,128)(2,1)S(1)}, bf16[256,512]{1,0:T(8,128)(2,1)}, u32[]{:S(2)}) copy-start(bf16[256,512]{1,0:T(8,128)(2,1)} %param.6) | copy-start | bytes 786436
  297.1 1.4 copy-start.5
  298.5 2.0 copy-start.3
  298.5 19.6 %slice-start = ((f32[16384]{0:T(1024)}), f32[12288]{0:T(1024)S(1)}, s32[]{:S(2)}) async-start(f32[16384]{0:T(1024)} %copy-done.5), calls=%async_computation.3 | async-start | bytes 98304 | tf_op jit(solution)/shard_map/slice | solution.py:20
  298.5 19.7 %slice-start.1 = ((f32[16384]{0:T(1024)}), f32[4096]{0:T(1024)S(1)}, s32[]{:S(2)}) async-start(f32[16384]{0:T(1024)} %copy-done.5), calls=%async_computation.4 | async-start | bytes 32768 | tf_op jit(solution)/shard_map/slice | solution.py:19
  318.9 85.7 %collective-permute-start.3 = (f32[4,1024]{1,0:T(4,128)S(1)}, f32[4,1024]{1,0:T(4,128)S(1)}, u32[]{:S(2)}, u32[]{:S(2)}) collective-permute-start(f32[4,1024]{1,0:T(4,128)S(1)} %bitcast.72), channel_id=1, source_target_pairs={{0,4},{4,8},{8,12},{12,16},{16,20},{20,24},{24,28},{28,0},{1,5},{5... | collective-permute-start | bytes 49160 | tf_op jit(solution)/shard_map/ppermute | solution.py:14
  399.1 5.9 collective-permute-start.4
  399.1 6.0 collective-permute-start.5
  405.3 5.8 collective-permute-start.6
  408.5 3.7 collective-permute-start.7
  409.6 4.6 collective-permute-start.8
  423.8 50.4 %collective-permute-start.10 = (f32[1024,512]{1,0:T(8,128)S(1)}, f32[1024,512]{1,0:T(8,128)S(1)}, u32[]{:S(2)}, u32[]{:S(2)}) collective-permute-start(f32[1024,512]{1,0:T(8,128)S(1)} %get-tuple-element.94), channel_id=1, source_target_pairs={{0,8},{4,12},{8,16},{12,20},{16,24},{20,28},{24,0},{28,4},{1,9},{5... | collective-permute-start | bytes 6291464 | tf_op jit(solution)/shard_map/ppermute | solution.py:14
  424.7 180.8 %collective-permute-start.11 = (f32[1024,512]{1,0:T(8,128)S(1)}, f32[1024,512]{1,0:T(8,128)S(1)}, u32[]{:S(2)}, u32[]{:S(2)}) collective-permute-start(f32[1024,512]{1,0:T(8,128)S(1)} %get-tuple-element.93), channel_id=1, source_target_pairs={{0,12},{4,16},{8,20},{12,24},{16,28},{20,0},{24,4},{28,8},{1,13},{... | collective-permute-start | bytes 6291464 | tf_op jit(solution)/shard_map/ppermute | solution.py:14
  426.7 178.9 %collective-permute-start.9 = (f32[1024,512]{1,0:T(8,128)S(1)}, f32[1024,512]{1,0:T(8,128)S(1)}, u32[]{:S(2)}, u32[]{:S(2)}) collective-permute-start(f32[1024,512]{1,0:T(8,128)S(1)} %get-tuple-element.92), channel_id=1, source_target_pairs={{0,4},{4,8},{8,12},{12,16},{16,20},{20,24},{24,28},{28,0},{1,5},{5... | collective-permute-start | bytes 6291464 | tf_op jit(solution)/shard_map/ppermute | solution.py:14
  607.9 29.8 %copy-start.1 = (bf16[256,1280]{1,0:T(8,128)(2,1)S(1)}, bf16[256,1280]{1,0:T(8,128)(2,1)}, u32[]{:S(2)}) copy-start(bf16[256,1280]{1,0:T(8,128)(2,1)} %param.8) | copy-start | bytes 1966084
Sparse Core Ops, SparseCore 0:
  9.6 34.1 all-gather.5
  608.0 27.7 reduce-scatter.1
where the time goes:
time: 645 us
  waiting for transfers between devices  473 us (73%)
  starting transfers between devices  96.2 us (15%)
  blocking collectives  21 us (3%)
  other arithmetic  17.7 us (3%)
  between operations  14.3 us (2%)
  local copies, waits for them, and re-layouts  12.5 us (2%)
  matrix products  10.3 us (2%)
    ppermute x12, waiting for transfers between devices, from_behind(): return lax.ppermute(value, axis, pairs)  415 us
    ppermute x12, starting transfers between devices, from_behind(): return lax.ppermute(value, axis, pairs)  96.1 us
    all_gather x1, waiting for transfers between devices, on_device(): own_block = lax.all_gather(both_text, 'pair', axis=0, tiled=True)  34.3 us
    reduce_scatter x1, waiting for transfers between devices, on_device(): lax.psum_scatter(text_home, 'pair', scatter_dimension=0, tiled=True)  23.3 us
    all_gather x4, blocking collectives, combined_all(): pieces = jax.tree.map(lambda part: lax.all_gather(part, axis), value)  21 us
  transfers between devices with their start and end apart: 14, of which 12 were waited for; matrix products, arithmetic and copies ran while one was open for 2% of the time, Pallas kernels for 0%

commit v1 on v0

v1 whole, which is shorter than its diff:
```python
import math

import jax
import jax.numpy as jnp
from jax import lax
from jax.experimental import pallas as pl
from jax.experimental.pallas import tpu as pltpu
from jax.sharding import PartitionSpec as P

AXES = ("dp", "pair")
MIB = 1024 * 1024
LOG2E = math.log2(math.e)
HEAVY = pl.CostEstimate(flops=10**11, bytes_accessed=10**9, transcendentals=0)
LIGHT = pl.CostEstimate(flops=3 * 10**9, bytes_accessed=3 * 10**7, transcendentals=0)


def send_to(value, place):
    count = lax.axis_size("dp")
    pairs = []
    for block in range(count):
        for member in range(4):
            to_block, to_x, to_core = place(block, member // 2, member % 2)
            pairs.append((block * 4 + member, (to_block % count) * 4 + to_x * 2 + to_core))
    return lax.ppermute(value, AXES, pairs)


def to_other_core(value):
    return send_to(value, lambda block, x, core: (block, x, 1 - core))


def to_other_x(value):
    return send_to(value, lambda block, x, core: (block, 1 - x, core))


def ahead(value, steps):
    return send_to(value, lambda block, x, core: (block + steps, x, core))


def joined(first, second):
    rows = []
    for offset in (0, 2):
        rows += merged(first[offset : offset + 2], second[offset : offset + 2])
    return rows


def pack_kernel(first, second, whole, *halves):
    width = first.shape[1]
    half = first.shape[0] // 2
    whole[:, :width] = first[...]
    whole[:, width:] = second[...]
    for index, out in enumerate(halves):
        here = pl.ds(index * half, half)
        out[:, :width] = first[here]
        out[:, width:] = second[here]


def pack_arrived_kernel(s_ahead, t_ahead, s_x, t_x, ahead_out, rest_out, x_out, part_out):
    width, first = s_x.shape[1], part_out.shape[0]
    for student, teacher, whole, part, here in (
        (s_ahead, t_ahead, ahead_out, rest_out, pl.ds(first, s_x.shape[0] - first)),
        (s_x, t_x, x_out, part_out, pl.ds(0, first)),
    ):
        whole[:, :width] = student[...]
        whole[:, width:] = teacher[...]
        part[:, :width] = student[here]
        part[:, width:] = teacher[here]


def rows_of(parts, columns):
    parts = [part[:, columns] for part in parts]
    return parts[0] if len(parts) == 1 else jnp.concatenate(parts, axis=0)


def tile_of(image, texts, span, scale):
    parts = [
        lax.dot_general(
            image,
            rows_of(text, span),
            (((1,), (1,)), ((), ())),
            preferred_element_type=jnp.float32,
        )
        for text in texts
    ]
    tile = parts[0] if len(parts) == 1 else jnp.concatenate(parts, axis=1)
    return tile * (scale * LOG2E)


def stats_along(tile, axis):
    top = jnp.max(tile, axis=axis, keepdims=True)
    below = jnp.exp2(tile - top)
    return top, jnp.sum(below, axis=axis, keepdims=True), below


def merged(first, second):
    top = jnp.maximum(first[0], second[0])
    return top, first[1] * jnp.exp2(first[0] - top) + second[1] * jnp.exp2(second[0] - top)


def as_rows(columns, shard):
    lane = lax.broadcasted_iota(jnp.int32, (shard, 128), 1)
    packed = jnp.zeros((shard, 128), jnp.float32)
    for k, column in enumerate(columns):
        packed = jnp.where(lane == k, column, packed)
    return packed.T[:8]


def score_shards(images, texts, spans, scales, outs, shard):
    stats = [([], []) for _ in images]
    waiting = None
    for step in [(index, which) for index in range(len(images)) for which in range(2)] + [None]:
        tile = None
        if step:
            index, which = step
            image = rows_of(images[index], spans[which])
            tile = tile_of(image, texts, spans[which], scales[which])
        if waiting:
            (index, which), old = waiting
            here = pl.ds(index * shard, shard)
            for axis, found in ((1, stats[index][0]), (0, stats[index][1])):
                top, total, outs[2 * which + 1 - axis][here] = stats_along(old, axis)
                found += (top, total)
        waiting = step, tile
    return stats


def rows4(ref, first, columns=slice(None)):
    part = ref[first : first + 4, columns]
    return [part[k : k + 1] for k in range(4)]


def text_parts(refs, count):
    whole = count - 1
    texts = [(ref,) for ref in refs[:whole]]
    if count == 3:
        return texts + [refs[whole : whole + 1]], refs[whole + 1 :]
    return texts + [refs[whole : whole + 2]], refs[whole + 2 :]


def part_kernel(shard, scales, spans, size, count, *refs):
    images, refs = (refs[:size], refs[size : 2 * size]), refs[2 * size :]
    texts, refs = text_parts(refs, count)
    others, refs = (refs[:4], refs[4:]) if len(refs) > 6 else ((), refs)
    outs, (row_out, col_out), stat_out = refs[:4], refs[4:6], refs[6:]
    stats = score_shards(images, texts, spans, scales, outs, shard)
    for index, (row, column) in enumerate(stats):
        row_out[:, pl.ds(index * shard, shard)] = as_rows(row, shard)
        for k, value in enumerate(column):
            col_out[4 * index + k : 4 * index + k + 1] = value
    if not others:
        return
    row_home, col_home, row_side, col_side = others
    rows = joined(rows4(row_home, 0), rows4(row_side, 0))
    columns = joined(rows4(col_out, 0), rows4(col_out, 4))
    seen = joined(rows4(col_home, 0), rows4(col_home, 4))
    seen = joined(seen, [part[:, : 3 * shard] for part in columns])
    last = joined(rows4(col_side, 0), rows4(col_side, 4))
    last = joined(last, [part[:, 3 * shard :] for part in columns])
    for k in range(4):
        stat_out[0][k : k + 1, : 2 * shard] = rows[k]
        stat_out[0][k : k + 1, 2 * shard :] = row_out[k : k + 1]
        stat_out[0][4 + k : 5 + k, : 3 * shard] = seen[k]
        stat_out[0][4 + k : 5 + k, 3 * shard :] = last[k]


def piece_stats(ref, kind, piece, shard):
    part = ref[4 * kind : 4 * kind + 4, piece * shard : (piece + 1) * shard]
    return [part[k : k + 1] for k in range(4)]


def block_parities():
    block = lax.axis_index("dp")
    return lax.rem(block, 2) == 0, lax.rem(block // 2, 2) == 0


def join_group_kernel(shard, mine_ref, core_ref, x_ref, home_ref, *outs):
    halves = []
    for kind, other_ref in enumerate((core_ref, x_ref)):
        for half in range(2):
            joint = []
            for piece in (2 * half, 2 * half + 1):
                total = joined(
                    piece_stats(mine_ref, kind, piece, shard),
                    piece_stats(other_ref, kind, piece ^ 1, shard),
                )
                for k, value in enumerate(total):
                    at = 4 * kind + k
                    home_ref[at : at + 1, piece * shard : (piece + 1) * shard] = value
                joint.append(total)
            halves.append([jnp.concatenate(pair, axis=1) for pair in zip(*joint)])
    for kind, upward in enumerate(block_parities()):
        up, down = halves[2 * kind + kind], halves[2 * kind + 1 - kind]
        for k in range(4):
            outs[2 * kind][k : k + 1] = jnp.where(upward, up[k], down[k])
            outs[2 * kind + 1][k : k + 1] = jnp.where(upward, down[k], up[k])
        for out in outs[2 * kind : 2 * kind + 2]:
            out[4:8] = jnp.zeros((4, 2 * shard), jnp.float32)


def join_blocks_kernel(shard, home_ref, *refs):
    ins, out = refs[:4], refs[4]
    for kind, upward in enumerate(block_parities()):
        first, second = (rows4(ref, 0) for ref in ins[2 * kind : 2 * kind + 2])
        above = [jnp.where(upward, x, y) for x, y in zip(first, second)]
        below = [jnp.where(upward, y, x) for x, y in zip(first, second)]
        for half in range(2):
            here = slice(2 * half * shard, 2 * (half + 1) * shard)
            total = joined(rows4(home_ref, 4 * kind, here), above if half == kind else below)
            for k, value in enumerate(total):
                at = 4 * kind + k
                out[at : at + 1, here] = value


def row_factors(stat_ref, tops, index, shard):
    max_s, total_s, max_t, total_t = rows4(stat_ref, 0, pl.ds(index * shard, shard))
    sub = lax.broadcasted_iota(jnp.int32, (128, shard), 0)
    packed = jnp.zeros((128, shard), jnp.float32)
    for k, (top_s, _, top_t, _) in enumerate(tops):
        packed = jnp.where(sub == 2 * k, jnp.exp2(top_s - max_s) / total_s, packed)
        packed = jnp.where(sub == 2 * k + 1, jnp.exp2(top_t - max_t) / total_t, packed)
    packed = packed.T
    return [packed[:, k : k + 1] for k in range(2 * len(tops))]


def weigh(below, here, columns, row, tops, stats):
    row_s, col_s, row_t, col_t = (ref[here, columns] for ref in below)
    top_s, _, top_t, _ = tops
    max_s, total_s, max_t, total_t = stats
    return (
        row_s * row[0]
        - row_t * row[1]
        + col_s * (jnp.exp2(top_s - max_s) / total_s)
        - col_t * (jnp.exp2(top_t - max_t) / total_t)
    ).astype(jnp.bfloat16)


def text_term(image, weights):
    return lax.dot_general(
        image, weights, (((0,), (0,)), ((), ())), preferred_element_type=jnp.float32
    )


def image_term(weights, texts, span):
    total = None
    for index, text in enumerate(texts):
        shard = weights[0].shape[1] // 2
        part = jnp.dot(
            weights[index // 2][:, (index % 2) * shard : (index % 2 + 1) * shard],
            rows_of(text, span),
            preferred_element_type=jnp.float32,
        )
        total = part if total is None else total + part
    return total


def ahead_kernel(shard, span, *refs):
    below_home, below_side, below_behind = refs[0:4], refs[4:8], refs[8:12]
    rows_in, cols_in, stat_ref = refs[12:18:2], refs[13:18:2], refs[18]
    images = (refs[19:20], refs[20:21], refs[21:23], refs[23:25])
    texts, refs = text_parts(refs[25:], 4)
    same_out, cross_out, weights_out, img_out, both_out = (
        refs[0:2], refs[2:4], refs[4], refs[5:7], refs[7]
    )
    home, third = slice(0, 2 * shard), slice(2 * shard, 3 * shard)
    fourth, far = slice(3 * shard, 4 * shard), slice(2 * shard, 4 * shard)
    col_home, col_third, col_last, col_far = (
        rows4(stat_ref, 4, at) for at in (home, third, fourth, far)
    )

    def weights_of(index):
        here = pl.ds((index % 2) * shard, shard)
        at = 4 * (index % 2)
        if index < 2:
            tops = (rows4(rows_in[0], 0, here), rows4(rows_in[1], 0, here))
            row = row_factors(stat_ref, tops, index, shard)
            seen = rows4(cols_in[0], at, third)
            weights = jnp.concatenate(
                [
                    weigh(below_home, here, third, row[:2], seen, col_third),
                    weigh(
                        below_side, here, slice(None), row[2:], rows4(cols_in[1], at), col_last
                    ),
                ],
                axis=1,
            )
        else:
            row = row_factors(stat_ref, (rows4(rows_in[2], 0, here),), index, shard)
            weights = weigh(below_behind, here, far, row, rows4(cols_in[2], at, far), col_far)
            near = weigh(below_behind, here, home, row, rows4(cols_in[2], at, home), col_home)
        return weights, None if index < 2 else near

    total = both = None
    ready = weights_of(0)
    for index in range(4):
        weights, near = ready
        if index < 3:
            ready = weights_of(index + 1)
        image = rows_of(images[index], span)
        term = text_term(image, weights)
        total = total + term if index else term
        if index < 2:
            weights_out[pl.ds(index * shard, shard)] = weights
            continue
        term = text_term(image, near)
        both = term if index == 2 else both + term
        out = img_out[index - 2]
        out[...] = image_term((near, weights), texts, span).astype(out.dtype)
    height = total.shape[0] // 2
    for index in range(2):
        part = total[index * height : (index + 1) * height]
        same_out[index][...] = part[:, :shard]
        cross_out[index][...] = part[:, shard:].astype(jnp.bfloat16)
    both_out[...] = both


def home_kernel(shard, span, *refs):
    below, (row_in, col_in, stat_ref) = refs[0:4], refs[4:7]
    images = (refs[7:8], refs[8:9])
    texts, (weights_in, both_in, *outs) = text_parts(refs[9:], 4)
    img_out, txt_own, txt_x = outs[0:2], *outs[2:]
    home = slice(0, 2 * shard)
    col_home = rows4(stat_ref, 4, home)
    total = both_in[...]
    for index in range(2):
        here = pl.ds(index * shard, shard)
        row = row_factors(stat_ref, (rows4(row_in, 0, here),), index, shard)
        tops = rows4(col_in, 4 * index, home)
        weights = weigh(below, here, home, row, tops, col_home)
        total = total + text_term(rows_of(images[index], span), weights)
        out = img_out[index]
        out[...] = image_term((weights, weights_in[here]), texts, span).astype(out.dtype)
    txt_own[...] = total[:, :shard]
    txt_x[...] = total[:, shard:].astype(jnp.bfloat16)


def add_kernel(first, second, out):
    total = first[...] + second[...].astype(jnp.float32)
    out[...] = total.astype(out.dtype)


def finish_image_kernel(scale, own, core, home, out):
    total = own[...] + core[...].astype(jnp.float32)
    out[...] = (total + home[...].astype(jnp.float32)) * scale


def finish_text_kernel(scale, own, *refs):
    homes, out = refs[:-1], refs[-1]
    width = homes[0].shape[0]
    for index, home in enumerate(homes):
        here = slice(index * width, (index + 1) * width)
        total = own[here] + home[...].astype(jnp.float32)
        out[:, here] = total.T * scale


def on_device(student_image, student_text, teacher_image, teacher_text):
    shard, width_s = student_image.shape
    width_t = teacher_image.shape[1]
    scale_s = 2.0 / math.sqrt(width_s)
    scale_t = 2.0 / math.sqrt(width_t)
    f32 = jnp.float32
    bf16 = jnp.bfloat16
    vmem = pl.BlockSpec(memory_space=pltpu.VMEM)

    def params(mib):
        return pltpu.CompilerParams(vmem_limit_bytes=mib * MIB)


    spans = (slice(0, width_s), slice(width_s, width_s + width_t))
    scales = (scale_s, scale_t)

    def pack(first, second, halves, name):
        heights = (shard,) + (shard // 2,) * halves
        return pl.pallas_call(
            pack_kernel,
            out_shape=tuple(
                jax.ShapeDtypeStruct((height, width_s + width_t), bf16) for height in heights
            ),
            in_specs=[vmem] * 2,
            out_specs=(vmem,) * len(heights),
            compiler_params=params(8),
            name=name,
        )(first, second)

    text_t_ahead, text_t_x = ahead(teacher_text, -2), to_other_x(teacher_text)
    text_s_ahead, text_s_x = ahead(student_text, -2), to_other_x(student_text)
    image_s_core, image_t_core = to_other_core(student_image), to_other_core(teacher_image)
    image, top, bottom = pack(student_image, teacher_image, 2, "pack_images")
    top, image_s_core, image_t_core = lax.optimization_barrier((top, image_s_core, image_t_core))
    top = send_to(top, lambda block, x, core: (block ^ 1, x, core))
    top, bottom, late_s, late_t = lax.optimization_barrier(
        (top, bottom, text_s_ahead, text_t_ahead, text_s_x, text_t_x)
    )[:4]
    packed, first = width_s + width_t, shard // 8
    text_ahead, rest, text_x, text_part = pl.pallas_call(
        pack_arrived_kernel,
        out_shape=tuple(
            jax.ShapeDtypeStruct((height, packed), bf16)
            for height in (shard, shard - first, shard, first)
        ),
        in_specs=[vmem] * 4,
        out_specs=(vmem,) * 4,
        compiler_params=params(8),
        name="pack_arrived",
    )(late_s, late_t, text_s_x, text_t_x)
    (text,) = pack(student_text, teacher_text, 0, "pack_own")
    (image_core,) = pack(image_s_core, image_t_core, 0, "pack_core")

    def stat(shards):
        return jax.ShapeDtypeStruct((8, shards * shard), f32)

    def score(rows, columns):
        return jax.ShapeDtypeStruct((rows * shard, columns * shard), f32)

    def part_scores(shards, texts, *others, name, cost=None):
        size, count = len(shards[0]), {3: 3, 2: 1, 5: 4}[len(texts)]
        outs = (score(2, count),) * 4 + (stat(2), stat(count)) + (stat(4),) * bool(others)
        return pl.pallas_call(
            lambda *refs: part_kernel(shard, scales, spans, size, count, *refs),
            out_shape=outs,
            in_specs=[vmem] * (2 * size + len(texts) + len(others)),
            out_specs=(vmem,) * len(outs),
            compiler_params=params(16),
            cost_estimate=cost,
            name=name,
        )(*shards[0], *shards[1], *texts, *others)

    text_both = (ahead(text_part, -2), to_other_x(rest))
    top = send_to(top, lambda block, x, core: (block + 2 - block % 2 * 2, x, core))
    bottom = ahead(bottom, 1)
    texts = (text, text_x, text_ahead, *text_both)
    own = ((image,), (image_core,))
    *below_home, row_home, col_home = part_scores(own, texts[:3], name="scores_home")
    *below_side, row_side, col_side = part_scores(own, texts[3:], name="scores_side", cost=HEAVY)
    top, bottom = lax.optimization_barrier((top, bottom, row_home))[:2]
    behind = ((top, bottom), (to_other_core(top), to_other_core(bottom)))
    images = (image, image_core, *behind[0], *behind[1])
    stats_own = (row_home, col_home, row_side, col_side)
    *below_behind, row_behind, col_behind, partial = part_scores(
        behind, texts, *stats_own, name="scores_behind"
    )

    shared = jax.ShapeDtypeStruct((8, 2 * shard), f32)
    home, *away = pl.pallas_call(
        lambda *refs: join_group_kernel(shard, *refs),
        out_shape=(stat(4),) + (shared,) * 4,
        in_specs=[vmem] * 3,
        out_specs=(vmem,) * 5,
        compiler_params=params(8),
        name="join_group",
    )(partial, to_other_core(partial), to_other_x(partial))
    away = [
        send_to(part, lambda block, x, core, step=step, first=first: (
            block + (step if (block // step) % 2 == first else -step), x, core
        ))
        for part, step, first in zip(away, (1, 1, 2, 2), (0, 1, 0, 1))
    ]
    stats = pl.pallas_call(
        lambda *refs: join_blocks_kernel(shard, *refs),
        out_shape=stat(4),
        in_specs=[vmem] * 5,
        out_specs=vmem,
        compiler_params=params(8),
        name="join_blocks",
    )(home, *away)

    wide = jax.ShapeDtypeStruct((shard, width_s), f32)
    tall = jax.ShapeDtypeStruct((width_s, shard), f32)
    sent = jax.ShapeDtypeStruct((width_s, shard), bf16)
    flat = jax.ShapeDtypeStruct((shard, width_s), bf16)
    tall_half = jax.ShapeDtypeStruct((width_s // 2, shard), f32)
    sent_half = jax.ShapeDtypeStruct((width_s // 2, shard), bf16)
    *txt_ahead, weights, img_back, img_cross, txt_both = pl.pallas_call(
        lambda *refs: ahead_kernel(shard, spans[0], *refs),
        out_shape=(
            tall_half,
            tall_half,
            sent_half,
            sent_half,
            jax.ShapeDtypeStruct((2 * shard, 2 * shard), bf16),
            wide,
            flat,
            jax.ShapeDtypeStruct((width_s, 2 * shard), f32),
        ),
        in_specs=[vmem] * 30,
        out_specs=(vmem,) * 8,
        compiler_params=params(24),
        name="gradients_ahead",
    )(
        *below_home, *below_side, *below_behind, *stats_own, row_behind, col_behind, stats,
        *images, *texts,
    )
    img_own, img_core, txt_own, txt_x = pl.pallas_call(
        lambda *refs: home_kernel(shard, spans[0], *refs),
        out_shape=(wide, flat, tall, sent),
        in_specs=[vmem] * 16,
        out_specs=(vmem,) * 4,
        compiler_params=params(24),
        name="gradients_home",
    )(*below_home, row_home, col_home, stats, *images[:2], *texts, weights, txt_both)

    img_cross = to_other_core(img_cross)
    img_sum = (img_back + img_cross.astype(f32)).astype(bf16)
    img_home = ahead(img_sum, -1)
    txt_same, txt_cross = txt_ahead[:2], [to_other_x(part) for part in txt_ahead[2:]]
    img_core = to_other_core(img_core)

    def add(first, second, out, name):
        return pl.pallas_call(
            add_kernel,
            out_shape=out,
            in_specs=[vmem] * 2,
            out_specs=vmem,
            compiler_params=params(8),
            cost_estimate=LIGHT,
            name=name,
        )(first, second)

    txt_cross[0] = lax.optimization_barrier((txt_cross[0], img_sum))[0]
    txt_sum = add(txt_same[0], txt_cross[0], sent_half, "add_text")
    txt_x, txt_cross[1] = lax.optimization_barrier((txt_x, txt_cross[1], txt_sum))[:2]
    txt_home = [
        ahead(txt_sum, 2), ahead(add(txt_same[1], txt_cross[1], sent_half, "add_text"), 2)
    ]
    txt_own = add(txt_own, to_other_x(txt_x), tall, "add_own_text")

    def finish(kernel, *args, name):
        return pl.pallas_call(
            lambda *refs: kernel(scale_s, *refs),
            out_shape=wide,
            in_specs=[vmem] * len(args),
            out_specs=vmem,
            compiler_params=params(8),
            name=name,
        )(*args)

    grad_image = finish(finish_image_kernel, img_own, img_core, img_home, name="finish_image")
    *txt_home, txt_own, grad_image = lax.optimization_barrier((*txt_home, txt_own, grad_image))
    grad_text = finish(finish_text_kernel, txt_own, *txt_home, name="finish_text")
    return (grad_image, grad_text)


def solution(mesh):
    spec = P(AXES, None)
    return jax.shard_map(
        on_device,
        mesh=mesh,
        in_specs=(spec, spec, spec, spec),
        out_specs=(spec, spec),
        check_vma=False,
    )
```

time: 645 us -> 88.4 us (0.14)
  waiting for transfers between devices: 473 us -> 40.5 us
  starting transfers between devices: 96.2 us -> 32 us
  blocking collectives: 21 us -> 0 us
  other arithmetic: 17.7 us -> 0.08 us
  between operations: 14.3 us -> 0.8 us
  Pallas kernels: 0 us -> 12.8 us
  local copies, waits for them, and re-layouts: 12.5 us -> 2.04 us
  matrix products: 10.3 us -> 0 us
    ppermute x12 -> x27, waiting for transfers between devices: 415 us -> 40.5 us  [send_to(): return lax.ppermute(value, AXES, pairs)]
    ppermute x12 -> x27, starting transfers between devices: 96.1 us -> 32 us  [send_to(): return lax.ppermute(value, AXES, pairs)]
    all_gather x1 -> x0, waiting for transfers between devices: 34.3 us -> none  [on_device(): own_block = lax.all_gather(both_text, 'pair', axis=0, tiled=True)]
    reduce_scatter x1 -> x0, waiting for transfers between devices: 23.3 us -> none  [on_device(): lax.psum_scatter(text_home, 'pair', scatter_dimension=0, tiled=True)]
    all_gather x4 -> x0, blocking collectives: 21 us -> none  [combined_all(): pieces = jax.tree.map(lambda part: lax.all_gather(part, axis), value)]
    pallas_call x0 -> x16, Pallas kernels: none -> 12.8 us  [the longest x3 6.47 us: part_scores(): pl.pallas_call(lambda *refs: part_kernel(shard, scales, spans, size, coun...]
    dot_general x4 -> x0, matrix products: 10.3 us -> none  [the longest x1 4.64 us: on_device(): image_terms = jnp.dot(weights, part_s, preferred_element_type=jnp.float32)]
    convert_element_type x1, other arithmetic: 7.4 us -> 0.08 us  [on_device(): img_sum = (img_back + img_cross.astype(f32)).astype(bf16)]
  transfers between devices with their start and end apart: 14 -> 27, of which waited for: 12 -> 13; matrix products, arithmetic and copies ran while one was open for 2% -> 0% of each run, Pallas kernels for 0% -> 7%
where the time goes in v1:
time: 88.4 us; the launch traced here: 88.1 us
  waiting for transfers between devices  40.5 us (46%)
  starting transfers between devices  32 us (36%)
  Pallas kernels  12.8 us (14%)
  local copies, waits for them, and re-layouts  2.04 us (2%)
    ppermute x27, waiting for transfers between devices, send_to(): return lax.ppermute(value, AXES, pairs)  40.5 us
    ppermute x27, starting transfers between devices, send_to(): return lax.ppermute(value, AXES, pairs)  32 us
    pallas_call x3, Pallas kernels, part_scores(): pl.pallas_call(lambda *refs: part_kernel(shard, scales, spans, size, coun...  6.47 us
    pallas_call x1, Pallas kernels, on_device(): pl.pallas_call(lambda *refs: ahead_kernel(shard, spans[0], *refs), out_sh...  2.44 us
    unnamed x8, local copies, waits for them, and re-layouts  2.04 us
    pallas_call x2, Pallas kernels, finish(): pl.pallas_call(lambda *refs: kernel(scale_s, *refs), out_shape=wide, in_s...  1.89 us
  transfers between devices with their start and end apart: 27, of which 13 were waited for; matrix products, arithmetic and copies ran while one was open for 0% of the time, Pallas kernels for 7%

profile of v1, /device:TPU:0, one launch (start us, length us, event | category | flops | bytes accessed | tf_op | source)
XLA Modules:
  0.0 88.1 jit_solution(6550950609049287111)
XLA Ops:
  0.6 0.5 collective-permute-start.1
  1.2 0.1 collective-permute-start
  1.2 2.9 %collective-permute-start.6 = (bf16[256,1280]{1,0:T(8,128)(2,1)}, bf16[256,1280]{1,0:T(8,128)(2,1)S(1)}, u32[]{:S(2)}, u32[]{:S(2)}) collective-permute-start(bf16[256,1280]{1,0:T(8,128)(2,1)} %second.3), channel_id=1, source_target_pairs={{0,2},{1,3},{2,0},{3,1},{4,6},{5,7},{6,4},{7,5},{8,10},{9,11},{10,... | collective-permute-start | bytes 1966088 | tf_op jit(solution)/shard_map/ppermute | solution.py:24
  4.2 3.6 %collective-permute-start.4 = (bf16[256,1280]{1,0:T(8,128)(2,1)}, bf16[256,1280]{1,0:T(8,128)(2,1)S(1)}, u32[]{:S(2)}, u32[]{:S(2)}) collective-permute-start(bf16[256,1280]{1,0:T(8,128)(2,1)} %second.3), channel_id=1, source_target_pairs={{0,24},{1,25},{2,26},{3,27},{4,28},{5,29},{6,30},{7,31},{8,0},{9,1... | collective-permute-start | bytes 1966088 | tf_op jit(solution)/shard_map/ppermute | solution.py:24
  7.8 1.1 %copy-done.1 = bf16[256,1280]{1,0:T(8,128)(2,1)S(1)} copy-done((bf16[256,1280]{1,0:T(8,128)(2,1)S(1)}, bf16[256,1280]{1,0:T(8,128)(2,1)}, u32[]{:S(2)}) %copy-start.1) | copy-done | bytes 655384
  8.8 0.9 %copy-done.2 = bf16[256,512]{1,0:T(8,128)(2,1)S(1)} copy-done((bf16[256,512]{1,0:T(8,128)(2,1)S(1)}, bf16[256,512]{1,0:T(8,128)(2,1)}, u32[]{:S(2)}) %copy-start.2) | copy-done | bytes 262168
  9.8 0.1 pack_images.1
  9.9 1.6 %collective-permute-start.2 = (bf16[128,1792]{1,0:T(8,128)(2,1)S(1)}, bf16[128,1792]{1,0:T(8,128)(2,1)S(1)}, u32[]{:S(2)}, u32[]{:S(2)}) collective-permute-start(bf16[128,1792]{1,0:T(8,128)(2,1)S(1)} %get-tuple-element.65), channel_id=1, source_target_pairs={{0,4},{1,5},{2,6},{3,7},{4,0},{5,1},{6,2},{7,3},{8,12},{9,13},{10,... | collective-permute-start | bytes 1376264 | tf_op jit(solution)/shard_map/ppermute | solution.py:24
  11.5 0.5 collective-permute-start.5
  12.1 0.4 collective-permute-start.3
  12.5 12.4 %collective-permute-done.5.s_x = bf16[256,512]{1,0:T(8,128)(2,1)S(1)} collective-permute-done((bf16[256,512]{1,0:T(8,128)(2,1)}, bf16[256,512]{1,0:T(8,128)(2,1)S(1)}, u32[]{:S(2)}, u32[]{:S(2)}) %collective-permute-start.5) | collective-permute-done | bytes 262176 | tf_op jit(solution)/shard_map/ppermute | solution.py:24
  25.0 2.7 %collective-permute-done.3.s_ahead = bf16[256,512]{1,0:T(8,128)(2,1)S(1)} collective-permute-done((bf16[256,512]{1,0:T(8,128)(2,1)}, bf16[256,512]{1,0:T(8,128)(2,1)S(1)}, u32[]{:S(2)}, u32[]{:S(2)}) %collective-permute-start.3) | collective-permute-done | bytes 262176 | tf_op jit(solution)/shard_map/ppermute | solution.py:24
  27.7 0.2 pack_arrived.1
  27.8 0.6 collective-permute-start.8
  28.4 2.2 %collective-permute-start.9 = (bf16[128,1792]{1,0:T(8,128)(2,1)S(1)}, bf16[128,1792]{1,0:T(8,128)(2,1)S(1)}, u32[]{:S(2)}, u32[]{:S(2)}) collective-permute-start(bf16[128,1792]{1,0:T(8,128)(2,1)S(1)} %collective-permute-done.2), channel_id=1, source_target_pairs={{0,8},{1,9},{2,10},{3,11},{4,4},{5,5},{6,6},{7,7},{8,16},{9,17},{1... | collective-permute-start | bytes 1376264 | tf_op jit(solution)/shard_map/ppermute | solution.py:24
  30.8 4.1 %collective-permute-start.7 = (bf16[32,1792]{1,0:T(8,128)(2,1)S(1)}, bf16[32,1792]{1,0:T(8,128)(2,1)S(1)}, u32[]{:S(2)}, u32[]{:S(2)}) collective-permute-start(bf16[32,1792]{1,0:T(8,128)(2,1)S(1)} %get-tuple-element.75), channel_id=1, source_target_pairs={{0,24},{1,25},{2,26},{3,27},{4,28},{5,29},{6,30},{7,31},{8,0},{9,1... | collective-permute-start | bytes 344072 | tf_op jit(solution)/shard_map/ppermute | solution.py:24
  35.0 2.3 %scores_home.1 = (f32[512,768]{1,0:T(8,128)S(1)}, f32[512,768]{1,0:T(8,128)S(1)}, f32[512,768]{1,0:T(8,128)S(1)}, f32[512,768]{1,0:T(8,128)S(1)}, f32[8,512]{1,0:T(8,128)S(1)}, /*index=5*/f32[8,768]{1,0:T(8,128)S(1)}) custom-call(bf16[256,1792]{1,0:T(8,128)(2,1)S(1)} %get-tuple-element.61.refs_0_.refs_19_.refs_7_, ...), custom_call_target="tpu_custom_call" | custom-call | tf_op jit(solution)/shard_map/scores_home/pallas_call | solution.py:416
  37.3 7.8 %collective-permute-done.9.refs_0_.refs_21_ = bf16[128,1792]{1,0:T(8,128)(2,1)S(1)} collective-permute-done((bf16[128,1792]{1,0:T(8,128)(2,1)S(1)}, bf16[128,1792]{1,0:T(8,128)(2,1)S(1)}, u32[]{:S(2)}, u32[]{:S(2)}) %collective-permute-start.9) | collective-permute-done | bytes 458784 | tf_op jit(solution)/shard_map/ppermute | solution.py:24
  45.2 0.5 collective-permute-done.10.refs_1_.refs_22_
  45.7 0.5 collective-permute-start.12
  46.2 0.4 collective-permute-done.8.refs_3_.refs_8_.refs_29_.refs_13_
  46.6 1.0 %scores_side.1 = (f32[512,256]{1,0:T(8,128)S(1)}, f32[512,256]{1,0:T(8,128)S(1)}, f32[512,256]{1,0:T(8,128)S(1)}, f32[512,256]{1,0:T(8,128)S(1)}, f32[8,512]{1,0:T(8,128)S(1)}, /*index=5*/f32[8,256]{1,0:T(8,128)S(1)}) custom-call(bf16[256,1792]{1,0:T(8,128)(2,1)S(1)} %get-tuple-element.61.refs_0_.refs_19_.refs_7_, ...), custom_call_target="tpu_custom_call" | custom-call | flops 99999997952 | bytes 1000000000 | tf_op jit(solution)/shard_map/scores_side/pallas_call | solution.py:416
  47.7 0.5 collective-permute-done.12.refs_3_.refs_24_
  48.2 3.1 %scores_behind.1 = (f32[512,1024]{1,0:T(8,128)S(1)}, f32[512,1024]{1,0:T(8,128)S(1)}, f32[512,1024]{1,0:T(8,128)S(1)}, f32[512,1024]{1,0:T(8,128)S(1)}, f32[8,51...) custom-call(bf16[128,1792]{1,0:T(8,128)(2,1)S(1)} %collective-permute-done.9.refs_0_.refs_21_, ...), custom_call_target="tpu_custom_call" | custom-call | tf_op jit(solution)/shard_map/scores_behind/pallas_call | solution.py:416
  51.3 1.5 %collective-permute-start.14 = (f32[8,1024]{1,0:T(8,128)S(1)}, f32[8,1024]{1,0:T(8,128)S(1)}, u32[]{:S(2)}, u32[]{:S(2)}) collective-permute-start(f32[8,1024]{1,0:T(8,128)S(1)} %get-tuple-element.95.refs_0_), channel_id=1, source_target_pairs={{0,2},{1,3},{2,0},{3,1},{4,6},{5,7},{6,4},{7,5},{8,10},{9,11},{10,... | collective-permute-start | bytes 98312 | tf_op jit(solution)/shard_map/ppermute | solution.py:24
  52.8 2.5 %collective-permute-done.14.refs_2_ = f32[8,1024]{1,0:T(8,128)S(1)} collective-permute-done((f32[8,1024]{1,0:T(8,128)S(1)}, f32[8,1024]{1,0:T(8,128)S(1)}, u32[]{:S(2)}, u32[]{:S(2)}) %collective-permute-start.14) | collective-permute-done | bytes 32800 | tf_op jit(solution)/shard_map/ppermute | solution.py:24
  55.3 1.1 %collective-permute-start.15 = (f32[8,512]{1,0:T(8,128)S(1)}, f32[8,512]{1,0:T(8,128)S(1)}, u32[]{:S(2)}, u32[]{:S(2)}) collective-permute-start(f32[8,512]{1,0:T(8,128)S(1)} %get-tuple-element.97), channel_id=1, source_target_pairs={{0,4},{1,5},{2,6},{3,7},{4,0},{5,1},{6,2},{7,3},{8,12},{9,13},{10,... | collective-permute-start | bytes 49160 | tf_op jit(solution)/shard_map/ppermute | solution.py:24
  56.4 4.1 %collective-permute-start.16 = (f32[8,512]{1,0:T(8,128)S(1)}, f32[8,512]{1,0:T(8,128)S(1)}, u32[]{:S(2)}, u32[]{:S(2)}) collective-permute-start(f32[8,512]{1,0:T(8,128)S(1)} %get-tuple-element.98), channel_id=1, source_target_pairs={{0,28},{1,29},{2,30},{3,31},{4,8},{5,9},{6,10},{7,11},{8,4},{9,5},... | collective-permute-start | bytes 49160 | tf_op jit(solution)/shard_map/ppermute | solution.py:24
  60.5 1.4 %collective-permute-start.18 = (f32[8,512]{1,0:T(8,128)S(1)}, f32[8,512]{1,0:T(8,128)S(1)}, u32[]{:S(2)}, u32[]{:S(2)}) collective-permute-start(f32[8,512]{1,0:T(8,128)S(1)} %get-tuple-element.100), channel_id=1, source_target_pairs={{0,24},{1,25},{2,26},{3,27},{4,28},{5,29},{6,30},{7,31},{8,16},{9,... | collective-permute-start | bytes 49160 | tf_op jit(solution)/shard_map/ppermute | solution.py:24
  61.9 1.0 %collective-permute-done.16.refs_2_ = f32[8,512]{1,0:T(8,128)S(1)} collective-permute-done((f32[8,512]{1,0:T(8,128)S(1)}, f32[8,512]{1,0:T(8,128)S(1)}, u32[]{:S(2)}, u32[]{:S(2)}) %collective-permute-start.16) | collective-permute-done | bytes 16416 | tf_op jit(solution)/shard_map/ppermute | solution.py:24
  62.8 1.4 %collective-permute-done.17.refs_3_ = f32[8,512]{1,0:T(8,128)S(1)} collective-permute-done((f32[8,512]{1,0:T(8,128)S(1)}, f32[8,512]{1,0:T(8,128)S(1)}, u32[]{:S(2)}, u32[]{:S(2)}) %collective-permute-start.17) | collective-permute-done | bytes 16416 | tf_op jit(solution)/shard_map/ppermute | solution.py:24
  64.3 1.8 %collective-permute-done.18.refs_4_ = f32[8,512]{1,0:T(8,128)S(1)} collective-permute-done((f32[8,512]{1,0:T(8,128)S(1)}, f32[8,512]{1,0:T(8,128)S(1)}, u32[]{:S(2)}, u32[]{:S(2)}) %collective-permute-start.18) | collective-permute-done | bytes 16416 | tf_op jit(solution)/shard_map/ppermute | solution.py:24
  66.1 2.4 %gradients_ahead.1 = (f32[256,256]{1,0:T(8,128)S(1)}, f32[256,256]{1,0:T(8,128)S(1)}, bf16[256,256]{1,0:T(8,128)(2,1)S(1)}, bf16[256,256]{1,0:T(8,128)(2,1)S(1)}...) custom-call(f32[512,768]{1,0:T(8,128)S(1)} %get-tuple-element.71.ref, ...), custom_call_target="tpu_custom_call" | custom-call | tf_op jit(solution)/shard_map/gradients_ahead/pallas_call | solution.py:471
  68.6 0.1 collective-permute-start.20
  68.6 1.2 %collective-permute-start.19 = (bf16[256,256]{1,0:T(8,128)(2,1)S(1)}, bf16[256,256]{1,0:T(8,128)(2,1)S(1)}, u32[]{:S(2)}, u32[]{:S(2)}) collective-permute-start(bf16[256,256]{1,0:T(8,128)(2,1)S(1)} %get-tuple-element.102), channel_id=1, source_target_pairs={{0,2},{1,3},{2,0},{3,1},{4,6},{5,7},{6,4},{7,5},{8,10},{9,11},{10,... | collective-permute-start | bytes 393224 | tf_op jit(solution)/shard_map/ppermute | solution.py:24
  69.8 0.9 %collective-permute-start.22 = (bf16[256,256]{1,0:T(8,128)(2,1)S(1)}, bf16[256,256]{1,0:T(8,128)(2,1)S(1)}, u32[]{:S(2)}, u32[]{:S(2)}) collective-permute-start(bf16[256,256]{1,0:T(8,128)(2,1)S(1)} %get-tuple-element.110), channel_id=1, source_target_pairs={{0,2},{1,3},{2,0},{3,1},{4,6},{5,7},{6,4},{7,5},{8,10},{9,11},{10,... | collective-permute-start | bytes 393224 | tf_op jit(solution)/shard_map/ppermute | solution.py:24
  70.7 1.3 %gradients_home.1 = (f32[256,512]{1,0:T(8,128)S(1)}, bf16[256,512]{1,0:T(8,128)(2,1)S(1)}, f32[512,256]{1,0:T(8,128)S(1)}, bf16[512,256]{1,0:T(8,128)(2,1)S(1)}) custom-call(f32[512,768]{1,0:T(8,128)S(1)} %get-tuple-element.71.refs_0_, f32[512,768]{1,0:T(8,128)S(1)} %get-tuple-element.72.refs_1_, f32[512,768]{1,0:T(8,128)S(1)} %get-tuple-element.73.refs_2_, ...), custom_call_target="tpu_custom_call" | custom-call | tf_op jit(solution)/shard_map/gradients_home/pallas_call | solution.py:491
  72.1 0.1 collective-permute-start.25
  72.2 0.1 add_convert_fusion
  72.2 3.0 %collective-permute-start.26 = (bf16[256,512]{1,0:T(8,128)(2,1)S(1)}, bf16[256,512]{1,0:T(8,128)(2,1)S(1)}, u32[]{:S(2)}, u32[]{:S(2)}) collective-permute-start(bf16[256,512]{1,0:T(8,128)(2,1)S(1)} %add_convert_fusion), channel_id=1, source_target_pairs={{0,28},{1,29},{2,30},{3,31},{4,0},{5,1},{6,2},{7,3},{8,4},{9,5},{1... | collective-permute-start | bytes 786440 | tf_op jit(solution)/shard_map/ppermute | solution.py:24
  75.4 2.0 %collective-permute-done.22.second = bf16[256,256]{1,0:T(8,128)(2,1)S(1)} collective-permute-done((bf16[256,256]{1,0:T(8,128)(2,1)S(1)}, bf16[256,256]{1,0:T(8,128)(2,1)S(1)}, u32[]{:S(2)}, u32[]{:S(2)}) %collective-permute-start.22) | collective-permute-done | bytes 131104 | tf_op jit(solution)/shard_map/ppermute | solution.py:24
  77.4 1.1 %collective-permute-start.24 = (bf16[512,256]{1,0:T(8,128)(2,1)S(1)}, bf16[512,256]{1,0:T(8,128)(2,1)S(1)}, u32[]{:S(2)}, u32[]{:S(2)}) collective-permute-start(bf16[512,256]{1,0:T(8,128)(2,1)S(1)} %get-tuple-element.113), channel_id=1, source_target_pairs={{0,2},{1,3},{2,0},{3,1},{4,6},{5,7},{6,4},{7,5},{8,10},{9,11},{10,... | collective-permute-start | bytes 786440 | tf_op jit(solution)/shard_map/ppermute | solution.py:24
  78.5 0.3 collective-permute-start.23
  78.8 6.4 %collective-permute-done.24.second = bf16[512,256]{1,0:T(8,128)(2,1)S(1)} collective-permute-done((bf16[512,256]{1,0:T(8,128)(2,1)S(1)}, bf16[512,256]{1,0:T(8,128)(2,1)S(1)}, u32[]{:S(2)}, u32[]{:S(2)}) %collective-permute-start.24) | collective-permute-done | bytes 262176 | tf_op jit(solution)/shard_map/ppermute | solution.py:24
  85.2 0.1 add_own_text.1.refs_0_
  85.3 0.9 %finish_image.1 = f32[256,512]{1,0:T(8,128)} custom-call(f32[256,512]{1,0:T(8,128)S(1)} %get-tuple-element.114.refs_0_, bf16[256,512]{1,0:T(8,128)(2,1)S(1)} %collective-permute-done.25.refs_1_, bf16[256,512]{1,0:T(8,128)(2,1)S(1)} %collective-permute-done.26.refs_2_), custom_call_target="tpu_custom_call" | custom-call | tf_op jit(solution)/shard_map/finish_image/pallas_call | solution.py:526
  86.2 0.9 %collective-permute-done.23.refs_2_ = bf16[256,256]{1,0:T(8,128)(2,1)S(1)} collective-permute-done((bf16[256,256]{1,0:T(8,128)(2,1)S(1)}, bf16[256,256]{1,0:T(8,128)(2,1)S(1)}, u32[]{:S(2)}, u32[]{:S(2)}) %collective-permute-start.23) | collective-permute-done | bytes 131104 | tf_op jit(solution)/shard_map/ppermute | solution.py:24
  87.1 1.0 %finish_text.1 = f32[256,512]{1,0:T(8,128)} custom-call(f32[512,256]{1,0:T(8,128)S(1)} %add_own_text.1.refs_0_, bf16[256,256]{1,0:T(8,128)(2,1)S(1)} %collective-permute-done.21.refs_1_, bf16[256,256]{1,0:T(8,128)(2,1)S(1)} %collective-permute-done.23.refs_2_), custom_call_target="tpu_custom_call" | custom-call | tf_op jit(solution)/shard_map/finish_text/pallas_call | solution.py:526
  (31 shorter events, 0.4 us)
Async XLA Ops:
  0.6 34.3 %copy-start = (bf16[256,1280]{1,0:T(8,128)(2,1)S(1)}, bf16[256,1280]{1,0:T(8,128)(2,1)}, u32[]{:S(2)}) copy-start(bf16[256,1280]{1,0:T(8,128)(2,1)} %second.3) | copy-start | bytes 1966084
  0.6 9.3 %collective-permute-start.1 = (bf16[256,1280]{1,0:T(8,128)(2,1)}, bf16[256,1280]{1,0:T(8,128)(2,1)S(1)}, u32[]{:S(2)}, u32[]{:S(2)}) collective-permute-start(bf16[256,1280]{1,0:T(8,128)(2,1)} %second.2), channel_id=1, source_target_pairs={{0,1},{1,0},{2,3},{3,2},{4,5},{5,4},{6,7},{7,6},{8,9},{9,8},{10,11... | collective-permute-start | bytes 1966088 | tf_op jit(solution)/shard_map/ppermute | solution.py:24
  1.2 8.8 %collective-permute-start = (bf16[256,512]{1,0:T(8,128)(2,1)}, bf16[256,512]{1,0:T(8,128)(2,1)S(1)}, u32[]{:S(2)}, u32[]{:S(2)}) collective-permute-start(bf16[256,512]{1,0:T(8,128)(2,1)} %first.2), channel_id=1, source_target_pairs={{0,1},{1,0},{2,3},{3,2},{4,5},{5,4},{6,7},{7,6},{8,9},{9,8},{10,11... | collective-permute-start | bytes 786440 | tf_op jit(solution)/shard_map/ppermute | solution.py:24
  1.2 26.4 %collective-permute-start.6 = (bf16[256,1280]{1,0:T(8,128)(2,1)}, bf16[256,1280]{1,0:T(8,128)(2,1)S(1)}, u32[]{:S(2)}, u32[]{:S(2)}) collective-permute-start(bf16[256,1280]{1,0:T(8,128)(2,1)} %second.3), channel_id=1, source_target_pairs={{0,2},{1,3},{2,0},{3,1},{4,6},{5,7},{6,4},{7,5},{8,10},{9,11},{10,... | collective-permute-start | bytes 1966088 | tf_op jit(solution)/shard_map/ppermute | solution.py:24
  4.2 23.5 %collective-permute-start.4 = (bf16[256,1280]{1,0:T(8,128)(2,1)}, bf16[256,1280]{1,0:T(8,128)(2,1)S(1)}, u32[]{:S(2)}, u32[]{:S(2)}) collective-permute-start(bf16[256,1280]{1,0:T(8,128)(2,1)} %second.3), channel_id=1, source_target_pairs={{0,24},{1,25},{2,26},{3,27},{4,28},{5,29},{6,30},{7,31},{8,0},{9,1... | collective-permute-start | bytes 1966088 | tf_op jit(solution)/shard_map/ppermute | solution.py:24
  7.8 1.1 %copy-start.1 = (bf16[256,1280]{1,0:T(8,128)(2,1)S(1)}, bf16[256,1280]{1,0:T(8,128)(2,1)}, u32[]{:S(2)}) copy-start(bf16[256,1280]{1,0:T(8,128)(2,1)} %second.2) | copy-start | bytes 1966084
  8.8 0.9 %copy-start.2 = (bf16[256,512]{1,0:T(8,128)(2,1)S(1)}, bf16[256,512]{1,0:T(8,128)(2,1)}, u32[]{:S(2)}) copy-start(bf16[256,512]{1,0:T(8,128)(2,1)} %first.2) | copy-start | bytes 786436
  9.8 25.1 %copy-start.3 = (bf16[256,512]{1,0:T(8,128)(2,1)S(1)}, bf16[256,512]{1,0:T(8,128)(2,1)}, u32[]{:S(2)}) copy-start(bf16[256,512]{1,0:T(8,128)(2,1)} %first.3) | copy-start | bytes 786436
  9.9 17.7 %collective-permute-start.2 = (bf16[128,1792]{1,0:T(8,128)(2,1)S(1)}, bf16[128,1792]{1,0:T(8,128)(2,1)S(1)}, u32[]{:S(2)}, u32[]{:S(2)}) collective-permute-start(bf16[128,1792]{1,0:T(8,128)(2,1)S(1)} %get-tuple-element.65), channel_id=1, source_target_pairs={{0,4},{1,5},{2,6},{3,7},{4,0},{5,1},{6,2},{7,3},{8,12},{9,13},{10,... | collective-permute-start | bytes 1376264 | tf_op jit(solution)/shard_map/ppermute | solution.py:24
  11.5 13.4 %collective-permute-start.5 = (bf16[256,512]{1,0:T(8,128)(2,1)}, bf16[256,512]{1,0:T(8,128)(2,1)S(1)}, u32[]{:S(2)}, u32[]{:S(2)}) collective-permute-start(bf16[256,512]{1,0:T(8,128)(2,1)} %first.3), channel_id=1, source_target_pairs={{0,2},{1,3},{2,0},{3,1},{4,6},{5,7},{6,4},{7,5},{8,10},{9,11},{10,... | collective-permute-start | bytes 786440 | tf_op jit(solution)/shard_map/ppermute | solution.py:24
  12.1 15.6 %collective-permute-start.3 = (bf16[256,512]{1,0:T(8,128)(2,1)}, bf16[256,512]{1,0:T(8,128)(2,1)S(1)}, u32[]{:S(2)}, u32[]{:S(2)}) collective-permute-start(bf16[256,512]{1,0:T(8,128)(2,1)} %first.3), channel_id=1, source_target_pairs={{0,24},{1,25},{2,26},{3,27},{4,28},{5,29},{6,30},{7,31},{8,0},{9,1... | collective-permute-start | bytes 786440 | tf_op jit(solution)/shard_map/ppermute | solution.py:24
  27.8 18.8 %collective-permute-start.8 = (bf16[224,1792]{1,0:T(8,128)(2,1)S(1)}, bf16[224,1792]{1,0:T(8,128)(2,1)S(1)}, u32[]{:S(2)}, u32[]{:S(2)}) collective-permute-start(bf16[224,1792]{1,0:T(8,128)(2,1)S(1)} %get-tuple-element.76), channel_id=1, source_target_pairs={{0,2},{1,3},{2,0},{3,1},{4,6},{5,7},{6,4},{7,5},{8,10},{9,11},{10,... | collective-permute-start | bytes 2408456 | tf_op jit(solution)/shard_map/ppermute | solution.py:24
  28.4 16.7 %collective-permute-start.9 = (bf16[128,1792]{1,0:T(8,128)(2,1)S(1)}, bf16[128,1792]{1,0:T(8,128)(2,1)S(1)}, u32[]{:S(2)}, u32[]{:S(2)}) collective-permute-start(bf16[128,1792]{1,0:T(8,128)(2,1)S(1)} %collective-permute-done.2), channel_id=1, source_target_pairs={{0,8},{1,9},{2,10},{3,11},{4,4},{5,5},{6,6},{7,7},{8,16},{9,17},{1... | collective-permute-start | bytes 1376264 | tf_op jit(solution)/shard_map/ppermute | solution.py:24
  30.7 15.0 %collective-permute-start.10 = (bf16[128,1792]{1,0:T(8,128)(2,1)S(1)}, bf16[128,1792]{1,0:T(8,128)(2,1)S(1)}, u32[]{:S(2)}, u32[]{:S(2)}) collective-permute-start(bf16[128,1792]{1,0:T(8,128)(2,1)S(1)} %get-tuple-element.82), channel_id=1, source_target_pairs={{0,4},{1,5},{2,6},{3,7},{4,8},{5,9},{6,10},{7,11},{8,12},{9,13},{1... | collective-permute-start | bytes 1376264 | tf_op jit(solution)/shard_map/ppermute | solution.py:24
  30.8 15.4 %collective-permute-start.7 = (bf16[32,1792]{1,0:T(8,128)(2,1)S(1)}, bf16[32,1792]{1,0:T(8,128)(2,1)S(1)}, u32[]{:S(2)}, u32[]{:S(2)}) collective-permute-start(bf16[32,1792]{1,0:T(8,128)(2,1)S(1)} %get-tuple-element.75), channel_id=1, source_target_pairs={{0,24},{1,25},{2,26},{3,27},{4,28},{5,29},{6,30},{7,31},{8,0},{9,1... | collective-permute-start | bytes 344072 | tf_op jit(solution)/shard_map/ppermute | solution.py:24
  45.7 2.0 %collective-permute-start.11 = (bf16[128,1792]{1,0:T(8,128)(2,1)S(1)}, bf16[128,1792]{1,0:T(8,128)(2,1)S(1)}, u32[]{:S(2)}, u32[]{:S(2)}) collective-permute-start(bf16[128,1792]{1,0:T(8,128)(2,1)S(1)} %collective-permute-done.9.refs_0_.refs_21_), channel_id=1, source_target_pairs={{0,1},{1,0},{2,3},{3,2},{4,5},{5,4},{6,7},{7,6},{8,9},{9,8},{10,11... | collective-permute-start | bytes 1376264 | tf_op jit(solution)/shard_map/ppermute | solution.py:24
  45.7 2.5 %collective-permute-start.12 = (bf16[128,1792]{1,0:T(8,128)(2,1)S(1)}, bf16[128,1792]{1,0:T(8,128)(2,1)S(1)}, u32[]{:S(2)}, u32[]{:S(2)}) collective-permute-start(bf16[128,1792]{1,0:T(8,128)(2,1)S(1)} %collective-permute-done.10.refs_1_.refs_22_), channel_id=1, source_target_pairs={{0,1},{1,0},{2,3},{3,2},{4,5},{5,4},{6,7},{7,6},{8,9},{9,8},{10,11... | collective-permute-start | bytes 1376264 | tf_op jit(solution)/shard_map/ppermute | solution.py:24
  51.3 3.9 %collective-permute-start.14 = (f32[8,1024]{1,0:T(8,128)S(1)}, f32[8,1024]{1,0:T(8,128)S(1)}, u32[]{:S(2)}, u32[]{:S(2)}) collective-permute-start(f32[8,1024]{1,0:T(8,128)S(1)} %get-tuple-element.95.refs_0_), channel_id=1, source_target_pairs={{0,2},{1,3},{2,0},{3,1},{4,6},{5,7},{6,4},{7,5},{8,10},{9,11},{10,... | collective-permute-start | bytes 98312 | tf_op jit(solution)/shard_map/ppermute | solution.py:24
  52.8 2.5 %collective-permute-start.13 = (f32[8,1024]{1,0:T(8,128)S(1)}, f32[8,1024]{1,0:T(8,128)S(1)}, u32[]{:S(2)}, u32[]{:S(2)}) collective-permute-start(f32[8,1024]{1,0:T(8,128)S(1)} %get-tuple-element.95.refs_0_), channel_id=1, source_target_pairs={{0,1},{1,0},{2,3},{3,2},{4,5},{5,4},{6,7},{7,6},{8,9},{9,8},{10,11... | collective-permute-start | bytes 98312 | tf_op jit(solution)/shard_map/ppermute | solution.py:24
  55.3 6.6 %collective-permute-start.15 = (f32[8,512]{1,0:T(8,128)S(1)}, f32[8,512]{1,0:T(8,128)S(1)}, u32[]{:S(2)}, u32[]{:S(2)}) collective-permute-start(f32[8,512]{1,0:T(8,128)S(1)} %get-tuple-element.97), channel_id=1, source_target_pairs={{0,4},{1,5},{2,6},{3,7},{4,0},{5,1},{6,2},{7,3},{8,12},{9,13},{10,... | collective-permute-start | bytes 49160 | tf_op jit(solution)/shard_map/ppermute | solution.py:24
  56.4 6.4 %collective-permute-start.16 = (f32[8,512]{1,0:T(8,128)S(1)}, f32[8,512]{1,0:T(8,128)S(1)}, u32[]{:S(2)}, u32[]{:S(2)}) collective-permute-start(f32[8,512]{1,0:T(8,128)S(1)} %get-tuple-element.98), channel_id=1, source_target_pairs={{0,28},{1,29},{2,30},{3,31},{4,8},{5,9},{6,10},{7,11},{8,4},{9,5},... | collective-permute-start | bytes 49160 | tf_op jit(solution)/shard_map/ppermute | solution.py:24
  60.5 3.7 %collective-permute-start.17 = (f32[8,512]{1,0:T(8,128)S(1)}, f32[8,512]{1,0:T(8,128)S(1)}, u32[]{:S(2)}, u32[]{:S(2)}) collective-permute-start(f32[8,512]{1,0:T(8,128)S(1)} %get-tuple-element.99), channel_id=1, source_target_pairs={{0,8},{1,9},{2,10},{3,11},{4,12},{5,13},{6,14},{7,15},{8,0},{9,1},... | collective-permute-start | bytes 49160 | tf_op jit(solution)/shard_map/ppermute | solution.py:24
  60.5 5.5 %collective-permute-start.18 = (f32[8,512]{1,0:T(8,128)S(1)}, f32[8,512]{1,0:T(8,128)S(1)}, u32[]{:S(2)}, u32[]{:S(2)}) collective-permute-start(f32[8,512]{1,0:T(8,128)S(1)} %get-tuple-element.100), channel_id=1, source_target_pairs={{0,24},{1,25},{2,26},{3,27},{4,28},{5,29},{6,30},{7,31},{8,16},{9,... | collective-permute-start | bytes 49160 | tf_op jit(solution)/shard_map/ppermute | solution.py:24
  68.6 3.6 %collective-permute-start.20 = (bf16[256,512]{1,0:T(8,128)(2,1)S(1)}, bf16[256,512]{1,0:T(8,128)(2,1)S(1)}, u32[]{:S(2)}, u32[]{:S(2)}) collective-permute-start(bf16[256,512]{1,0:T(8,128)(2,1)S(1)} %get-tuple-element.104), channel_id=1, source_target_pairs={{0,1},{1,0},{2,3},{3,2},{4,5},{5,4},{6,7},{7,6},{8,9},{9,8},{10,11... | collective-permute-start | bytes 786440 | tf_op jit(solution)/shard_map/ppermute | solution.py:24
  68.6 6.6 %collective-permute-start.19 = (bf16[256,256]{1,0:T(8,128)(2,1)S(1)}, bf16[256,256]{1,0:T(8,128)(2,1)S(1)}, u32[]{:S(2)}, u32[]{:S(2)}) collective-permute-start(bf16[256,256]{1,0:T(8,128)(2,1)S(1)} %get-tuple-element.102), channel_id=1, source_target_pairs={{0,2},{1,3},{2,0},{3,1},{4,6},{5,7},{6,4},{7,5},{8,10},{9,11},{10,... | collective-permute-start | bytes 393224 | tf_op jit(solution)/shard_map/ppermute | solution.py:24
  69.8 7.5 %collective-permute-start.22 = (bf16[256,256]{1,0:T(8,128)(2,1)S(1)}, bf16[256,256]{1,0:T(8,128)(2,1)S(1)}, u32[]{:S(2)}, u32[]{:S(2)}) collective-permute-start(bf16[256,256]{1,0:T(8,128)(2,1)S(1)} %get-tuple-element.110), channel_id=1, source_target_pairs={{0,2},{1,3},{2,0},{3,1},{4,6},{5,7},{6,4},{7,5},{8,10},{9,11},{10,... | collective-permute-start | bytes 393224 | tf_op jit(solution)/shard_map/ppermute | solution.py:24
  72.1 13.2 %collective-permute-start.25 = (bf16[256,512]{1,0:T(8,128)(2,1)S(1)}, bf16[256,512]{1,0:T(8,128)(2,1)S(1)}, u32[]{:S(2)}, u32[]{:S(2)}) collective-permute-start(bf16[256,512]{1,0:T(8,128)(2,1)S(1)} %get-tuple-element.115), channel_id=1, source_target_pairs={{0,1},{1,0},{2,3},{3,2},{4,5},{5,4},{6,7},{7,6},{8,9},{9,8},{10,11... | collective-permute-start | bytes 786440 | tf_op jit(solution)/shard_map/ppermute | solution.py:24
  72.2 13.1 %collective-permute-start.26 = (bf16[256,512]{1,0:T(8,128)(2,1)S(1)}, bf16[256,512]{1,0:T(8,128)(2,1)S(1)}, u32[]{:S(2)}, u32[]{:S(2)}) collective-permute-start(bf16[256,512]{1,0:T(8,128)(2,1)S(1)} %add_convert_fusion), channel_id=1, source_target_pairs={{0,28},{1,29},{2,30},{3,31},{4,0},{5,1},{6,2},{7,3},{8,4},{9,5},{1... | collective-permute-start | bytes 786440 | tf_op jit(solution)/shard_map/ppermute | solution.py:24
  75.3 11.8 %collective-permute-start.21 = (bf16[256,256]{1,0:T(8,128)(2,1)S(1)}, bf16[256,256]{1,0:T(8,128)(2,1)S(1)}, u32[]{:S(2)}, u32[]{:S(2)}) collective-permute-start(bf16[256,256]{1,0:T(8,128)(2,1)S(1)} %add_text.2), channel_id=1, source_target_pairs={{0,8},{1,9},{2,10},{3,11},{4,12},{5,13},{6,14},{7,15},{8,16},{9,17... | collective-permute-start | bytes 393224 | tf_op jit(solution)/shard_map/ppermute | solution.py:24
  77.4 7.9 %collective-permute-start.24 = (bf16[512,256]{1,0:T(8,128)(2,1)S(1)}, bf16[512,256]{1,0:T(8,128)(2,1)S(1)}, u32[]{:S(2)}, u32[]{:S(2)}) collective-permute-start(bf16[512,256]{1,0:T(8,128)(2,1)S(1)} %get-tuple-element.113), channel_id=1, source_target_pairs={{0,2},{1,3},{2,0},{3,1},{4,6},{5,7},{6,4},{7,5},{8,10},{9,11},{10,... | collective-permute-start | bytes 786440 | tf_op jit(solution)/shard_map/ppermute | solution.py:24
  78.5 8.6 %collective-permute-start.23 = (bf16[256,256]{1,0:T(8,128)(2,1)S(1)}, bf16[256,256]{1,0:T(8,128)(2,1)S(1)}, u32[]{:S(2)}, u32[]{:S(2)}) collective-permute-start(bf16[256,256]{1,0:T(8,128)(2,1)S(1)} %add_text.3), channel_id=1, source_target_pairs={{0,8},{1,9},{2,10},{3,11},{4,12},{5,13},{6,14},{7,15},{8,16},{9,17... | collective-permute-start | bytes 393224 | tf_op jit(solution)/shard_map/ppermute | solution.py:24

commit v2 on v1

--- a/solution.py
+++ b/solution.py
@@ -136,30 +136,54 @@
     return texts + [refs[whole : whole + 2]], refs[whole + 2 :]
 
 
-def part_kernel(shard, scales, spans, size, count, *refs):
-    images, refs = (refs[:size], refs[size : 2 * size]), refs[2 * size :]
+def part_kernel(shard, scales, spans, sizes, count, *refs):
+    images = []
+    for size in sizes:
+        images.append(refs[:size])
+        refs = refs[size:]
     texts, refs = text_parts(refs, count)
-    others, refs = (refs[:4], refs[4:]) if len(refs) > 6 else ((), refs)
-    outs, (row_out, col_out), stat_out = refs[:4], refs[4:6], refs[6:]
+    outs, (row_out, col_out) = refs[:4], refs[4:]
     stats = score_shards(images, texts, spans, scales, outs, shard)
     for index, (row, column) in enumerate(stats):
         row_out[:, pl.ds(index * shard, shard)] = as_rows(row, shard)
         for k, value in enumerate(column):
             col_out[4 * index + k : 4 * index + k + 1] = value
-    if not others:
-        return
-    row_home, col_home, row_side, col_side = others
-    rows = joined(rows4(row_home, 0), rows4(row_side, 0))
-    columns = joined(rows4(col_out, 0), rows4(col_out, 4))
-    seen = joined(rows4(col_home, 0), rows4(col_home, 4))
-    seen = joined(seen, [part[:, : 3 * shard] for part in columns])
-    last = joined(rows4(col_side, 0), rows4(col_side, 4))
-    last = joined(last, [part[:, 3 * shard :] for part in columns])
+
+
+def far_kernel(shard, scales, spans, *refs):
+    outs = refs[13:]
+    part_kernel(shard, scales, spans, (2,), 4, *refs[:7], *outs[:6])
+    total_kernel(shard, *refs[7:13], outs[4], outs[5], outs[6])
+
+
+HOME, NEAR, SIDE, FAR = range(4)
+
+
+def join_calls(rows_in, cols_in, shard):
+    rows = []
+    for index in range(3):
+        call, place = (HOME, index) if index < 2 else (NEAR, 0)
+        first = rows4(rows_in[call], 0, pl.ds(place * shard, shard))
+        rows.append(joined(first, rows4(rows_in[SIDE], 0, pl.ds(index * shard, shard))))
+    rows.append(rows4(rows_in[FAR], 0))
+    columns = rows4(cols_in[FAR], 0)
+    seen = [part[:, : 3 * shard] for part in columns]
+    last = [part[:, 3 * shard :] for part in columns]
+    for call, place in ((HOME, 0), (HOME, 1), (NEAR, 0)):
+        seen = joined(seen, rows4(cols_in[call], 4 * place))
+    for place in range(3):
+        last = joined(last, rows4(cols_in[SIDE], 4 * place))
+    return rows, seen, last
+
+
+def total_kernel(shard, *refs):
+    rows, seen, last = join_calls(refs[0:8:2], refs[1:8:2], shard)
+    out = refs[8]
     for k in range(4):
-        stat_out[0][k : k + 1, : 2 * shard] = rows[k]
-        stat_out[0][k : k + 1, 2 * shard :] = row_out[k : k + 1]
-        stat_out[0][4 + k : 5 + k, : 3 * shard] = seen[k]
-        stat_out[0][4 + k : 5 + k, 3 * shard :] = last[k]
+        for index in range(4):
+            out[k : k + 1, index * shard : (index + 1) * shard] = rows[index][k]
+        out[4 + k : 5 + k, : 3 * shard] = seen[k]
+        out[4 + k : 5 + k, 3 * shard :] = last[k]
 
 
 def piece_stats(ref, kind, piece, shard):
@@ -253,10 +277,10 @@
 
 
 def ahead_kernel(shard, span, *refs):
-    below_home, below_side, below_behind = refs[0:4], refs[4:8], refs[8:12]
-    rows_in, cols_in, stat_ref = refs[12:18:2], refs[13:18:2], refs[18]
-    images = (refs[19:20], refs[20:21], refs[21:23], refs[23:25])
-    texts, refs = text_parts(refs[25:], 4)
+    below, refs = (refs[0:4], refs[4:8], refs[8:12], refs[12:16]), refs[16:]
+    rows_in, cols_in, stat_ref = refs[0:8:2], refs[1:8:2], refs[8]
+    images = (refs[9:10], refs[10:11], refs[11:13], refs[13:15])
+    texts, refs = text_parts(refs[15:], 4)
     same_out, cross_out, weights_out, img_out, both_out = (
         refs[0:2], refs[2:4], refs[4], refs[5:7], refs[7]
     )
@@ -267,26 +291,27 @@
     )
 
     def weights_of(index):
-        here = pl.ds((index % 2) * shard, shard)
-        at = 4 * (index % 2)
-        if index < 2:
-            tops = (rows4(rows_in[0], 0, here), rows4(rows_in[1], 0, here))
-            row = row_factors(stat_ref, tops, index, shard)
-            seen = rows4(cols_in[0], at, third)
-            weights = jnp.concatenate(
-                [
-                    weigh(below_home, here, third, row[:2], seen, col_third),
-                    weigh(
-                        below_side, here, slice(None), row[2:], rows4(cols_in[1], at), col_last
-                    ),
-                ],
-                axis=1,
+        if index == 3:
+            here = pl.ds(0, shard)
+            row = row_factors(stat_ref, (rows4(rows_in[FAR], 0),), index, shard)
+            weights, near = (
+                weigh(below[FAR], here, at, row, rows4(cols_in[FAR], 0, at), columns)
+                for at, columns in ((far, col_far), (home, col_home))
             )
-        else:
-            row = row_factors(stat_ref, (rows4(rows_in[2], 0, here),), index, shard)
-            weights = weigh(below_behind, here, far, row, rows4(cols_in[2], at, far), col_far)
-            near = weigh(below_behind, here, home, row, rows4(cols_in[2], at, home), col_home)
-        return weights, None if index < 2 else near
+            return weights, near
+        call, place = (HOME, index) if index < 2 else (NEAR, 0)
+        here, side = pl.ds(place * shard, shard), pl.ds(index * shard, shard)
+        tops = (rows4(rows_in[call], 0, here), rows4(rows_in[SIDE], 0, side))
+        row = row_factors(stat_ref, tops, index, shard)
+        seen = rows4(cols_in[call], 4 * place, third)
+        weights = [weigh(below[call], here, third, row[:2], seen, col_third)]
+        seen = rows4(cols_in[SIDE], 4 * index)
+        weights.append(weigh(below[SIDE], side, slice(None), row[2:], seen, col_last))
+        near = None
+        if index == 2:
+            seen = rows4(cols_in[call], 4 * place, home)
+            near = weigh(below[call], here, home, row[:2], seen, col_home)
+        return jnp.concatenate(weights, axis=1), near
 
     total = both = None
     ready = weights_of(0)
@@ -410,36 +435,47 @@
     def score(rows, columns):
         return jax.ShapeDtypeStruct((rows * shard, columns * shard), f32)
 
-    def part_scores(shards, texts, *others, name, cost=None):
-        size, count = len(shards[0]), {3: 3, 2: 1, 5: 4}[len(texts)]
-        outs = (score(2, count),) * 4 + (stat(2), stat(count)) + (stat(4),) * bool(others)
-        return pl.pallas_call(
-            lambda *refs: part_kernel(shard, scales, spans, size, count, *refs),
+    def part_scores(shards, texts, name, cost=None):
+        sizes, count = tuple(len(parts) for parts in shards), {3: 3, 2: 1, 5: 4}[len(texts)]
+        outs = (score(len(sizes), count),) * 4
+        outs += (stat(len(sizes)), jax.ShapeDtypeStruct((4 * len(sizes), count * shard), f32))
+        args = [part for parts in shards for part in parts] + list(texts)
+        *below, row, col = pl.pallas_call(
+            lambda *refs: part_kernel(shard, scales, spans, sizes, count, *refs),
             out_shape=outs,
-            in_specs=[vmem] * (2 * size + len(texts) + len(others)),
+            in_specs=[vmem] * len(args),
             out_specs=(vmem,) * len(outs),
             compiler_params=params(16),
             cost_estimate=cost,
             name=name,
-        )(*shards[0], *shards[1], *texts, *others)
+        )(*args)
+        return below, [row, col]
 
     text_both = (ahead(text_part, -2), to_other_x(rest))
     top = send_to(top, lambda block, x, core: (block + 2 - block % 2 * 2, x, core))
     bottom = ahead(bottom, 1)
     texts = (text, text_x, text_ahead, *text_both)
     own = ((image,), (image_core,))
-    *below_home, row_home, col_home = part_scores(own, texts[:3], name="scores_home")
-    *below_side, row_side, col_side = part_scores(own, texts[3:], name="scores_side", cost=HEAVY)
-    top, bottom = lax.optimization_barrier((top, bottom, row_home))[:2]
+    home, home_stats = part_scores(own, texts[:3], "scores_home")
+    top, bottom = lax.optimization_barrier((top, bottom, home_stats[0]))[:2]
     behind = ((top, bottom), (to_other_core(top), to_other_core(bottom)))
+    near, near_stats = part_scores(behind[:1], texts[:3], "scores_near")
+    side, side_stats = part_scores((*own, behind[0]), texts[3:], "scores_side", HEAVY)
+    others = (*home_stats, *near_stats, *side_stats)
+    *far, far_row, far_col, partial = pl.pallas_call(
+        lambda *refs: far_kernel(shard, scales, spans, *refs),
+        out_shape=(score(1, 4),) * 4
+        + (stat(1), jax.ShapeDtypeStruct((4, 4 * shard), f32), stat(4)),
+        in_specs=[vmem] * 13,
+        out_specs=(vmem,) * 7,
+        compiler_params=params(16),
+        name="scores_far",
+    )(*behind[1], *texts, *others)
     images = (image, image_core, *behind[0], *behind[1])
-    stats_own = (row_home, col_home, row_side, col_side)
-    *below_behind, row_behind, col_behind, partial = part_scores(
-        behind, texts, *stats_own, name="scores_behind"
-    )
+    calls_stats = (*others, far_row, far_col)
 
     shared = jax.ShapeDtypeStruct((8, 2 * shard), f32)
-    home, *away = pl.pallas_call(
+    group, *away = pl.pallas_call(
         lambda *refs: join_group_kernel(shard, *refs),
         out_shape=(stat(4),) + (shared,) * 4,
         in_specs=[vmem] * 3,
@@ -460,7 +496,7 @@
         out_specs=vmem,
         compiler_params=params(8),
         name="join_blocks",
-    )(home, *away)
+    )(group, *away)
 
     wide = jax.ShapeDtypeStruct((shard, width_s), f32)
     tall = jax.ShapeDtypeStruct((width_s, shard), f32)
@@ -480,12 +516,12 @@
             flat,
             jax.ShapeDtypeStruct((width_s, 2 * shard), f32),
         ),
-        in_specs=[vmem] * 30,
+        in_specs=[vmem] * 36,
         out_specs=(vmem,) * 8,
         compiler_params=params(24),
         name="gradients_ahead",
     )(
-        *below_home, *below_side, *below_behind, *stats_own, row_behind, col_behind, stats,
+        *home, *near, *side, *far, *calls_stats, stats,
         *images, *texts,
     )
     img_own, img_core, txt_own, txt_x = pl.pallas_call(
@@ -495,7 +531,7 @@
         out_specs=(vmem,) * 4,
         compiler_params=params(24),
         name="gradients_home",
-    )(*below_home, row_home, col_home, stats, *images[:2], *texts, weights, txt_both)
+    )(*home, *home_stats, stats, *images[:2], *texts, weights, txt_both)
 
     img_cross = to_other_core(img_cross)
     img_sum = (img_back + img_cross.astype(f32)).astype(bf16)

time: 88.4 us -> 87.9 us (level)
  waiting for transfers between devices: 40.5 us -> 38.7 us
  Pallas kernels: 12.8 us -> 13.9 us
    ppermute x27, waiting for transfers between devices: 40.5 us -> 38.7 us  [send_to(): return lax.ppermute(value, AXES, pairs)]
    pallas_call x3 -> x4, Pallas kernels: 6.47 us -> 7.2 us  [the longest x3 5.34 us: part_scores(): pl.pallas_call(lambda *refs: part_kernel(shard, scales, spans, sizes, cou...]
  transfers between devices with their start and end apart: 27 -> 27, of which waited for: 13 -> 11; matrix products, arithmetic and copies ran while one was open for 0% -> 0% of each run, Pallas kernels for 7% -> 9%
where the time goes in v2:
time: 87.9 us; the launch traced here: 87.7 us
  waiting for transfers between devices  38.7 us (44%)
  starting transfers between devices  32.2 us (37%)
  Pallas kernels  13.9 us (16%)
  local copies, waits for them, and re-layouts  2.04 us (2%)
    ppermute x27, waiting for transfers between devices, send_to(): return lax.ppermute(value, AXES, pairs)  38.7 us
    ppermute x27, starting transfers between devices, send_to(): return lax.ppermute(value, AXES, pairs)  32.2 us
    pallas_call x3, Pallas kernels, part_scores(): pl.pallas_call(lambda *refs: part_kernel(shard, scales, spans, sizes, cou...  5.34 us
    pallas_call x1, Pallas kernels, on_device(): pl.pallas_call(lambda *refs: ahead_kernel(shard, spans[0], *refs), out_sh...  2.67 us
    unnamed x8, local copies, waits for them, and re-layouts  2.04 us
    pallas_call x2, Pallas kernels, finish(): pl.pallas_call(lambda *refs: kernel(scale_s, *refs), out_shape=wide, in_s...  1.89 us
    pallas_call x1, Pallas kernels, on_device(): pl.pallas_call(lambda *refs: far_kernel(shard, scales, spans, *refs), out...  1.86 us
  transfers between devices with their start and end apart: 27, of which 11 were waited for; matrix products, arithmetic and copies ran while one was open for 0% of the time, Pallas kernels for 9%

profile of v2, /device:TPU:0, one launch (start us, length us, event | category | flops | bytes accessed | tf_op | source)
XLA Modules:
  0.0 87.7 jit_solution(12829077700561311167)
XLA Ops:
  0.6 0.5 collective-permute-start.1
  1.2 0.1 collective-permute-start
  1.2 2.9 %collective-permute-start.6 = (bf16[256,1280]{1,0:T(8,128)(2,1)}, bf16[256,1280]{1,0:T(8,128)(2,1)S(1)}, u32[]{:S(2)}, u32[]{:S(2)}) collective-permute-start(bf16[256,1280]{1,0:T(8,128)(2,1)} %second.3), channel_id=1, source_target_pairs={{0,2},{1,3},{2,0},{3,1},{4,6},{5,7},{6,4},{7,5},{8,10},{9,11},{10,... | collective-permute-start | bytes 1966088 | tf_op jit(solution)/shard_map/ppermute | solution.py:24
  4.2 3.6 %collective-permute-start.4 = (bf16[256,1280]{1,0:T(8,128)(2,1)}, bf16[256,1280]{1,0:T(8,128)(2,1)S(1)}, u32[]{:S(2)}, u32[]{:S(2)}) collective-permute-start(bf16[256,1280]{1,0:T(8,128)(2,1)} %second.3), channel_id=1, source_target_pairs={{0,24},{1,25},{2,26},{3,27},{4,28},{5,29},{6,30},{7,31},{8,0},{9,1... | collective-permute-start | bytes 1966088 | tf_op jit(solution)/shard_map/ppermute | solution.py:24
  7.8 1.1 %copy-done.1 = bf16[256,1280]{1,0:T(8,128)(2,1)S(1)} copy-done((bf16[256,1280]{1,0:T(8,128)(2,1)S(1)}, bf16[256,1280]{1,0:T(8,128)(2,1)}, u32[]{:S(2)}) %copy-start.1) | copy-done | bytes 655384
  8.8 0.9 %copy-done.2 = bf16[256,512]{1,0:T(8,128)(2,1)S(1)} copy-done((bf16[256,512]{1,0:T(8,128)(2,1)S(1)}, bf16[256,512]{1,0:T(8,128)(2,1)}, u32[]{:S(2)}) %copy-start.2) | copy-done | bytes 262168
  9.8 0.1 pack_images.1
  9.9 1.6 %collective-permute-start.2 = (bf16[128,1792]{1,0:T(8,128)(2,1)S(1)}, bf16[128,1792]{1,0:T(8,128)(2,1)S(1)}, u32[]{:S(2)}, u32[]{:S(2)}) collective-permute-start(bf16[128,1792]{1,0:T(8,128)(2,1)S(1)} %get-tuple-element.71), channel_id=1, source_target_pairs={{0,4},{1,5},{2,6},{3,7},{4,0},{5,1},{6,2},{7,3},{8,12},{9,13},{10,... | collective-permute-start | bytes 1376264 | tf_op jit(solution)/shard_map/ppermute | solution.py:24
  11.5 0.5 collective-permute-start.5
  12.1 0.4 collective-permute-start.3
  12.5 12.4 %collective-permute-done.5.s_x = bf16[256,512]{1,0:T(8,128)(2,1)S(1)} collective-permute-done((bf16[256,512]{1,0:T(8,128)(2,1)}, bf16[256,512]{1,0:T(8,128)(2,1)S(1)}, u32[]{:S(2)}, u32[]{:S(2)}) %collective-permute-start.5) | collective-permute-done | bytes 262176 | tf_op jit(solution)/shard_map/ppermute | solution.py:24
  25.0 2.7 %collective-permute-done.3.s_ahead = bf16[256,512]{1,0:T(8,128)(2,1)S(1)} collective-permute-done((bf16[256,512]{1,0:T(8,128)(2,1)}, bf16[256,512]{1,0:T(8,128)(2,1)S(1)}, u32[]{:S(2)}, u32[]{:S(2)}) %collective-permute-start.3) | collective-permute-done | bytes 262176 | tf_op jit(solution)/shard_map/ppermute | solution.py:24
  27.7 0.2 pack_arrived.1
  27.8 0.6 collective-permute-start.10
  28.4 2.2 %collective-permute-start.7 = (bf16[128,1792]{1,0:T(8,128)(2,1)S(1)}, bf16[128,1792]{1,0:T(8,128)(2,1)S(1)}, u32[]{:S(2)}, u32[]{:S(2)}) collective-permute-start(bf16[128,1792]{1,0:T(8,128)(2,1)S(1)} %collective-permute-done.2), channel_id=1, source_target_pairs={{0,8},{1,9},{2,10},{3,11},{4,4},{5,5},{6,6},{7,7},{8,16},{9,17},{1... | collective-permute-start | bytes 1376264 | tf_op jit(solution)/shard_map/ppermute | solution.py:24
  30.8 4.1 %collective-permute-start.9 = (bf16[32,1792]{1,0:T(8,128)(2,1)S(1)}, bf16[32,1792]{1,0:T(8,128)(2,1)S(1)}, u32[]{:S(2)}, u32[]{:S(2)}) collective-permute-start(bf16[32,1792]{1,0:T(8,128)(2,1)S(1)} %get-tuple-element.90), channel_id=1, source_target_pairs={{0,24},{1,25},{2,26},{3,27},{4,28},{5,29},{6,30},{7,31},{8,0},{9,1... | collective-permute-start | bytes 344072 | tf_op jit(solution)/shard_map/ppermute | solution.py:24
  35.0 2.5 %scores_home.1 = (f32[512,768]{1,0:T(8,128)S(1)}, f32[512,768]{1,0:T(8,128)S(1)}, f32[512,768]{1,0:T(8,128)S(1)}, f32[512,768]{1,0:T(8,128)S(1)}, f32[8,512]{1,0:T(8,128)S(1)}, /*index=5*/f32[8,768]{1,0:T(8,128)S(1)}) custom-call(bf16[256,1792]{1,0:T(8,128)(2,1)S(1)} %get-tuple-element.67.refs_0_.refs_25_.refs_7_, ...), custom_call_target="tpu_custom_call" | custom-call | tf_op jit(solution)/shard_map/scores_home/pallas_call | solution.py:443
  37.5 7.7 %collective-permute-done.7.refs_0_.refs_2_.refs_27_ = bf16[128,1792]{1,0:T(8,128)(2,1)S(1)} collective-permute-done((bf16[128,1792]{1,0:T(8,128)(2,1)S(1)}, bf16[128,1792]{1,0:T(8,128)(2,1)S(1)}, u32[]{:S(2)}, u32[]{:S(2)}) %collective-permute-start.7) | collective-permute-done | bytes 458784 | tf_op jit(solution)/shard_map/ppermute | solution.py:24
  45.2 0.5 collective-permute-done.8.refs_1_.refs_3_.refs_28_
  45.7 0.5 collective-permute-start.12
  46.2 1.5 %scores_near.1 = (f32[256,768]{1,0:T(8,128)S(1)}, f32[256,768]{1,0:T(8,128)S(1)}, f32[256,768]{1,0:T(8,128)S(1)}, f32[256,768]{1,0:T(8,128)S(1)}, f32[8,256]{1,0:T(8,128)S(1)}, /*index=5*/f32[4,768]{1,0:T(4,128)S(1)}) custom-call(bf16[128,1792]{1,0:T(8,128)(2,1)S(1)} %collective-permute-done.7.refs_0_.refs_2_.refs_27_, ...), custom_call_target="tpu_custom_call" | custom-call | tf_op jit(solution)/shard_map/scores_near/pallas_call | solution.py:443
  47.7 1.4 %scores_side.1 = (f32[768,256]{1,0:T(8,128)S(1)}, f32[768,256]{1,0:T(8,128)S(1)}, f32[768,256]{1,0:T(8,128)S(1)}, f32[768,256]{1,0:T(8,128)S(1)}, f32[8,768]{1,0:T(8,128)S(1)}, /*index=5*/f32[12,256]{1,0:T(8,128)S(1)}) custom-call(bf16[256,1792]{1,0:T(8,128)(2,1)S(1)} %get-tuple-element.67.refs_0_.refs_25_.refs_7_, ...), custom_call_target="tpu_custom_call" | custom-call | flops 99999997952 | bytes 1000000000 | tf_op jit(solution)/shard_map/scores_side/pallas_call | solution.py:443
  49.1 1.9 %scores_far.1 = (f32[256,1024]{1,0:T(8,128)S(1)}, f32[256,1024]{1,0:T(8,128)S(1)}, f32[256,1024]{1,0:T(8,128)S(1)}, f32[256,1024]{1,0:T(8,128)S(1)}, f32[8,256]{...) custom-call(bf16[128,1792]{1,0:T(8,128)(2,1)S(1)} %collective-permute-done.11.refs_0_.refs_29_, ...), custom_call_target="tpu_custom_call" | custom-call | tf_op jit(solution)/shard_map/scores_far/pallas_call | solution.py:465
  51.0 1.4 %collective-permute-start.14 = (f32[8,1024]{1,0:T(8,128)S(1)}, f32[8,1024]{1,0:T(8,128)S(1)}, u32[]{:S(2)}, u32[]{:S(2)}) collective-permute-start(f32[8,1024]{1,0:T(8,128)S(1)} %get-tuple-element.107.refs_0_), channel_id=1, source_target_pairs={{0,2},{1,3},{2,0},{3,1},{4,6},{5,7},{6,4},{7,5},{8,10},{9,11},{10,... | collective-permute-start | bytes 98312 | tf_op jit(solution)/shard_map/ppermute | solution.py:24
  52.4 2.5 %collective-permute-done.14.refs_2_ = f32[8,1024]{1,0:T(8,128)S(1)} collective-permute-done((f32[8,1024]{1,0:T(8,128)S(1)}, f32[8,1024]{1,0:T(8,128)S(1)}, u32[]{:S(2)}, u32[]{:S(2)}) %collective-permute-start.14) | collective-permute-done | bytes 32800 | tf_op jit(solution)/shard_map/ppermute | solution.py:24
  55.0 0.5 collective-permute-start.15
  55.5 4.3 %collective-permute-start.16 = (f32[8,512]{1,0:T(8,128)S(1)}, f32[8,512]{1,0:T(8,128)S(1)}, u32[]{:S(2)}, u32[]{:S(2)}) collective-permute-start(f32[8,512]{1,0:T(8,128)S(1)} %get-tuple-element.110), channel_id=1, source_target_pairs={{0,28},{1,29},{2,30},{3,31},{4,8},{5,9},{6,10},{7,11},{8,4},{9,5},... | collective-permute-start | bytes 49160 | tf_op jit(solution)/shard_map/ppermute | solution.py:24
  59.8 1.7 %collective-permute-start.18 = (f32[8,512]{1,0:T(8,128)S(1)}, f32[8,512]{1,0:T(8,128)S(1)}, u32[]{:S(2)}, u32[]{:S(2)}) collective-permute-start(f32[8,512]{1,0:T(8,128)S(1)} %get-tuple-element.112), channel_id=1, source_target_pairs={{0,24},{1,25},{2,26},{3,27},{4,28},{5,29},{6,30},{7,31},{8,16},{9,... | collective-permute-start | bytes 49160 | tf_op jit(solution)/shard_map/ppermute | solution.py:24
  61.5 0.5 collective-permute-done.16.refs_2_
  62.0 1.5 %collective-permute-done.17.refs_3_ = f32[8,512]{1,0:T(8,128)S(1)} collective-permute-done((f32[8,512]{1,0:T(8,128)S(1)}, f32[8,512]{1,0:T(8,128)S(1)}, u32[]{:S(2)}, u32[]{:S(2)}) %collective-permute-start.17) | collective-permute-done | bytes 16416 | tf_op jit(solution)/shard_map/ppermute | solution.py:24
  63.5 1.8 %collective-permute-done.18.refs_4_ = f32[8,512]{1,0:T(8,128)S(1)} collective-permute-done((f32[8,512]{1,0:T(8,128)S(1)}, f32[8,512]{1,0:T(8,128)S(1)}, u32[]{:S(2)}, u32[]{:S(2)}) %collective-permute-start.18) | collective-permute-done | bytes 16416 | tf_op jit(solution)/shard_map/ppermute | solution.py:24
  65.4 2.7 %gradients_ahead.1 = (f32[256,256]{1,0:T(8,128)S(1)}, f32[256,256]{1,0:T(8,128)S(1)}, bf16[256,256]{1,0:T(8,128)(2,1)S(1)}, bf16[256,256]{1,0:T(8,128)(2,1)S(1)}...) custom-call(f32[512,768]{1,0:T(8,128)S(1)} %get-tuple-element.77.ref, ...), custom_call_target="tpu_custom_call" | custom-call | tf_op jit(solution)/shard_map/gradients_ahead/pallas_call | solution.py:507
  68.1 0.1 collective-permute-start.20
  68.2 1.6 %collective-permute-start.19 = (bf16[256,256]{1,0:T(8,128)(2,1)S(1)}, bf16[256,256]{1,0:T(8,128)(2,1)S(1)}, u32[]{:S(2)}, u32[]{:S(2)}) collective-permute-start(bf16[256,256]{1,0:T(8,128)(2,1)S(1)} %get-tuple-element.114), channel_id=1, source_target_pairs={{0,2},{1,3},{2,0},{3,1},{4,6},{5,7},{6,4},{7,5},{8,10},{9,11},{10,... | collective-permute-start | bytes 393224 | tf_op jit(solution)/shard_map/ppermute | solution.py:24
  69.7 0.5 collective-permute-start.22
  70.2 1.5 %gradients_home.1 = (f32[256,512]{1,0:T(8,128)S(1)}, bf16[256,512]{1,0:T(8,128)(2,1)S(1)}, f32[512,256]{1,0:T(8,128)S(1)}, bf16[512,256]{1,0:T(8,128)(2,1)S(1)}) custom-call(f32[512,768]{1,0:T(8,128)S(1)} %get-tuple-element.77.refs_0_, f32[512,768]{1,0:T(8,128)S(1)} %get-tuple-element.78.refs_1_, f32[512,768]{1,0:T(8,128)S(1)} %get-tuple-element.79.refs_2_, ...), custom_call_target="tpu_custom_call" | custom-call | tf_op jit(solution)/shard_map/gradients_home/pallas_call | solution.py:527
  71.7 0.1 collective-permute-start.25
  71.8 0.1 add_convert_fusion
  71.9 2.8 %collective-permute-start.26 = (bf16[256,512]{1,0:T(8,128)(2,1)S(1)}, bf16[256,512]{1,0:T(8,128)(2,1)S(1)}, u32[]{:S(2)}, u32[]{:S(2)}) collective-permute-start(bf16[256,512]{1,0:T(8,128)(2,1)S(1)} %add_convert_fusion), channel_id=1, source_target_pairs={{0,28},{1,29},{2,30},{3,31},{4,0},{5,1},{6,2},{7,3},{8,4},{9,5},{1... | collective-permute-start | bytes 786440 | tf_op jit(solution)/shard_map/ppermute | solution.py:24
  74.8 0.1 collective-permute-start.21
  74.8 2.0 %collective-permute-done.22.second = bf16[256,256]{1,0:T(8,128)(2,1)S(1)} collective-permute-done((bf16[256,256]{1,0:T(8,128)(2,1)S(1)}, bf16[256,256]{1,0:T(8,128)(2,1)S(1)}, u32[]{:S(2)}, u32[]{:S(2)}) %collective-permute-start.22) | collective-permute-done | bytes 131104 | tf_op jit(solution)/shard_map/ppermute | solution.py:24
  76.9 1.5 %collective-permute-start.24 = (bf16[512,256]{1,0:T(8,128)(2,1)S(1)}, bf16[512,256]{1,0:T(8,128)(2,1)S(1)}, u32[]{:S(2)}, u32[]{:S(2)}) collective-permute-start(bf16[512,256]{1,0:T(8,128)(2,1)S(1)} %get-tuple-element.125), channel_id=1, source_target_pairs={{0,2},{1,3},{2,0},{3,1},{4,6},{5,7},{6,4},{7,5},{8,10},{9,11},{10,... | collective-permute-start | bytes 786440 | tf_op jit(solution)/shard_map/ppermute | solution.py:24
  78.4 0.3 collective-permute-start.23
  78.7 6.1 %collective-permute-done.24.second = bf16[512,256]{1,0:T(8,128)(2,1)S(1)} collective-permute-done((bf16[512,256]{1,0:T(8,128)(2,1)S(1)}, bf16[512,256]{1,0:T(8,128)(2,1)S(1)}, u32[]{:S(2)}, u32[]{:S(2)}) %collective-permute-start.24) | collective-permute-done | bytes 262176 | tf_op jit(solution)/shard_map/ppermute | solution.py:24
  84.7 0.1 add_own_text.1.refs_0_
  84.8 0.9 %finish_image.1 = f32[256,512]{1,0:T(8,128)} custom-call(f32[256,512]{1,0:T(8,128)S(1)} %get-tuple-element.126.refs_0_, bf16[256,512]{1,0:T(8,128)(2,1)S(1)} %collective-permute-done.25.refs_1_, bf16[256,512]{1,0:T(8,128)(2,1)S(1)} %collective-permute-done.26.refs_2_), custom_call_target="tpu_custom_call" | custom-call | tf_op jit(solution)/shard_map/finish_image/pallas_call | solution.py:562
  85.7 0.9 %collective-permute-done.23.refs_2_ = bf16[256,256]{1,0:T(8,128)(2,1)S(1)} collective-permute-done((bf16[256,256]{1,0:T(8,128)(2,1)S(1)}, bf16[256,256]{1,0:T(8,128)(2,1)S(1)}, u32[]{:S(2)}, u32[]{:S(2)}) %collective-permute-start.23) | collective-permute-done | bytes 131104 | tf_op jit(solution)/shard_map/ppermute | solution.py:24
  86.7 1.0 %finish_text.1 = f32[256,512]{1,0:T(8,128)} custom-call(f32[512,256]{1,0:T(8,128)S(1)} %add_own_text.1.refs_0_, bf16[256,256]{1,0:T(8,128)(2,1)S(1)} %collective-permute-done.21.refs_1_, bf16[256,256]{1,0:T(8,128)(2,1)S(1)} %collective-permute-done.23.refs_2_), custom_call_target="tpu_custom_call" | custom-call | tf_op jit(solution)/shard_map/finish_text/pallas_call | solution.py:562
  (32 shorter events, 0.4 us)
Async XLA Ops:
  0.6 34.3 %copy-start = (bf16[256,1280]{1,0:T(8,128)(2,1)S(1)}, bf16[256,1280]{1,0:T(8,128)(2,1)}, u32[]{:S(2)}) copy-start(bf16[256,1280]{1,0:T(8,128)(2,1)} %second.3) | copy-start | bytes 1966084
  0.6 9.3 %collective-permute-start.1 = (bf16[256,1280]{1,0:T(8,128)(2,1)}, bf16[256,1280]{1,0:T(8,128)(2,1)S(1)}, u32[]{:S(2)}, u32[]{:S(2)}) collective-permute-start(bf16[256,1280]{1,0:T(8,128)(2,1)} %second.2), channel_id=1, source_target_pairs={{0,1},{1,0},{2,3},{3,2},{4,5},{5,4},{6,7},{7,6},{8,9},{9,8},{10,11... | collective-permute-start | bytes 1966088 | tf_op jit(solution)/shard_map/ppermute | solution.py:24
  1.2 8.8 %collective-permute-start = (bf16[256,512]{1,0:T(8,128)(2,1)}, bf16[256,512]{1,0:T(8,128)(2,1)S(1)}, u32[]{:S(2)}, u32[]{:S(2)}) collective-permute-start(bf16[256,512]{1,0:T(8,128)(2,1)} %first.2), channel_id=1, source_target_pairs={{0,1},{1,0},{2,3},{3,2},{4,5},{5,4},{6,7},{7,6},{8,9},{9,8},{10,11... | collective-permute-start | bytes 786440 | tf_op jit(solution)/shard_map/ppermute | solution.py:24
  1.2 26.4 %collective-permute-start.6 = (bf16[256,1280]{1,0:T(8,128)(2,1)}, bf16[256,1280]{1,0:T(8,128)(2,1)S(1)}, u32[]{:S(2)}, u32[]{:S(2)}) collective-permute-start(bf16[256,1280]{1,0:T(8,128)(2,1)} %second.3), channel_id=1, source_target_pairs={{0,2},{1,3},{2,0},{3,1},{4,6},{5,7},{6,4},{7,5},{8,10},{9,11},{10,... | collective-permute-start | bytes 1966088 | tf_op jit(solution)/shard_map/ppermute | solution.py:24
  4.2 23.5 %collective-permute-start.4 = (bf16[256,1280]{1,0:T(8,128)(2,1)}, bf16[256,1280]{1,0:T(8,128)(2,1)S(1)}, u32[]{:S(2)}, u32[]{:S(2)}) collective-permute-start(bf16[256,1280]{1,0:T(8,128)(2,1)} %second.3), channel_id=1, source_target_pairs={{0,24},{1,25},{2,26},{3,27},{4,28},{5,29},{6,30},{7,31},{8,0},{9,1... | collective-permute-start | bytes 1966088 | tf_op jit(solution)/shard_map/ppermute | solution.py:24
  7.8 1.1 %copy-start.1 = (bf16[256,1280]{1,0:T(8,128)(2,1)S(1)}, bf16[256,1280]{1,0:T(8,128)(2,1)}, u32[]{:S(2)}) copy-start(bf16[256,1280]{1,0:T(8,128)(2,1)} %second.2) | copy-start | bytes 1966084
  8.8 0.9 %copy-start.2 = (bf16[256,512]{1,0:T(8,128)(2,1)S(1)}, bf16[256,512]{1,0:T(8,128)(2,1)}, u32[]{:S(2)}) copy-start(bf16[256,512]{1,0:T(8,128)(2,1)} %first.2) | copy-start | bytes 786436
  9.8 25.1 %copy-start.3 = (bf16[256,512]{1,0:T(8,128)(2,1)S(1)}, bf16[256,512]{1,0:T(8,128)(2,1)}, u32[]{:S(2)}) copy-start(bf16[256,512]{1,0:T(8,128)(2,1)} %first.3) | copy-start | bytes 786436
  9.9 17.7 %collective-permute-start.2 = (bf16[128,1792]{1,0:T(8,128)(2,1)S(1)}, bf16[128,1792]{1,0:T(8,128)(2,1)S(1)}, u32[]{:S(2)}, u32[]{:S(2)}) collective-permute-start(bf16[128,1792]{1,0:T(8,128)(2,1)S(1)} %get-tuple-element.71), channel_id=1, source_target_pairs={{0,4},{1,5},{2,6},{3,7},{4,0},{5,1},{6,2},{7,3},{8,12},{9,13},{10,... | collective-permute-start | bytes 1376264 | tf_op jit(solution)/shard_map/ppermute | solution.py:24
  11.5 13.4 %collective-permute-start.5 = (bf16[256,512]{1,0:T(8,128)(2,1)}, bf16[256,512]{1,0:T(8,128)(2,1)S(1)}, u32[]{:S(2)}, u32[]{:S(2)}) collective-permute-start(bf16[256,512]{1,0:T(8,128)(2,1)} %first.3), channel_id=1, source_target_pairs={{0,2},{1,3},{2,0},{3,1},{4,6},{5,7},{6,4},{7,5},{8,10},{9,11},{10,... | collective-permute-start | bytes 786440 | tf_op jit(solution)/shard_map/ppermute | solution.py:24
  12.1 15.6 %collective-permute-start.3 = (bf16[256,512]{1,0:T(8,128)(2,1)}, bf16[256,512]{1,0:T(8,128)(2,1)S(1)}, u32[]{:S(2)}, u32[]{:S(2)}) collective-permute-start(bf16[256,512]{1,0:T(8,128)(2,1)} %first.3), channel_id=1, source_target_pairs={{0,24},{1,25},{2,26},{3,27},{4,28},{5,29},{6,30},{7,31},{8,0},{9,1... | collective-permute-start | bytes 786440 | tf_op jit(solution)/shard_map/ppermute | solution.py:24
  27.8 19.8 %collective-permute-start.10 = (bf16[224,1792]{1,0:T(8,128)(2,1)S(1)}, bf16[224,1792]{1,0:T(8,128)(2,1)S(1)}, u32[]{:S(2)}, u32[]{:S(2)}) collective-permute-start(bf16[224,1792]{1,0:T(8,128)(2,1)S(1)} %get-tuple-element.91), channel_id=1, source_target_pairs={{0,2},{1,3},{2,0},{3,1},{4,6},{5,7},{6,4},{7,5},{8,10},{9,11},{10,... | collective-permute-start | bytes 2408456 | tf_op jit(solution)/shard_map/ppermute | solution.py:24
  28.4 16.7 %collective-permute-start.7 = (bf16[128,1792]{1,0:T(8,128)(2,1)S(1)}, bf16[128,1792]{1,0:T(8,128)(2,1)S(1)}, u32[]{:S(2)}, u32[]{:S(2)}) collective-permute-start(bf16[128,1792]{1,0:T(8,128)(2,1)S(1)} %collective-permute-done.2), channel_id=1, source_target_pairs={{0,8},{1,9},{2,10},{3,11},{4,4},{5,5},{6,6},{7,7},{8,16},{9,17},{1... | collective-permute-start | bytes 1376264 | tf_op jit(solution)/shard_map/ppermute | solution.py:24
  30.7 15.0 %collective-permute-start.8 = (bf16[128,1792]{1,0:T(8,128)(2,1)S(1)}, bf16[128,1792]{1,0:T(8,128)(2,1)S(1)}, u32[]{:S(2)}, u32[]{:S(2)}) collective-permute-start(bf16[128,1792]{1,0:T(8,128)(2,1)S(1)} %get-tuple-element.82), channel_id=1, source_target_pairs={{0,4},{1,5},{2,6},{3,7},{4,8},{5,9},{6,10},{7,11},{8,12},{9,13},{1... | collective-permute-start | bytes 1376264 | tf_op jit(solution)/shard_map/ppermute | solution.py:24
  30.8 16.9 %collective-permute-start.9 = (bf16[32,1792]{1,0:T(8,128)(2,1)S(1)}, bf16[32,1792]{1,0:T(8,128)(2,1)S(1)}, u32[]{:S(2)}, u32[]{:S(2)}) collective-permute-start(bf16[32,1792]{1,0:T(8,128)(2,1)S(1)} %get-tuple-element.90), channel_id=1, source_target_pairs={{0,24},{1,25},{2,26},{3,27},{4,28},{5,29},{6,30},{7,31},{8,0},{9,1... | collective-permute-start | bytes 344072 | tf_op jit(solution)/shard_map/ppermute | solution.py:24
  45.7 3.4 %collective-permute-start.11 = (bf16[128,1792]{1,0:T(8,128)(2,1)S(1)}, bf16[128,1792]{1,0:T(8,128)(2,1)S(1)}, u32[]{:S(2)}, u32[]{:S(2)}) collective-permute-start(bf16[128,1792]{1,0:T(8,128)(2,1)S(1)} %collective-permute-done.7.refs_0_.refs_2_.refs_27_), channel_id=1, source_target_pairs={{0,1},{1,0},{2,3},{3,2},{4,5},{5,4},{6,7},{7,6},{8,9},{9,8},{10,11... | collective-permute-start | bytes 1376264 | tf_op jit(solution)/shard_map/ppermute | solution.py:24
  45.7 3.4 %collective-permute-start.12 = (bf16[128,1792]{1,0:T(8,128)(2,1)S(1)}, bf16[128,1792]{1,0:T(8,128)(2,1)S(1)}, u32[]{:S(2)}, u32[]{:S(2)}) collective-permute-start(bf16[128,1792]{1,0:T(8,128)(2,1)S(1)} %collective-permute-done.8.refs_1_.refs_3_.refs_28_), channel_id=1, source_target_pairs={{0,1},{1,0},{2,3},{3,2},{4,5},{5,4},{6,7},{7,6},{8,9},{9,8},{10,11... | collective-permute-start | bytes 1376264 | tf_op jit(solution)/shard_map/ppermute | solution.py:24
  51.0 3.9 %collective-permute-start.14 = (f32[8,1024]{1,0:T(8,128)S(1)}, f32[8,1024]{1,0:T(8,128)S(1)}, u32[]{:S(2)}, u32[]{:S(2)}) collective-permute-start(f32[8,1024]{1,0:T(8,128)S(1)} %get-tuple-element.107.refs_0_), channel_id=1, source_target_pairs={{0,2},{1,3},{2,0},{3,1},{4,6},{5,7},{6,4},{7,5},{8,10},{9,11},{10,... | collective-permute-start | bytes 98312 | tf_op jit(solution)/shard_map/ppermute | solution.py:24
  52.4 2.5 %collective-permute-start.13 = (f32[8,1024]{1,0:T(8,128)S(1)}, f32[8,1024]{1,0:T(8,128)S(1)}, u32[]{:S(2)}, u32[]{:S(2)}) collective-permute-start(f32[8,1024]{1,0:T(8,128)S(1)} %get-tuple-element.107.refs_0_), channel_id=1, source_target_pairs={{0,1},{1,0},{2,3},{3,2},{4,5},{5,4},{6,7},{7,6},{8,9},{9,8},{10,11... | collective-permute-start | bytes 98312 | tf_op jit(solution)/shard_map/ppermute | solution.py:24
  55.0 6.6 %collective-permute-start.15 = (f32[8,512]{1,0:T(8,128)S(1)}, f32[8,512]{1,0:T(8,128)S(1)}, u32[]{:S(2)}, u32[]{:S(2)}) collective-permute-start(f32[8,512]{1,0:T(8,128)S(1)} %get-tuple-element.109), channel_id=1, source_target_pairs={{0,4},{1,5},{2,6},{3,7},{4,0},{5,1},{6,2},{7,3},{8,12},{9,13},{10,... | collective-permute-start | bytes 49160 | tf_op jit(solution)/shard_map/ppermute | solution.py:24
  55.5 6.5 %collective-permute-start.16 = (f32[8,512]{1,0:T(8,128)S(1)}, f32[8,512]{1,0:T(8,128)S(1)}, u32[]{:S(2)}, u32[]{:S(2)}) collective-permute-start(f32[8,512]{1,0:T(8,128)S(1)} %get-tuple-element.110), channel_id=1, source_target_pairs={{0,28},{1,29},{2,30},{3,31},{4,8},{5,9},{6,10},{7,11},{8,4},{9,5},... | collective-permute-start | bytes 49160 | tf_op jit(solution)/shard_map/ppermute | solution.py:24
  59.8 3.7 %collective-permute-start.17 = (f32[8,512]{1,0:T(8,128)S(1)}, f32[8,512]{1,0:T(8,128)S(1)}, u32[]{:S(2)}, u32[]{:S(2)}) collective-permute-start(f32[8,512]{1,0:T(8,128)S(1)} %get-tuple-element.111), channel_id=1, source_target_pairs={{0,8},{1,9},{2,10},{3,11},{4,12},{5,13},{6,14},{7,15},{8,0},{9,1},... | collective-permute-start | bytes 49160 | tf_op jit(solution)/shard_map/ppermute | solution.py:24
  59.8 5.5 %collective-permute-start.18 = (f32[8,512]{1,0:T(8,128)S(1)}, f32[8,512]{1,0:T(8,128)S(1)}, u32[]{:S(2)}, u32[]{:S(2)}) collective-permute-start(f32[8,512]{1,0:T(8,128)S(1)} %get-tuple-element.112), channel_id=1, source_target_pairs={{0,24},{1,25},{2,26},{3,27},{4,28},{5,29},{6,30},{7,31},{8,16},{9,... | collective-permute-start | bytes 49160 | tf_op jit(solution)/shard_map/ppermute | solution.py:24
  68.1 3.7 %collective-permute-start.20 = (bf16[256,512]{1,0:T(8,128)(2,1)S(1)}, bf16[256,512]{1,0:T(8,128)(2,1)S(1)}, u32[]{:S(2)}, u32[]{:S(2)}) collective-permute-start(bf16[256,512]{1,0:T(8,128)(2,1)S(1)} %get-tuple-element.116), channel_id=1, source_target_pairs={{0,1},{1,0},{2,3},{3,2},{4,5},{5,4},{6,7},{7,6},{8,9},{9,8},{10,11... | collective-permute-start | bytes 786440 | tf_op jit(solution)/shard_map/ppermute | solution.py:24
  68.2 6.6 %collective-permute-start.19 = (bf16[256,256]{1,0:T(8,128)(2,1)S(1)}, bf16[256,256]{1,0:T(8,128)(2,1)S(1)}, u32[]{:S(2)}, u32[]{:S(2)}) collective-permute-start(bf16[256,256]{1,0:T(8,128)(2,1)S(1)} %get-tuple-element.114), channel_id=1, source_target_pairs={{0,2},{1,3},{2,0},{3,1},{4,6},{5,7},{6,4},{7,5},{8,10},{9,11},{10,... | collective-permute-start | bytes 393224 | tf_op jit(solution)/shard_map/ppermute | solution.py:24
  69.7 7.2 %collective-permute-start.22 = (bf16[256,256]{1,0:T(8,128)(2,1)S(1)}, bf16[256,256]{1,0:T(8,128)(2,1)S(1)}, u32[]{:S(2)}, u32[]{:S(2)}) collective-permute-start(bf16[256,256]{1,0:T(8,128)(2,1)S(1)} %get-tuple-element.122), channel_id=1, source_target_pairs={{0,2},{1,3},{2,0},{3,1},{4,6},{5,7},{6,4},{7,5},{8,10},{9,11},{10,... | collective-permute-start | bytes 393224 | tf_op jit(solution)/shard_map/ppermute | solution.py:24
  71.7 13.1 %collective-permute-start.25 = (bf16[256,512]{1,0:T(8,128)(2,1)S(1)}, bf16[256,512]{1,0:T(8,128)(2,1)S(1)}, u32[]{:S(2)}, u32[]{:S(2)}) collective-permute-start(bf16[256,512]{1,0:T(8,128)(2,1)S(1)} %get-tuple-element.127), channel_id=1, source_target_pairs={{0,1},{1,0},{2,3},{3,2},{4,5},{5,4},{6,7},{7,6},{8,9},{9,8},{10,11... | collective-permute-start | bytes 786440 | tf_op jit(solution)/shard_map/ppermute | solution.py:24
  71.9 12.9 %collective-permute-start.26 = (bf16[256,512]{1,0:T(8,128)(2,1)S(1)}, bf16[256,512]{1,0:T(8,128)(2,1)S(1)}, u32[]{:S(2)}, u32[]{:S(2)}) collective-permute-start(bf16[256,512]{1,0:T(8,128)(2,1)S(1)} %add_convert_fusion), channel_id=1, source_target_pairs={{0,28},{1,29},{2,30},{3,31},{4,0},{5,1},{6,2},{7,3},{8,4},{9,5},{1... | collective-permute-start | bytes 786440 | tf_op jit(solution)/shard_map/ppermute | solution.py:24
  74.8 11.9 %collective-permute-start.21 = (bf16[256,256]{1,0:T(8,128)(2,1)S(1)}, bf16[256,256]{1,0:T(8,128)(2,1)S(1)}, u32[]{:S(2)}, u32[]{:S(2)}) collective-permute-start(bf16[256,256]{1,0:T(8,128)(2,1)S(1)} %add_text.2), channel_id=1, source_target_pairs={{0,8},{1,9},{2,10},{3,11},{4,12},{5,13},{6,14},{7,15},{8,16},{9,17... | collective-permute-start | bytes 393224 | tf_op jit(solution)/shard_map/ppermute | solution.py:24
  76.9 7.9 %collective-permute-start.24 = (bf16[512,256]{1,0:T(8,128)(2,1)S(1)}, bf16[512,256]{1,0:T(8,128)(2,1)S(1)}, u32[]{:S(2)}, u32[]{:S(2)}) collective-permute-start(bf16[512,256]{1,0:T(8,128)(2,1)S(1)} %get-tuple-element.125), channel_id=1, source_target_pairs={{0,2},{1,3},{2,0},{3,1},{4,6},{5,7},{6,4},{7,5},{8,10},{9,11},{10,... | collective-permute-start | bytes 786440 | tf_op jit(solution)/shard_map/ppermute | solution.py:24
  78.4 8.2 %collective-permute-start.23 = (bf16[256,256]{1,0:T(8,128)(2,1)S(1)}, bf16[256,256]{1,0:T(8,128)(2,1)S(1)}, u32[]{:S(2)}, u32[]{:S(2)}) collective-permute-start(bf16[256,256]{1,0:T(8,128)(2,1)S(1)} %add_text.3), channel_id=1, source_target_pairs={{0,8},{1,9},{2,10},{3,11},{4,12},{5,13},{6,14},{7,15},{8,16},{9,17... | collective-permute-start | bytes 393224 | tf_op jit(solution)/shard_map/ppermute | solution.py:24

commit v3 on v2

--- a/solution.py
+++ b/solution.py
@@ -409,8 +409,10 @@
     text_s_ahead, text_s_x = ahead(student_text, -2), to_other_x(student_text)
     image_s_core, image_t_core = to_other_core(student_image), to_other_core(teacher_image)
     image, top, bottom = pack(student_image, teacher_image, 2, "pack_images")
-    top, image_s_core, image_t_core = lax.optimization_barrier((top, image_s_core, image_t_core))
-    top = send_to(top, lambda block, x, core: (block ^ 1, x, core))
+    bottom, image_s_core, image_t_core = lax.optimization_barrier(
+        (bottom, image_s_core, image_t_core)
+    )
+    bottom = send_to(bottom, lambda block, x, core: (block ^ 1, x, core))
     top, bottom, late_s, late_t = lax.optimization_barrier(
         (top, bottom, text_s_ahead, text_t_ahead, text_s_x, text_t_x)
     )[:4]
@@ -452,8 +454,8 @@
         return below, [row, col]
 
     text_both = (ahead(text_part, -2), to_other_x(rest))
-    top = send_to(top, lambda block, x, core: (block + 2 - block % 2 * 2, x, core))
-    bottom = ahead(bottom, 1)
+    top = ahead(top, 1)
+    bottom = send_to(bottom, lambda block, x, core: (block + 2 - block % 2 * 2, x, core))
     texts = (text, text_x, text_ahead, *text_both)
     own = ((image,), (image_core,))
     home, home_stats = part_scores(own, texts[:3], "scores_home")

time: 87.9 us -> 87.8 us (level)
  starting transfers between devices: 32.2 us -> 31.2 us
  waiting for transfers between devices: 38.7 us -> 39.6 us
    ppermute x27, starting transfers between devices: 32.2 us -> 31.2 us  [send_to(): return lax.ppermute(value, AXES, pairs)]
where the time goes in v3:
time: 87.8 us; the launch traced here: 87.6 us
  waiting for transfers between devices  39.6 us (45%)
  starting transfers between devices  31.2 us (36%)
  Pallas kernels  13.9 us (16%)
  local copies, waits for them, and re-layouts  2.04 us (2%)
    ppermute x27, waiting for transfers between devices, send_to(): return lax.ppermute(value, AXES, pairs)  39.6 us
    ppermute x27, starting transfers between devices, send_to(): return lax.ppermute(value, AXES, pairs)  31.2 us
    pallas_call x3, Pallas kernels, part_scores(): pl.pallas_call(lambda *refs: part_kernel(shard, scales, spans, sizes, cou...  5.34 us
    pallas_call x1, Pallas kernels, on_device(): pl.pallas_call(lambda *refs: ahead_kernel(shard, spans[0], *refs), out_sh...  2.67 us
    unnamed x8, local copies, waits for them, and re-layouts  2.04 us
    pallas_call x2, Pallas kernels, finish(): pl.pallas_call(lambda *refs: kernel(scale_s, *refs), out_shape=wide, in_s...  1.89 us
    pallas_call x1, Pallas kernels, on_device(): pl.pallas_call(lambda *refs: far_kernel(shard, scales, spans, *refs), out...  1.86 us
  transfers between devices with their start and end apart: 27, of which 11 were waited for; matrix products, arithmetic and copies ran while one was open for 0% of the time, Pallas kernels for 9%

profile of v3, /device:TPU:0, one launch (start us, length us, event | category | flops | bytes accessed | tf_op | source)
XLA Modules:
  0.0 87.6 jit_solution(2475353791783101288)
XLA Ops:
  0.6 0.5 collective-permute-start.1
  1.2 0.1 collective-permute-start
  1.2 2.9 %collective-permute-start.6 = (bf16[256,1280]{1,0:T(8,128)(2,1)}, bf16[256,1280]{1,0:T(8,128)(2,1)S(1)}, u32[]{:S(2)}, u32[]{:S(2)}) collective-permute-start(bf16[256,1280]{1,0:T(8,128)(2,1)} %second.3), channel_id=1, source_target_pairs={{0,2},{1,3},{2,0},{3,1},{4,6},{5,7},{6,4},{7,5},{8,10},{9,11},{10,... | collective-permute-start | bytes 1966088 | tf_op jit(solution)/shard_map/ppermute | solution.py:24
  4.2 3.6 %collective-permute-start.4 = (bf16[256,1280]{1,0:T(8,128)(2,1)}, bf16[256,1280]{1,0:T(8,128)(2,1)S(1)}, u32[]{:S(2)}, u32[]{:S(2)}) collective-permute-start(bf16[256,1280]{1,0:T(8,128)(2,1)} %second.3), channel_id=1, source_target_pairs={{0,24},{1,25},{2,26},{3,27},{4,28},{5,29},{6,30},{7,31},{8,0},{9,1... | collective-permute-start | bytes 1966088 | tf_op jit(solution)/shard_map/ppermute | solution.py:24
  7.8 1.1 %copy-done.1 = bf16[256,1280]{1,0:T(8,128)(2,1)S(1)} copy-done((bf16[256,1280]{1,0:T(8,128)(2,1)S(1)}, bf16[256,1280]{1,0:T(8,128)(2,1)}, u32[]{:S(2)}) %copy-start.1) | copy-done | bytes 655384
  8.8 0.9 %copy-done.2 = bf16[256,512]{1,0:T(8,128)(2,1)S(1)} copy-done((bf16[256,512]{1,0:T(8,128)(2,1)S(1)}, bf16[256,512]{1,0:T(8,128)(2,1)}, u32[]{:S(2)}) %copy-start.2) | copy-done | bytes 262168
  9.8 0.1 pack_images.1
  9.9 1.6 %collective-permute-start.2 = (bf16[128,1792]{1,0:T(8,128)(2,1)S(1)}, bf16[128,1792]{1,0:T(8,128)(2,1)S(1)}, u32[]{:S(2)}, u32[]{:S(2)}) collective-permute-start(bf16[128,1792]{1,0:T(8,128)(2,1)S(1)} %get-tuple-element.72), channel_id=1, source_target_pairs={{0,4},{1,5},{2,6},{3,7},{4,0},{5,1},{6,2},{7,3},{8,12},{9,13},{10,... | collective-permute-start | bytes 1376264 | tf_op jit(solution)/shard_map/ppermute | solution.py:24
  11.5 0.5 collective-permute-start.5
  12.1 0.4 collective-permute-start.3
  12.5 12.4 %collective-permute-done.5.s_x = bf16[256,512]{1,0:T(8,128)(2,1)S(1)} collective-permute-done((bf16[256,512]{1,0:T(8,128)(2,1)}, bf16[256,512]{1,0:T(8,128)(2,1)S(1)}, u32[]{:S(2)}, u32[]{:S(2)}) %collective-permute-start.5) | collective-permute-done | bytes 262176 | tf_op jit(solution)/shard_map/ppermute | solution.py:24
  25.0 2.7 %collective-permute-done.3.s_ahead = bf16[256,512]{1,0:T(8,128)(2,1)S(1)} collective-permute-done((bf16[256,512]{1,0:T(8,128)(2,1)}, bf16[256,512]{1,0:T(8,128)(2,1)S(1)}, u32[]{:S(2)}, u32[]{:S(2)}) %collective-permute-start.3) | collective-permute-done | bytes 262176 | tf_op jit(solution)/shard_map/ppermute | solution.py:24
  27.7 0.2 pack_arrived.1
  27.8 0.6 collective-permute-start.10
  28.4 1.5 %collective-permute-start.7 = (bf16[128,1792]{1,0:T(8,128)(2,1)S(1)}, bf16[128,1792]{1,0:T(8,128)(2,1)S(1)}, u32[]{:S(2)}, u32[]{:S(2)}) collective-permute-start(bf16[128,1792]{1,0:T(8,128)(2,1)S(1)} %get-tuple-element.81), channel_id=1, source_target_pairs={{0,4},{1,5},{2,6},{3,7},{4,8},{5,9},{6,10},{7,11},{8,12},{9,13},{1... | collective-permute-start | bytes 1376264 | tf_op jit(solution)/shard_map/ppermute | solution.py:24
  30.0 2.2 %collective-permute-start.8 = (bf16[128,1792]{1,0:T(8,128)(2,1)S(1)}, bf16[128,1792]{1,0:T(8,128)(2,1)S(1)}, u32[]{:S(2)}, u32[]{:S(2)}) collective-permute-start(bf16[128,1792]{1,0:T(8,128)(2,1)S(1)} %collective-permute-done.2), channel_id=1, source_target_pairs={{0,8},{1,9},{2,10},{3,11},{4,4},{5,5},{6,6},{7,7},{8,16},{9,17},{1... | collective-permute-start | bytes 1376264 | tf_op jit(solution)/shard_map/ppermute | solution.py:24
  32.2 3.9 %collective-permute-start.9 = (bf16[32,1792]{1,0:T(8,128)(2,1)S(1)}, bf16[32,1792]{1,0:T(8,128)(2,1)S(1)}, u32[]{:S(2)}, u32[]{:S(2)}) collective-permute-start(bf16[32,1792]{1,0:T(8,128)(2,1)S(1)} %get-tuple-element.90), channel_id=1, source_target_pairs={{0,24},{1,25},{2,26},{3,27},{4,28},{5,29},{6,30},{7,31},{8,0},{9,1... | collective-permute-start | bytes 344072 | tf_op jit(solution)/shard_map/ppermute | solution.py:24
  36.2 2.5 %scores_home.1 = (f32[512,768]{1,0:T(8,128)S(1)}, f32[512,768]{1,0:T(8,128)S(1)}, f32[512,768]{1,0:T(8,128)S(1)}, f32[512,768]{1,0:T(8,128)S(1)}, f32[8,512]{1,0:T(8,128)S(1)}, /*index=5*/f32[8,768]{1,0:T(8,128)S(1)}) custom-call(bf16[256,1792]{1,0:T(8,128)(2,1)S(1)} %get-tuple-element.67.refs_0_.refs_25_.refs_7_, ...), custom_call_target="tpu_custom_call" | custom-call | tf_op jit(solution)/shard_map/scores_home/pallas_call | solution.py:445
  38.7 5.5 %collective-permute-done.7.refs_0_.refs_2_.refs_27_ = bf16[128,1792]{1,0:T(8,128)(2,1)S(1)} collective-permute-done((bf16[128,1792]{1,0:T(8,128)(2,1)S(1)}, bf16[128,1792]{1,0:T(8,128)(2,1)S(1)}, u32[]{:S(2)}, u32[]{:S(2)}) %collective-permute-start.7) | collective-permute-done | bytes 458784 | tf_op jit(solution)/shard_map/ppermute | solution.py:24
  44.2 2.2 %collective-permute-done.8.refs_1_.refs_3_.refs_28_ = bf16[128,1792]{1,0:T(8,128)(2,1)S(1)} collective-permute-done((bf16[128,1792]{1,0:T(8,128)(2,1)S(1)}, bf16[128,1792]{1,0:T(8,128)(2,1)S(1)}, u32[]{:S(2)}, u32[]{:S(2)}) %collective-permute-start.8) | collective-permute-done | bytes 458784 | tf_op jit(solution)/shard_map/ppermute | solution.py:24
  46.4 0.5 collective-permute-start.12
  46.9 1.5 %scores_near.1 = (f32[256,768]{1,0:T(8,128)S(1)}, f32[256,768]{1,0:T(8,128)S(1)}, f32[256,768]{1,0:T(8,128)S(1)}, f32[256,768]{1,0:T(8,128)S(1)}, f32[8,256]{1,0:T(8,128)S(1)}, /*index=5*/f32[4,768]{1,0:T(4,128)S(1)}) custom-call(bf16[128,1792]{1,0:T(8,128)(2,1)S(1)} %collective-permute-done.7.refs_0_.refs_2_.refs_27_, ...), custom_call_target="tpu_custom_call" | custom-call | tf_op jit(solution)/shard_map/scores_near/pallas_call | solution.py:445
  48.4 1.4 %scores_side.1 = (f32[768,256]{1,0:T(8,128)S(1)}, f32[768,256]{1,0:T(8,128)S(1)}, f32[768,256]{1,0:T(8,128)S(1)}, f32[768,256]{1,0:T(8,128)S(1)}, f32[8,768]{1,0:T(8,128)S(1)}, /*index=5*/f32[12,256]{1,0:T(8,128)S(1)}) custom-call(bf16[256,1792]{1,0:T(8,128)(2,1)S(1)} %get-tuple-element.67.refs_0_.refs_25_.refs_7_, ...), custom_call_target="tpu_custom_call" | custom-call | flops 99999997952 | bytes 1000000000 | tf_op jit(solution)/shard_map/scores_side/pallas_call | solution.py:445
  49.8 1.9 %scores_far.1 = (f32[256,1024]{1,0:T(8,128)S(1)}, f32[256,1024]{1,0:T(8,128)S(1)}, f32[256,1024]{1,0:T(8,128)S(1)}, f32[256,1024]{1,0:T(8,128)S(1)}, f32[8,256]{...) custom-call(bf16[128,1792]{1,0:T(8,128)(2,1)S(1)} %collective-permute-done.11.refs_0_.refs_29_, ...), custom_call_target="tpu_custom_call" | custom-call | tf_op jit(solution)/shard_map/scores_far/pallas_call | solution.py:467
  51.7 1.5 %collective-permute-start.14 = (f32[8,1024]{1,0:T(8,128)S(1)}, f32[8,1024]{1,0:T(8,128)S(1)}, u32[]{:S(2)}, u32[]{:S(2)}) collective-permute-start(f32[8,1024]{1,0:T(8,128)S(1)} %get-tuple-element.107.refs_0_), channel_id=1, source_target_pairs={{0,2},{1,3},{2,0},{3,1},{4,6},{5,7},{6,4},{7,5},{8,10},{9,11},{10,... | collective-permute-start | bytes 98312 | tf_op jit(solution)/shard_map/ppermute | solution.py:24
  53.2 2.4 %collective-permute-done.14.refs_2_ = f32[8,1024]{1,0:T(8,128)S(1)} collective-permute-done((f32[8,1024]{1,0:T(8,128)S(1)}, f32[8,1024]{1,0:T(8,128)S(1)}, u32[]{:S(2)}, u32[]{:S(2)}) %collective-permute-start.14) | collective-permute-done | bytes 32800 | tf_op jit(solution)/shard_map/ppermute | solution.py:24
  55.7 0.1 collective-permute-start.15
  55.7 4.3 %collective-permute-start.16 = (f32[8,512]{1,0:T(8,128)S(1)}, f32[8,512]{1,0:T(8,128)S(1)}, u32[]{:S(2)}, u32[]{:S(2)}) collective-permute-start(f32[8,512]{1,0:T(8,128)S(1)} %get-tuple-element.110), channel_id=1, source_target_pairs={{0,28},{1,29},{2,30},{3,31},{4,8},{5,9},{6,10},{7,11},{8,4},{9,5},... | collective-permute-start | bytes 49160 | tf_op jit(solution)/shard_map/ppermute | solution.py:24
  60.1 2.2 %collective-permute-done.16.refs_2_ = f32[8,512]{1,0:T(8,128)S(1)} collective-permute-done((f32[8,512]{1,0:T(8,128)S(1)}, f32[8,512]{1,0:T(8,128)S(1)}, u32[]{:S(2)}, u32[]{:S(2)}) %collective-permute-start.16) | collective-permute-done | bytes 16416 | tf_op jit(solution)/shard_map/ppermute | solution.py:24
  62.2 1.6 %collective-permute-done.17.refs_3_ = f32[8,512]{1,0:T(8,128)S(1)} collective-permute-done((f32[8,512]{1,0:T(8,128)S(1)}, f32[8,512]{1,0:T(8,128)S(1)}, u32[]{:S(2)}, u32[]{:S(2)}) %collective-permute-start.17) | collective-permute-done | bytes 16416 | tf_op jit(solution)/shard_map/ppermute | solution.py:24
  63.8 1.8 %collective-permute-done.18.refs_4_ = f32[8,512]{1,0:T(8,128)S(1)} collective-permute-done((f32[8,512]{1,0:T(8,128)S(1)}, f32[8,512]{1,0:T(8,128)S(1)}, u32[]{:S(2)}, u32[]{:S(2)}) %collective-permute-start.18) | collective-permute-done | bytes 16416 | tf_op jit(solution)/shard_map/ppermute | solution.py:24
  65.7 2.7 %gradients_ahead.1 = (f32[256,256]{1,0:T(8,128)S(1)}, f32[256,256]{1,0:T(8,128)S(1)}, bf16[256,256]{1,0:T(8,128)(2,1)S(1)}, bf16[256,256]{1,0:T(8,128)(2,1)S(1)}...) custom-call(f32[512,768]{1,0:T(8,128)S(1)} %get-tuple-element.77.ref, ...), custom_call_target="tpu_custom_call" | custom-call | tf_op jit(solution)/shard_map/gradients_ahead/pallas_call | solution.py:509
  68.3 0.1 collective-permute-start.20
  68.4 1.6 %collective-permute-start.19 = (bf16[256,256]{1,0:T(8,128)(2,1)S(1)}, bf16[256,256]{1,0:T(8,128)(2,1)S(1)}, u32[]{:S(2)}, u32[]{:S(2)}) collective-permute-start(bf16[256,256]{1,0:T(8,128)(2,1)S(1)} %get-tuple-element.114), channel_id=1, source_target_pairs={{0,2},{1,3},{2,0},{3,1},{4,6},{5,7},{6,4},{7,5},{8,10},{9,11},{10,... | collective-permute-start | bytes 393224 | tf_op jit(solution)/shard_map/ppermute | solution.py:24
  70.0 0.5 collective-permute-start.22
  70.5 1.5 %gradients_home.1 = (f32[256,512]{1,0:T(8,128)S(1)}, bf16[256,512]{1,0:T(8,128)(2,1)S(1)}, f32[512,256]{1,0:T(8,128)S(1)}, bf16[512,256]{1,0:T(8,128)(2,1)S(1)}) custom-call(f32[512,768]{1,0:T(8,128)S(1)} %get-tuple-element.77.refs_0_, f32[512,768]{1,0:T(8,128)S(1)} %get-tuple-element.78.refs_1_, f32[512,768]{1,0:T(8,128)S(1)} %get-tuple-element.79.refs_2_, ...), custom_call_target="tpu_custom_call" | custom-call | tf_op jit(solution)/shard_map/gradients_home/pallas_call | solution.py:529
  72.0 0.1 collective-permute-start.25
  72.0 0.1 add_convert_fusion
  72.1 2.6 %collective-permute-start.26 = (bf16[256,512]{1,0:T(8,128)(2,1)S(1)}, bf16[256,512]{1,0:T(8,128)(2,1)S(1)}, u32[]{:S(2)}, u32[]{:S(2)}) collective-permute-start(bf16[256,512]{1,0:T(8,128)(2,1)S(1)} %add_convert_fusion), channel_id=1, source_target_pairs={{0,28},{1,29},{2,30},{3,31},{4,0},{5,1},{6,2},{7,3},{8,4},{9,5},{1... | collective-permute-start | bytes 786440 | tf_op jit(solution)/shard_map/ppermute | solution.py:24
  74.8 0.3 collective-permute-start.21
  75.1 2.0 %collective-permute-done.22.second = bf16[256,256]{1,0:T(8,128)(2,1)S(1)} collective-permute-done((bf16[256,256]{1,0:T(8,128)(2,1)S(1)}, bf16[256,256]{1,0:T(8,128)(2,1)S(1)}, u32[]{:S(2)}, u32[]{:S(2)}) %collective-permute-start.22) | collective-permute-done | bytes 131104 | tf_op jit(solution)/shard_map/ppermute | solution.py:24
  77.1 1.5 %collective-permute-start.24 = (bf16[512,256]{1,0:T(8,128)(2,1)S(1)}, bf16[512,256]{1,0:T(8,128)(2,1)S(1)}, u32[]{:S(2)}, u32[]{:S(2)}) collective-permute-start(bf16[512,256]{1,0:T(8,128)(2,1)S(1)} %get-tuple-element.125), channel_id=1, source_target_pairs={{0,2},{1,3},{2,0},{3,1},{4,6},{5,7},{6,4},{7,5},{8,10},{9,11},{10,... | collective-permute-start | bytes 786440 | tf_op jit(solution)/shard_map/ppermute | solution.py:24
  78.7 0.3 collective-permute-start.23
  78.9 6.1 %collective-permute-done.24.second = bf16[512,256]{1,0:T(8,128)(2,1)S(1)} collective-permute-done((bf16[512,256]{1,0:T(8,128)(2,1)S(1)}, bf16[512,256]{1,0:T(8,128)(2,1)S(1)}, u32[]{:S(2)}, u32[]{:S(2)}) %collective-permute-start.24) | collective-permute-done | bytes 262176 | tf_op jit(solution)/shard_map/ppermute | solution.py:24
  85.0 0.1 add_own_text.1.refs_0_
  85.1 0.9 %finish_image.1 = f32[256,512]{1,0:T(8,128)} custom-call(f32[256,512]{1,0:T(8,128)S(1)} %get-tuple-element.126.refs_0_, bf16[256,512]{1,0:T(8,128)(2,1)S(1)} %collective-permute-done.25.refs_1_, bf16[256,512]{1,0:T(8,128)(2,1)S(1)} %collective-permute-done.26.refs_2_), custom_call_target="tpu_custom_call" | custom-call | tf_op jit(solution)/shard_map/finish_image/pallas_call | solution.py:564
  86.0 0.6 collective-permute-done.23.refs_2_
  86.6 1.0 %finish_text.1 = f32[256,512]{1,0:T(8,128)} custom-call(f32[512,256]{1,0:T(8,128)S(1)} %add_own_text.1.refs_0_, bf16[256,256]{1,0:T(8,128)(2,1)S(1)} %collective-permute-done.21.refs_1_, bf16[256,256]{1,0:T(8,128)(2,1)S(1)} %collective-permute-done.23.refs_2_), custom_call_target="tpu_custom_call" | custom-call | tf_op jit(solution)/shard_map/finish_text/pallas_call | solution.py:564
  (32 shorter events, 0.4 us)
Async XLA Ops:
  0.6 35.5 %copy-start = (bf16[256,1280]{1,0:T(8,128)(2,1)S(1)}, bf16[256,1280]{1,0:T(8,128)(2,1)}, u32[]{:S(2)}) copy-start(bf16[256,1280]{1,0:T(8,128)(2,1)} %second.3) | copy-start | bytes 1966084
  0.6 9.3 %collective-permute-start.1 = (bf16[256,1280]{1,0:T(8,128)(2,1)}, bf16[256,1280]{1,0:T(8,128)(2,1)S(1)}, u32[]{:S(2)}, u32[]{:S(2)}) collective-permute-start(bf16[256,1280]{1,0:T(8,128)(2,1)} %second.2), channel_id=1, source_target_pairs={{0,1},{1,0},{2,3},{3,2},{4,5},{5,4},{6,7},{7,6},{8,9},{9,8},{10,11... | collective-permute-start | bytes 1966088 | tf_op jit(solution)/shard_map/ppermute | solution.py:24
  1.2 8.8 %collective-permute-start = (bf16[256,512]{1,0:T(8,128)(2,1)}, bf16[256,512]{1,0:T(8,128)(2,1)S(1)}, u32[]{:S(2)}, u32[]{:S(2)}) collective-permute-start(bf16[256,512]{1,0:T(8,128)(2,1)} %first.2), channel_id=1, source_target_pairs={{0,1},{1,0},{2,3},{3,2},{4,5},{5,4},{6,7},{7,6},{8,9},{9,8},{10,11... | collective-permute-start | bytes 786440 | tf_op jit(solution)/shard_map/ppermute | solution.py:24
  1.2 26.4 %collective-permute-start.6 = (bf16[256,1280]{1,0:T(8,128)(2,1)}, bf16[256,1280]{1,0:T(8,128)(2,1)S(1)}, u32[]{:S(2)}, u32[]{:S(2)}) collective-permute-start(bf16[256,1280]{1,0:T(8,128)(2,1)} %second.3), channel_id=1, source_target_pairs={{0,2},{1,3},{2,0},{3,1},{4,6},{5,7},{6,4},{7,5},{8,10},{9,11},{10,... | collective-permute-start | bytes 1966088 | tf_op jit(solution)/shard_map/ppermute | solution.py:24
  4.2 23.5 %collective-permute-start.4 = (bf16[256,1280]{1,0:T(8,128)(2,1)}, bf16[256,1280]{1,0:T(8,128)(2,1)S(1)}, u32[]{:S(2)}, u32[]{:S(2)}) collective-permute-start(bf16[256,1280]{1,0:T(8,128)(2,1)} %second.3), channel_id=1, source_target_pairs={{0,24},{1,25},{2,26},{3,27},{4,28},{5,29},{6,30},{7,31},{8,0},{9,1... | collective-permute-start | bytes 1966088 | tf_op jit(solution)/shard_map/ppermute | solution.py:24
  7.8 1.1 %copy-start.1 = (bf16[256,1280]{1,0:T(8,128)(2,1)S(1)}, bf16[256,1280]{1,0:T(8,128)(2,1)}, u32[]{:S(2)}) copy-start(bf16[256,1280]{1,0:T(8,128)(2,1)} %second.2) | copy-start | bytes 1966084
  8.8 0.9 %copy-start.2 = (bf16[256,512]{1,0:T(8,128)(2,1)S(1)}, bf16[256,512]{1,0:T(8,128)(2,1)}, u32[]{:S(2)}) copy-start(bf16[256,512]{1,0:T(8,128)(2,1)} %first.2) | copy-start | bytes 786436
  9.8 26.3 %copy-start.3 = (bf16[256,512]{1,0:T(8,128)(2,1)S(1)}, bf16[256,512]{1,0:T(8,128)(2,1)}, u32[]{:S(2)}) copy-start(bf16[256,512]{1,0:T(8,128)(2,1)} %first.3) | copy-start | bytes 786436
  9.9 17.7 %collective-permute-start.2 = (bf16[128,1792]{1,0:T(8,128)(2,1)S(1)}, bf16[128,1792]{1,0:T(8,128)(2,1)S(1)}, u32[]{:S(2)}, u32[]{:S(2)}) collective-permute-start(bf16[128,1792]{1,0:T(8,128)(2,1)S(1)} %get-tuple-element.72), channel_id=1, source_target_pairs={{0,4},{1,5},{2,6},{3,7},{4,0},{5,1},{6,2},{7,3},{8,12},{9,13},{10,... | collective-permute-start | bytes 1376264 | tf_op jit(solution)/shard_map/ppermute | solution.py:24
  11.5 13.4 %collective-permute-start.5 = (bf16[256,512]{1,0:T(8,128)(2,1)}, bf16[256,512]{1,0:T(8,128)(2,1)S(1)}, u32[]{:S(2)}, u32[]{:S(2)}) collective-permute-start(bf16[256,512]{1,0:T(8,128)(2,1)} %first.3), channel_id=1, source_target_pairs={{0,2},{1,3},{2,0},{3,1},{4,6},{5,7},{6,4},{7,5},{8,10},{9,11},{10,... | collective-permute-start | bytes 786440 | tf_op jit(solution)/shard_map/ppermute | solution.py:24
  12.1 15.6 %collective-permute-start.3 = (bf16[256,512]{1,0:T(8,128)(2,1)}, bf16[256,512]{1,0:T(8,128)(2,1)S(1)}, u32[]{:S(2)}, u32[]{:S(2)}) collective-permute-start(bf16[256,512]{1,0:T(8,128)(2,1)} %first.3), channel_id=1, source_target_pairs={{0,24},{1,25},{2,26},{3,27},{4,28},{5,29},{6,30},{7,31},{8,0},{9,1... | collective-permute-start | bytes 786440 | tf_op jit(solution)/shard_map/ppermute | solution.py:24
  27.8 20.5 %collective-permute-start.10 = (bf16[224,1792]{1,0:T(8,128)(2,1)S(1)}, bf16[224,1792]{1,0:T(8,128)(2,1)S(1)}, u32[]{:S(2)}, u32[]{:S(2)}) collective-permute-start(bf16[224,1792]{1,0:T(8,128)(2,1)S(1)} %get-tuple-element.91), channel_id=1, source_target_pairs={{0,2},{1,3},{2,0},{3,1},{4,6},{5,7},{6,4},{7,5},{8,10},{9,11},{10,... | collective-permute-start | bytes 2408456 | tf_op jit(solution)/shard_map/ppermute | solution.py:24
  28.4 15.8 %collective-permute-start.7 = (bf16[128,1792]{1,0:T(8,128)(2,1)S(1)}, bf16[128,1792]{1,0:T(8,128)(2,1)S(1)}, u32[]{:S(2)}, u32[]{:S(2)}) collective-permute-start(bf16[128,1792]{1,0:T(8,128)(2,1)S(1)} %get-tuple-element.81), channel_id=1, source_target_pairs={{0,4},{1,5},{2,6},{3,7},{4,8},{5,9},{6,10},{7,11},{8,12},{9,13},{1... | collective-permute-start | bytes 1376264 | tf_op jit(solution)/shard_map/ppermute | solution.py:24
  30.0 16.4 %collective-permute-start.8 = (bf16[128,1792]{1,0:T(8,128)(2,1)S(1)}, bf16[128,1792]{1,0:T(8,128)(2,1)S(1)}, u32[]{:S(2)}, u32[]{:S(2)}) collective-permute-start(bf16[128,1792]{1,0:T(8,128)(2,1)S(1)} %collective-permute-done.2), channel_id=1, source_target_pairs={{0,8},{1,9},{2,10},{3,11},{4,4},{5,5},{6,6},{7,7},{8,16},{9,17},{1... | collective-permute-start | bytes 1376264 | tf_op jit(solution)/shard_map/ppermute | solution.py:24
  32.2 16.2 %collective-permute-start.9 = (bf16[32,1792]{1,0:T(8,128)(2,1)S(1)}, bf16[32,1792]{1,0:T(8,128)(2,1)S(1)}, u32[]{:S(2)}, u32[]{:S(2)}) collective-permute-start(bf16[32,1792]{1,0:T(8,128)(2,1)S(1)} %get-tuple-element.90), channel_id=1, source_target_pairs={{0,24},{1,25},{2,26},{3,27},{4,28},{5,29},{6,30},{7,31},{8,0},{9,1... | collective-permute-start | bytes 344072 | tf_op jit(solution)/shard_map/ppermute | solution.py:24
  46.4 3.4 %collective-permute-start.11 = (bf16[128,1792]{1,0:T(8,128)(2,1)S(1)}, bf16[128,1792]{1,0:T(8,128)(2,1)S(1)}, u32[]{:S(2)}, u32[]{:S(2)}) collective-permute-start(bf16[128,1792]{1,0:T(8,128)(2,1)S(1)} %collective-permute-done.7.refs_0_.refs_2_.refs_27_), channel_id=1, source_target_pairs={{0,1},{1,0},{2,3},{3,2},{4,5},{5,4},{6,7},{7,6},{8,9},{9,8},{10,11... | collective-permute-start | bytes 1376264 | tf_op jit(solution)/shard_map/ppermute | solution.py:24
  46.4 3.4 %collective-permute-start.12 = (bf16[128,1792]{1,0:T(8,128)(2,1)S(1)}, bf16[128,1792]{1,0:T(8,128)(2,1)S(1)}, u32[]{:S(2)}, u32[]{:S(2)}) collective-permute-start(bf16[128,1792]{1,0:T(8,128)(2,1)S(1)} %collective-permute-done.8.refs_1_.refs_3_.refs_28_), channel_id=1, source_target_pairs={{0,1},{1,0},{2,3},{3,2},{4,5},{5,4},{6,7},{7,6},{8,9},{9,8},{10,11... | collective-permute-start | bytes 1376264 | tf_op jit(solution)/shard_map/ppermute | solution.py:24
  51.7 3.9 %collective-permute-start.14 = (f32[8,1024]{1,0:T(8,128)S(1)}, f32[8,1024]{1,0:T(8,128)S(1)}, u32[]{:S(2)}, u32[]{:S(2)}) collective-permute-start(f32[8,1024]{1,0:T(8,128)S(1)} %get-tuple-element.107.refs_0_), channel_id=1, source_target_pairs={{0,2},{1,3},{2,0},{3,1},{4,6},{5,7},{6,4},{7,5},{8,10},{9,11},{10,... | collective-permute-start | bytes 98312 | tf_op jit(solution)/shard_map/ppermute | solution.py:24
  53.2 2.4 %collective-permute-start.13 = (f32[8,1024]{1,0:T(8,128)S(1)}, f32[8,1024]{1,0:T(8,128)S(1)}, u32[]{:S(2)}, u32[]{:S(2)}) collective-permute-start(f32[8,1024]{1,0:T(8,128)S(1)} %get-tuple-element.107.refs_0_), channel_id=1, source_target_pairs={{0,1},{1,0},{2,3},{3,2},{4,5},{5,4},{6,7},{7,6},{8,9},{9,8},{10,11... | collective-permute-start | bytes 98312 | tf_op jit(solution)/shard_map/ppermute | solution.py:24
  55.7 4.4 %collective-permute-start.15 = (f32[8,512]{1,0:T(8,128)S(1)}, f32[8,512]{1,0:T(8,128)S(1)}, u32[]{:S(2)}, u32[]{:S(2)}) collective-permute-start(f32[8,512]{1,0:T(8,128)S(1)} %get-tuple-element.109), channel_id=1, source_target_pairs={{0,4},{1,5},{2,6},{3,7},{4,0},{5,1},{6,2},{7,3},{8,12},{9,13},{10,... | collective-permute-start | bytes 49160 | tf_op jit(solution)/shard_map/ppermute | solution.py:24
  55.7 6.5 %collective-permute-start.16 = (f32[8,512]{1,0:T(8,128)S(1)}, f32[8,512]{1,0:T(8,128)S(1)}, u32[]{:S(2)}, u32[]{:S(2)}) collective-permute-start(f32[8,512]{1,0:T(8,128)S(1)} %get-tuple-element.110), channel_id=1, source_target_pairs={{0,28},{1,29},{2,30},{3,31},{4,8},{5,9},{6,10},{7,11},{8,4},{9,5},... | collective-permute-start | bytes 49160 | tf_op jit(solution)/shard_map/ppermute | solution.py:24
  60.1 3.7 %collective-permute-start.17 = (f32[8,512]{1,0:T(8,128)S(1)}, f32[8,512]{1,0:T(8,128)S(1)}, u32[]{:S(2)}, u32[]{:S(2)}) collective-permute-start(f32[8,512]{1,0:T(8,128)S(1)} %get-tuple-element.111), channel_id=1, source_target_pairs={{0,8},{1,9},{2,10},{3,11},{4,12},{5,13},{6,14},{7,15},{8,0},{9,1},... | collective-permute-start | bytes 49160 | tf_op jit(solution)/shard_map/ppermute | solution.py:24
  60.1 5.5 %collective-permute-start.18 = (f32[8,512]{1,0:T(8,128)S(1)}, f32[8,512]{1,0:T(8,128)S(1)}, u32[]{:S(2)}, u32[]{:S(2)}) collective-permute-start(f32[8,512]{1,0:T(8,128)S(1)} %get-tuple-element.112), channel_id=1, source_target_pairs={{0,24},{1,25},{2,26},{3,27},{4,28},{5,29},{6,30},{7,31},{8,16},{9,... | collective-permute-start | bytes 49160 | tf_op jit(solution)/shard_map/ppermute | solution.py:24
  68.3 3.7 %collective-permute-start.20 = (bf16[256,512]{1,0:T(8,128)(2,1)S(1)}, bf16[256,512]{1,0:T(8,128)(2,1)S(1)}, u32[]{:S(2)}, u32[]{:S(2)}) collective-permute-start(bf16[256,512]{1,0:T(8,128)(2,1)S(1)} %get-tuple-element.116), channel_id=1, source_target_pairs={{0,1},{1,0},{2,3},{3,2},{4,5},{5,4},{6,7},{7,6},{8,9},{9,8},{10,11... | collective-permute-start | bytes 786440 | tf_op jit(solution)/shard_map/ppermute | solution.py:24
  68.4 6.4 %collective-permute-start.19 = (bf16[256,256]{1,0:T(8,128)(2,1)S(1)}, bf16[256,256]{1,0:T(8,128)(2,1)S(1)}, u32[]{:S(2)}, u32[]{:S(2)}) collective-permute-start(bf16[256,256]{1,0:T(8,128)(2,1)S(1)} %get-tuple-element.114), channel_id=1, source_target_pairs={{0,2},{1,3},{2,0},{3,1},{4,6},{5,7},{6,4},{7,5},{8,10},{9,11},{10,... | collective-permute-start | bytes 393224 | tf_op jit(solution)/shard_map/ppermute | solution.py:24
  70.0 7.2 %collective-permute-start.22 = (bf16[256,256]{1,0:T(8,128)(2,1)S(1)}, bf16[256,256]{1,0:T(8,128)(2,1)S(1)}, u32[]{:S(2)}, u32[]{:S(2)}) collective-permute-start(bf16[256,256]{1,0:T(8,128)(2,1)S(1)} %get-tuple-element.122), channel_id=1, source_target_pairs={{0,2},{1,3},{2,0},{3,1},{4,6},{5,7},{6,4},{7,5},{8,10},{9,11},{10,... | collective-permute-start | bytes 393224 | tf_op jit(solution)/shard_map/ppermute | solution.py:24
  72.0 13.1 %collective-permute-start.25 = (bf16[256,512]{1,0:T(8,128)(2,1)S(1)}, bf16[256,512]{1,0:T(8,128)(2,1)S(1)}, u32[]{:S(2)}, u32[]{:S(2)}) collective-permute-start(bf16[256,512]{1,0:T(8,128)(2,1)S(1)} %get-tuple-element.127), channel_id=1, source_target_pairs={{0,1},{1,0},{2,3},{3,2},{4,5},{5,4},{6,7},{7,6},{8,9},{9,8},{10,11... | collective-permute-start | bytes 786440 | tf_op jit(solution)/shard_map/ppermute | solution.py:24
  72.1 12.9 %collective-permute-start.26 = (bf16[256,512]{1,0:T(8,128)(2,1)S(1)}, bf16[256,512]{1,0:T(8,128)(2,1)S(1)}, u32[]{:S(2)}, u32[]{:S(2)}) collective-permute-start(bf16[256,512]{1,0:T(8,128)(2,1)S(1)} %add_convert_fusion), channel_id=1, source_target_pairs={{0,28},{1,29},{2,30},{3,31},{4,0},{5,1},{6,2},{7,3},{8,4},{9,5},{1... | collective-permute-start | bytes 786440 | tf_op jit(solution)/shard_map/ppermute | solution.py:24
  74.8 11.8 %collective-permute-start.21 = (bf16[256,256]{1,0:T(8,128)(2,1)S(1)}, bf16[256,256]{1,0:T(8,128)(2,1)S(1)}, u32[]{:S(2)}, u32[]{:S(2)}) collective-permute-start(bf16[256,256]{1,0:T(8,128)(2,1)S(1)} %add_text.2), channel_id=1, source_target_pairs={{0,8},{1,9},{2,10},{3,11},{4,12},{5,13},{6,14},{7,15},{8,16},{9,17... | collective-permute-start | bytes 393224 | tf_op jit(solution)/shard_map/ppermute | solution.py:24
  77.1 7.9 %collective-permute-start.24 = (bf16[512,256]{1,0:T(8,128)(2,1)S(1)}, bf16[512,256]{1,0:T(8,128)(2,1)S(1)}, u32[]{:S(2)}, u32[]{:S(2)}) collective-permute-start(bf16[512,256]{1,0:T(8,128)(2,1)S(1)} %get-tuple-element.125), channel_id=1, source_target_pairs={{0,2},{1,3},{2,0},{3,1},{4,6},{5,7},{6,4},{7,5},{8,10},{9,11},{10,... | collective-permute-start | bytes 786440 | tf_op jit(solution)/shard_map/ppermute | solution.py:24
  78.7 8.0 %collective-permute-start.23 = (bf16[256,256]{1,0:T(8,128)(2,1)S(1)}, bf16[256,256]{1,0:T(8,128)(2,1)S(1)}, u32[]{:S(2)}, u32[]{:S(2)}) collective-permute-start(bf16[256,256]{1,0:T(8,128)(2,1)S(1)} %add_text.3), channel_id=1, source_target_pairs={{0,8},{1,9},{2,10},{3,11},{4,12},{5,13},{6,14},{7,15},{8,16},{9,17... | collective-permute-start | bytes 393224 | tf_op jit(solution)/shard_map/ppermute | solution.py:24

commit v4 on v3

--- a/solution.py
+++ b/solution.py
@@ -43,15 +43,16 @@
     return rows
 
 
-def pack_kernel(first, second, whole, *halves):
+def pack_kernel(first, second, whole, *parts):
     width = first.shape[1]
-    half = first.shape[0] // 2
     whole[:, :width] = first[...]
     whole[:, width:] = second[...]
-    for index, out in enumerate(halves):
-        here = pl.ds(index * half, half)
+    start = 0
+    for out in parts:
+        here = pl.ds(start, out.shape[0])
         out[:, :width] = first[here]
         out[:, width:] = second[here]
+        start += out.shape[0]
 
 
 def pack_arrived_kernel(s_ahead, t_ahead, s_x, t_x, ahead_out, rest_out, x_out, part_out):
@@ -392,8 +393,8 @@
     spans = (slice(0, width_s), slice(width_s, width_s + width_t))
     scales = (scale_s, scale_t)
 
-    def pack(first, second, halves, name):
-        heights = (shard,) + (shard // 2,) * halves
+    def pack(first, second, *heights, name):
+        heights = (shard, *heights)
         return pl.pallas_call(
             pack_kernel,
             out_shape=tuple(
@@ -406,13 +407,15 @@
         )(first, second)
 
     text_t_ahead, text_t_x = ahead(teacher_text, -2), to_other_x(teacher_text)
-    text_s_ahead, text_s_x = ahead(student_text, -2), to_other_x(student_text)
     image_s_core, image_t_core = to_other_core(student_image), to_other_core(teacher_image)
-    image, top, bottom = pack(student_image, teacher_image, 2, "pack_images")
-    bottom, image_s_core, image_t_core = lax.optimization_barrier(
-        (bottom, image_s_core, image_t_core)
+    image, top, bottom = pack(
+        student_image, teacher_image, shard * 9 // 16, shard * 7 // 16, name="pack_images"
     )
     bottom = send_to(bottom, lambda block, x, core: (block ^ 1, x, core))
+    late_s, image_s_core, image_t_core = lax.optimization_barrier(
+        (student_text, image_s_core, image_t_core)
+    )
+    text_s_ahead, text_s_x = ahead(late_s, -2), to_other_x(late_s)
     top, bottom, late_s, late_t = lax.optimization_barrier(
         (top, bottom, text_s_ahead, text_t_ahead, text_s_x, text_t_x)
     )[:4]
@@ -428,8 +431,8 @@
         compiler_params=params(8),
         name="pack_arrived",
     )(late_s, late_t, text_s_x, text_t_x)
-    (text,) = pack(student_text, teacher_text, 0, "pack_own")
-    (image_core,) = pack(image_s_core, image_t_core, 0, "pack_core")
+    (text,) = pack(student_text, teacher_text, name="pack_own")
+    (image_core,) = pack(image_s_core, image_t_core, name="pack_core")
 
     def stat(shards):
         return jax.ShapeDtypeStruct((8, shards * shard), f32)
@@ -526,6 +529,10 @@
         *home, *near, *side, *far, *calls_stats, stats,
         *images, *texts,
     )
+    img_cross = to_other_core(img_cross)
+    img_sum = (img_back + img_cross.astype(f32)).astype(bf16)
+    img_home = ahead(img_sum, -1)
+    weights = lax.optimization_barrier((weights, img_sum))[0]
     img_own, img_core, txt_own, txt_x = pl.pallas_call(
         lambda *refs: home_kernel(shard, spans[0], *refs),
         out_shape=(wide, flat, tall, sent),
@@ -535,9 +542,6 @@
         name="gradients_home",
     )(*home, *home_stats, stats, *images[:2], *texts, weights, txt_both)
 
-    img_cross = to_other_core(img_cross)
-    img_sum = (img_back + img_cross.astype(f32)).astype(bf16)
-    img_home = ahead(img_sum, -1)
     txt_same, txt_cross = txt_ahead[:2], [to_other_x(part) for part in txt_ahead[2:]]
     img_core = to_other_core(img_core)
 

time: 87.8 us -> 87.1 us (level)
  transfers between devices with their start and end apart: 27 -> 27, of which waited for: 11 -> 13; matrix products, arithmetic and copies ran while one was open for 0% -> 0% of each run, Pallas kernels for 9% -> 9%
where the time goes in v4:
time: 87.1 us; the launch traced here: 86.9 us
  waiting for transfers between devices  39 us (45%)
  starting transfers between devices  31.2 us (36%)
  Pallas kernels  13.9 us (16%)
  local copies, waits for them, and re-layouts  2.04 us (2%)
    ppermute x27, waiting for transfers between devices, send_to(): return lax.ppermute(value, AXES, pairs)  39 us
    ppermute x27, starting transfers between devices, send_to(): return lax.ppermute(value, AXES, pairs)  31.2 us
    pallas_call x3, Pallas kernels, part_scores(): pl.pallas_call(lambda *refs: part_kernel(shard, scales, spans, sizes, cou...  5.33 us
    pallas_call x1, Pallas kernels, on_device(): pl.pallas_call(lambda *refs: ahead_kernel(shard, spans[0], *refs), out_sh...  2.68 us
    unnamed x8, local copies, waits for them, and re-layouts  2.04 us
    pallas_call x2, Pallas kernels, finish(): pl.pallas_call(lambda *refs: kernel(scale_s, *refs), out_shape=wide, in_s...  1.91 us
    pallas_call x1, Pallas kernels, on_device(): pl.pallas_call(lambda *refs: far_kernel(shard, scales, spans, *refs), out...  1.84 us
  transfers between devices with their start and end apart: 27, of which 13 were waited for; matrix products, arithmetic and copies ran while one was open for 0% of the time, Pallas kernels for 9%

profile of v4, /device:TPU:0, one launch (start us, length us, event | category | flops | bytes accessed | tf_op | source)
XLA Modules:
  0.0 86.9 jit_solution(17370514896995668135)
XLA Ops:
  0.6 0.5 collective-permute-start.1
  1.2 2.6 %collective-permute-start.6 = (bf16[256,1280]{1,0:T(8,128)(2,1)}, bf16[256,1280]{1,0:T(8,128)(2,1)S(1)}, u32[]{:S(2)}, u32[]{:S(2)}) collective-permute-start(bf16[256,1280]{1,0:T(8,128)(2,1)} %second.3), channel_id=1, source_target_pairs={{0,2},{1,3},{2,0},{3,1},{4,6},{5,7},{6,4},{7,5},{8,10},{9,11},{10,... | collective-permute-start | bytes 1966088 | tf_op jit(solution)/shard_map/ppermute | solution.py:24
  3.7 3.6 %collective-permute-start.4 = (bf16[256,1280]{1,0:T(8,128)(2,1)}, bf16[256,1280]{1,0:T(8,128)(2,1)S(1)}, u32[]{:S(2)}, u32[]{:S(2)}) collective-permute-start(bf16[256,1280]{1,0:T(8,128)(2,1)} %second.3), channel_id=1, source_target_pairs={{0,24},{1,25},{2,26},{3,27},{4,28},{5,29},{6,30},{7,31},{8,0},{9,1... | collective-permute-start | bytes 1966088 | tf_op jit(solution)/shard_map/ppermute | solution.py:24
  7.3 1.1 %copy-done.1 = bf16[256,1280]{1,0:T(8,128)(2,1)S(1)} copy-done((bf16[256,1280]{1,0:T(8,128)(2,1)S(1)}, bf16[256,1280]{1,0:T(8,128)(2,1)}, u32[]{:S(2)}) %copy-start.1) | copy-done | bytes 655384
  8.4 0.9 %copy-done.2 = bf16[256,512]{1,0:T(8,128)(2,1)S(1)} copy-done((bf16[256,512]{1,0:T(8,128)(2,1)S(1)}, bf16[256,512]{1,0:T(8,128)(2,1)}, u32[]{:S(2)}) %copy-start.2) | copy-done | bytes 262168
  9.4 0.1 pack_images.1
  9.5 1.6 %collective-permute-start.2 = (bf16[112,1792]{1,0:T(8,128)(2,1)S(1)}, bf16[112,1792]{1,0:T(8,128)(2,1)S(1)}, u32[]{:S(2)}, u32[]{:S(2)}) collective-permute-start(bf16[112,1792]{1,0:T(8,128)(2,1)S(1)} %get-tuple-element.72), channel_id=1, source_target_pairs={{0,4},{1,5},{2,6},{3,7},{4,0},{5,1},{6,2},{7,3},{8,12},{9,13},{10,... | collective-permute-start | bytes 1204232 | tf_op jit(solution)/shard_map/ppermute | solution.py:24
  11.1 0.5 collective-permute-start.5
  11.6 0.4 collective-permute-start.3
  12.1 9.2 %collective-permute-done.2 = bf16[112,1792]{1,0:T(8,128)(2,1)S(1)} collective-permute-done((bf16[112,1792]{1,0:T(8,128)(2,1)S(1)}, bf16[112,1792]{1,0:T(8,128)(2,1)S(1)}, u32[]{:S(2)}, u32[]{:S(2)}) %collective-permute-start.2) | collective-permute-done | bytes 401440 | tf_op jit(solution)/shard_map/ppermute | solution.py:24
  21.3 1.5 %collective-permute-done.4.t_ahead = bf16[256,1280]{1,0:T(8,128)(2,1)S(1)} collective-permute-done((bf16[256,1280]{1,0:T(8,128)(2,1)}, bf16[256,1280]{1,0:T(8,128)(2,1)S(1)}, u32[]{:S(2)}, u32[]{:S(2)}) %collective-permute-start.4) | collective-permute-done | bytes 655392 | tf_op jit(solution)/shard_map/ppermute | solution.py:24
  22.7 2.1 %collective-permute-done.5.s_x = bf16[256,512]{1,0:T(8,128)(2,1)S(1)} collective-permute-done((bf16[256,512]{1,0:T(8,128)(2,1)}, bf16[256,512]{1,0:T(8,128)(2,1)S(1)}, u32[]{:S(2)}, u32[]{:S(2)}) %collective-permute-start.5) | collective-permute-done | bytes 262176 | tf_op jit(solution)/shard_map/ppermute | solution.py:24
  24.9 2.7 %collective-permute-done.3.s_ahead = bf16[256,512]{1,0:T(8,128)(2,1)S(1)} collective-permute-done((bf16[256,512]{1,0:T(8,128)(2,1)}, bf16[256,512]{1,0:T(8,128)(2,1)S(1)}, u32[]{:S(2)}, u32[]{:S(2)}) %collective-permute-start.3) | collective-permute-done | bytes 262176 | tf_op jit(solution)/shard_map/ppermute | solution.py:24
  27.6 0.2 pack_arrived.1
  27.8 0.6 collective-permute-start.10
  28.4 1.5 %collective-permute-start.7 = (bf16[144,1792]{1,0:T(8,128)(2,1)S(1)}, bf16[144,1792]{1,0:T(8,128)(2,1)S(1)}, u32[]{:S(2)}, u32[]{:S(2)}) collective-permute-start(bf16[144,1792]{1,0:T(8,128)(2,1)S(1)} %get-tuple-element.82), channel_id=1, source_target_pairs={{0,4},{1,5},{2,6},{3,7},{4,8},{5,9},{6,10},{7,11},{8,12},{9,13},{1... | collective-permute-start | bytes 1548296 | tf_op jit(solution)/shard_map/ppermute | solution.py:24
  29.9 2.2 %collective-permute-start.8 = (bf16[112,1792]{1,0:T(8,128)(2,1)S(1)}, bf16[112,1792]{1,0:T(8,128)(2,1)S(1)}, u32[]{:S(2)}, u32[]{:S(2)}) collective-permute-start(bf16[112,1792]{1,0:T(8,128)(2,1)S(1)} %collective-permute-done.2), channel_id=1, source_target_pairs={{0,8},{1,9},{2,10},{3,11},{4,4},{5,5},{6,6},{7,7},{8,16},{9,17},{1... | collective-permute-start | bytes 1204232 | tf_op jit(solution)/shard_map/ppermute | solution.py:24
  32.1 3.9 %collective-permute-start.9 = (bf16[32,1792]{1,0:T(8,128)(2,1)S(1)}, bf16[32,1792]{1,0:T(8,128)(2,1)S(1)}, u32[]{:S(2)}, u32[]{:S(2)}) collective-permute-start(bf16[32,1792]{1,0:T(8,128)(2,1)S(1)} %get-tuple-element.91), channel_id=1, source_target_pairs={{0,24},{1,25},{2,26},{3,27},{4,28},{5,29},{6,30},{7,31},{8,0},{9,1... | collective-permute-start | bytes 344072 | tf_op jit(solution)/shard_map/ppermute | solution.py:24
  36.2 2.5 %scores_home.1 = (f32[512,768]{1,0:T(8,128)S(1)}, f32[512,768]{1,0:T(8,128)S(1)}, f32[512,768]{1,0:T(8,128)S(1)}, f32[512,768]{1,0:T(8,128)S(1)}, f32[8,512]{1,0:T(8,128)S(1)}, /*index=5*/f32[8,768]{1,0:T(8,128)S(1)}) custom-call(bf16[256,1792]{1,0:T(8,128)(2,1)S(1)} %get-tuple-element.68.refs_0_.refs_25_.refs_7_, ...), custom_call_target="tpu_custom_call" | custom-call | tf_op jit(solution)/shard_map/scores_home/pallas_call | solution.py:448
  38.6 6.9 %collective-permute-done.8.refs_1_.refs_3_.refs_28_ = bf16[112,1792]{1,0:T(8,128)(2,1)S(1)} collective-permute-done((bf16[112,1792]{1,0:T(8,128)(2,1)S(1)}, bf16[112,1792]{1,0:T(8,128)(2,1)S(1)}, u32[]{:S(2)}, u32[]{:S(2)}) %collective-permute-start.8) | collective-permute-done | bytes 401440 | tf_op jit(solution)/shard_map/ppermute | solution.py:24
  45.5 0.3 collective-permute-done.7.refs_0_.refs_2_.refs_27_
  45.8 0.5 collective-permute-start.11
  46.3 1.5 %scores_near.1 = (f32[256,768]{1,0:T(8,128)S(1)}, f32[256,768]{1,0:T(8,128)S(1)}, f32[256,768]{1,0:T(8,128)S(1)}, f32[256,768]{1,0:T(8,128)S(1)}, f32[8,256]{1,0:T(8,128)S(1)}, /*index=5*/f32[4,768]{1,0:T(4,128)S(1)}) custom-call(bf16[144,1792]{1,0:T(8,128)(2,1)S(1)} %collective-permute-done.7.refs_0_.refs_2_.refs_27_, ...), custom_call_target="tpu_custom_call" | custom-call | tf_op jit(solution)/shard_map/scores_near/pallas_call | solution.py:448
  47.8 1.4 %scores_side.1 = (f32[768,256]{1,0:T(8,128)S(1)}, f32[768,256]{1,0:T(8,128)S(1)}, f32[768,256]{1,0:T(8,128)S(1)}, f32[768,256]{1,0:T(8,128)S(1)}, f32[8,768]{1,0:T(8,128)S(1)}, /*index=5*/f32[12,256]{1,0:T(8,128)S(1)}) custom-call(bf16[256,1792]{1,0:T(8,128)(2,1)S(1)} %get-tuple-element.68.refs_0_.refs_25_.refs_7_, ...), custom_call_target="tpu_custom_call" | custom-call | flops 99999997952 | bytes 1000000000 | tf_op jit(solution)/shard_map/scores_side/pallas_call | solution.py:448
  49.2 1.8 %scores_far.1 = (f32[256,1024]{1,0:T(8,128)S(1)}, f32[256,1024]{1,0:T(8,128)S(1)}, f32[256,1024]{1,0:T(8,128)S(1)}, f32[256,1024]{1,0:T(8,128)S(1)}, f32[8,256]{...) custom-call(bf16[144,1792]{1,0:T(8,128)(2,1)S(1)} %collective-permute-done.11.refs_0_.refs_29_, ...), custom_call_target="tpu_custom_call" | custom-call | tf_op jit(solution)/shard_map/scores_far/pallas_call | solution.py:470
  51.0 1.5 %collective-permute-start.14 = (f32[8,1024]{1,0:T(8,128)S(1)}, f32[8,1024]{1,0:T(8,128)S(1)}, u32[]{:S(2)}, u32[]{:S(2)}) collective-permute-start(f32[8,1024]{1,0:T(8,128)S(1)} %get-tuple-element.108.refs_0_), channel_id=1, source_target_pairs={{0,2},{1,3},{2,0},{3,1},{4,6},{5,7},{6,4},{7,5},{8,10},{9,11},{10,... | collective-permute-start | bytes 98312 | tf_op jit(solution)/shard_map/ppermute | solution.py:24
  52.5 2.4 %collective-permute-done.14.refs_2_ = f32[8,1024]{1,0:T(8,128)S(1)} collective-permute-done((f32[8,1024]{1,0:T(8,128)S(1)}, f32[8,1024]{1,0:T(8,128)S(1)}, u32[]{:S(2)}, u32[]{:S(2)}) %collective-permute-start.14) | collective-permute-done | bytes 32800 | tf_op jit(solution)/shard_map/ppermute | solution.py:24
  55.0 0.8 collective-permute-start.15
  55.8 4.1 %collective-permute-start.16 = (f32[8,512]{1,0:T(8,128)S(1)}, f32[8,512]{1,0:T(8,128)S(1)}, u32[]{:S(2)}, u32[]{:S(2)}) collective-permute-start(f32[8,512]{1,0:T(8,128)S(1)} %get-tuple-element.111), channel_id=1, source_target_pairs={{0,28},{1,29},{2,30},{3,31},{4,8},{5,9},{6,10},{7,11},{8,4},{9,5},... | collective-permute-start | bytes 49160 | tf_op jit(solution)/shard_map/ppermute | solution.py:24
  60.0 2.2 %collective-permute-done.16.refs_2_ = f32[8,512]{1,0:T(8,128)S(1)} collective-permute-done((f32[8,512]{1,0:T(8,128)S(1)}, f32[8,512]{1,0:T(8,128)S(1)}, u32[]{:S(2)}, u32[]{:S(2)}) %collective-permute-start.16) | collective-permute-done | bytes 16416 | tf_op jit(solution)/shard_map/ppermute | solution.py:24
  62.2 1.4 %collective-permute-done.17.refs_3_ = f32[8,512]{1,0:T(8,128)S(1)} collective-permute-done((f32[8,512]{1,0:T(8,128)S(1)}, f32[8,512]{1,0:T(8,128)S(1)}, u32[]{:S(2)}, u32[]{:S(2)}) %collective-permute-start.17) | collective-permute-done | bytes 16416 | tf_op jit(solution)/shard_map/ppermute | solution.py:24
  63.7 1.8 %collective-permute-done.18.refs_4_ = f32[8,512]{1,0:T(8,128)S(1)} collective-permute-done((f32[8,512]{1,0:T(8,128)S(1)}, f32[8,512]{1,0:T(8,128)S(1)}, u32[]{:S(2)}, u32[]{:S(2)}) %collective-permute-start.18) | collective-permute-done | bytes 16416 | tf_op jit(solution)/shard_map/ppermute | solution.py:24
  65.5 2.7 %gradients_ahead.1 = (f32[256,256]{1,0:T(8,128)S(1)}, f32[256,256]{1,0:T(8,128)S(1)}, bf16[256,256]{1,0:T(8,128)(2,1)S(1)}, bf16[256,256]{1,0:T(8,128)(2,1)S(1)}...) custom-call(f32[512,768]{1,0:T(8,128)S(1)} %get-tuple-element.78.ref, ...), custom_call_target="tpu_custom_call" | custom-call | tf_op jit(solution)/shard_map/gradients_ahead/pallas_call | solution.py:512
  68.2 0.1 collective-permute-start.20
  68.3 1.0 %collective-permute-start.19 = (bf16[256,256]{1,0:T(8,128)(2,1)S(1)}, bf16[256,256]{1,0:T(8,128)(2,1)S(1)}, u32[]{:S(2)}, u32[]{:S(2)}) collective-permute-start(bf16[256,256]{1,0:T(8,128)(2,1)S(1)} %get-tuple-element.115), channel_id=1, source_target_pairs={{0,2},{1,3},{2,0},{3,1},{4,6},{5,7},{6,4},{7,5},{8,10},{9,11},{10,... | collective-permute-start | bytes 393224 | tf_op jit(solution)/shard_map/ppermute | solution.py:24
  69.3 1.1 %collective-permute-start.22 = (bf16[256,256]{1,0:T(8,128)(2,1)S(1)}, bf16[256,256]{1,0:T(8,128)(2,1)S(1)}, u32[]{:S(2)}, u32[]{:S(2)}) collective-permute-start(bf16[256,256]{1,0:T(8,128)(2,1)S(1)} %get-tuple-element.124), channel_id=1, source_target_pairs={{0,2},{1,3},{2,0},{3,1},{4,6},{5,7},{6,4},{7,5},{8,10},{9,11},{10,... | collective-permute-start | bytes 393224 | tf_op jit(solution)/shard_map/ppermute | solution.py:24
  70.4 0.1 add_convert_fusion
  70.4 3.0 %collective-permute-start.26 = (bf16[256,512]{1,0:T(8,128)(2,1)S(1)}, bf16[256,512]{1,0:T(8,128)(2,1)S(1)}, u32[]{:S(2)}, u32[]{:S(2)}) collective-permute-start(bf16[256,512]{1,0:T(8,128)(2,1)S(1)} %add_convert_fusion), channel_id=1, source_target_pairs={{0,28},{1,29},{2,30},{3,31},{4,0},{5,1},{6,2},{7,3},{8,4},{9,5},{1... | collective-permute-start | bytes 786440 | tf_op jit(solution)/shard_map/ppermute | solution.py:24
  73.5 1.2 %collective-permute-done.19.second = bf16[256,256]{1,0:T(8,128)(2,1)S(1)} collective-permute-done((bf16[256,256]{1,0:T(8,128)(2,1)S(1)}, bf16[256,256]{1,0:T(8,128)(2,1)S(1)}, u32[]{:S(2)}, u32[]{:S(2)}) %collective-permute-start.19) | collective-permute-done | bytes 131104 | tf_op jit(solution)/shard_map/ppermute | solution.py:24
  74.7 0.3 collective-permute-start.21
  74.9 1.5 %gradients_home.1 = (f32[256,512]{1,0:T(8,128)S(1)}, bf16[256,512]{1,0:T(8,128)(2,1)S(1)}, f32[512,256]{1,0:T(8,128)S(1)}, bf16[512,256]{1,0:T(8,128)(2,1)S(1)}) custom-call(f32[512,768]{1,0:T(8,128)S(1)} %get-tuple-element.78.refs_0_, f32[512,768]{1,0:T(8,128)S(1)} %get-tuple-element.79.refs_1_, f32[512,768]{1,0:T(8,128)S(1)} %get-tuple-element.80.refs_2_, ...), custom_call_target="tpu_custom_call" | custom-call | tf_op jit(solution)/shard_map/gradients_home/pallas_call | solution.py:536
  76.4 0.6 collective-permute-done.22.second
  77.0 0.9 %collective-permute-start.24 = (bf16[512,256]{1,0:T(8,128)(2,1)S(1)}, bf16[512,256]{1,0:T(8,128)(2,1)S(1)}, u32[]{:S(2)}, u32[]{:S(2)}) collective-permute-start(bf16[512,256]{1,0:T(8,128)(2,1)S(1)} %get-tuple-element.127), channel_id=1, source_target_pairs={{0,2},{1,3},{2,0},{3,1},{4,6},{5,7},{6,4},{7,5},{8,10},{9,11},{10,... | collective-permute-start | bytes 786440 | tf_op jit(solution)/shard_map/ppermute | solution.py:24
  78.0 0.3 collective-permute-start.23
  78.2 6.6 %collective-permute-done.24.second = bf16[512,256]{1,0:T(8,128)(2,1)S(1)} collective-permute-done((bf16[512,256]{1,0:T(8,128)(2,1)S(1)}, bf16[512,256]{1,0:T(8,128)(2,1)S(1)}, u32[]{:S(2)}, u32[]{:S(2)}) %collective-permute-start.24) | collective-permute-done | bytes 262176 | tf_op jit(solution)/shard_map/ppermute | solution.py:24
  84.9 0.1 add_own_text.1.refs_0_
  85.0 0.9 %finish_image.1 = f32[256,512]{1,0:T(8,128)} custom-call(f32[256,512]{1,0:T(8,128)S(1)} %get-tuple-element.128.refs_0_, bf16[256,512]{1,0:T(8,128)(2,1)S(1)} %collective-permute-done.25.refs_1_, bf16[256,512]{1,0:T(8,128)(2,1)S(1)} %collective-permute-done.26.refs_2_), custom_call_target="tpu_custom_call" | custom-call | tf_op jit(solution)/shard_map/finish_image/pallas_call | solution.py:568
  85.9 1.0 %finish_text.1 = f32[256,512]{1,0:T(8,128)} custom-call(f32[512,256]{1,0:T(8,128)S(1)} %add_own_text.1.refs_0_, bf16[256,256]{1,0:T(8,128)(2,1)S(1)} %collective-permute-done.21.refs_1_, bf16[256,256]{1,0:T(8,128)(2,1)S(1)} %collective-permute-done.23.refs_2_), custom_call_target="tpu_custom_call" | custom-call | tf_op jit(solution)/shard_map/finish_text/pallas_call | solution.py:568
  (32 shorter events, 0.4 us)
Async XLA Ops:
  0.6 35.4 %copy-start = (bf16[256,1280]{1,0:T(8,128)(2,1)S(1)}, bf16[256,1280]{1,0:T(8,128)(2,1)}, u32[]{:S(2)}) copy-start(bf16[256,1280]{1,0:T(8,128)(2,1)} %second.3) | copy-start | bytes 1966084
  0.6 10.4 %collective-permute-start.1 = (bf16[256,1280]{1,0:T(8,128)(2,1)}, bf16[256,1280]{1,0:T(8,128)(2,1)S(1)}, u32[]{:S(2)}, u32[]{:S(2)}) collective-permute-start(bf16[256,1280]{1,0:T(8,128)(2,1)} %second.2), channel_id=1, source_target_pairs={{0,1},{1,0},{2,3},{3,2},{4,5},{5,4},{6,7},{7,6},{8,9},{9,8},{10,11... | collective-permute-start | bytes 1966088 | tf_op jit(solution)/shard_map/ppermute | solution.py:24
  1.2 20.1 %collective-permute-start.6 = (bf16[256,1280]{1,0:T(8,128)(2,1)}, bf16[256,1280]{1,0:T(8,128)(2,1)S(1)}, u32[]{:S(2)}, u32[]{:S(2)}) collective-permute-start(bf16[256,1280]{1,0:T(8,128)(2,1)} %second.3), channel_id=1, source_target_pairs={{0,2},{1,3},{2,0},{3,1},{4,6},{5,7},{6,4},{7,5},{8,10},{9,11},{10,... | collective-permute-start | bytes 1966088 | tf_op jit(solution)/shard_map/ppermute | solution.py:24
  3.7 19.0 %collective-permute-start.4 = (bf16[256,1280]{1,0:T(8,128)(2,1)}, bf16[256,1280]{1,0:T(8,128)(2,1)S(1)}, u32[]{:S(2)}, u32[]{:S(2)}) collective-permute-start(bf16[256,1280]{1,0:T(8,128)(2,1)} %second.3), channel_id=1, source_target_pairs={{0,24},{1,25},{2,26},{3,27},{4,28},{5,29},{6,30},{7,31},{8,0},{9,1... | collective-permute-start | bytes 1966088 | tf_op jit(solution)/shard_map/ppermute | solution.py:24
  7.3 3.8 %collective-permute-start = (bf16[256,512]{1,0:T(8,128)(2,1)}, bf16[256,512]{1,0:T(8,128)(2,1)S(1)}, u32[]{:S(2)}, u32[]{:S(2)}) collective-permute-start(bf16[256,512]{1,0:T(8,128)(2,1)} %first.2), channel_id=1, source_target_pairs={{0,1},{1,0},{2,3},{3,2},{4,5},{5,4},{6,7},{7,6},{8,9},{9,8},{10,11... | collective-permute-start | bytes 786440 | tf_op jit(solution)/shard_map/ppermute | solution.py:24
  7.3 1.1 %copy-start.1 = (bf16[256,1280]{1,0:T(8,128)(2,1)S(1)}, bf16[256,1280]{1,0:T(8,128)(2,1)}, u32[]{:S(2)}) copy-start(bf16[256,1280]{1,0:T(8,128)(2,1)} %second.2) | copy-start | bytes 1966084
  8.4 0.9 %copy-start.2 = (bf16[256,512]{1,0:T(8,128)(2,1)S(1)}, bf16[256,512]{1,0:T(8,128)(2,1)}, u32[]{:S(2)}) copy-start(bf16[256,512]{1,0:T(8,128)(2,1)} %first.2) | copy-start | bytes 786436
  9.4 26.7 %copy-start.3 = (bf16[256,512]{1,0:T(8,128)(2,1)S(1)}, bf16[256,512]{1,0:T(8,128)(2,1)}, u32[]{:S(2)}) copy-start(bf16[256,512]{1,0:T(8,128)(2,1)} %first.3) | copy-start | bytes 786436
  9.5 11.8 %collective-permute-start.2 = (bf16[112,1792]{1,0:T(8,128)(2,1)S(1)}, bf16[112,1792]{1,0:T(8,128)(2,1)S(1)}, u32[]{:S(2)}, u32[]{:S(2)}) collective-permute-start(bf16[112,1792]{1,0:T(8,128)(2,1)S(1)} %get-tuple-element.72), channel_id=1, source_target_pairs={{0,4},{1,5},{2,6},{3,7},{4,0},{5,1},{6,2},{7,3},{8,12},{9,13},{10,... | collective-permute-start | bytes 1204232 | tf_op jit(solution)/shard_map/ppermute | solution.py:24
  11.1 13.8 %collective-permute-start.5 = (bf16[256,512]{1,0:T(8,128)(2,1)}, bf16[256,512]{1,0:T(8,128)(2,1)S(1)}, u32[]{:S(2)}, u32[]{:S(2)}) collective-permute-start(bf16[256,512]{1,0:T(8,128)(2,1)} %first.3), channel_id=1, source_target_pairs={{0,2},{1,3},{2,0},{3,1},{4,6},{5,7},{6,4},{7,5},{8,10},{9,11},{10,... | collective-permute-start | bytes 786440 | tf_op jit(solution)/shard_map/ppermute | solution.py:24
  11.6 16.0 %collective-permute-start.3 = (bf16[256,512]{1,0:T(8,128)(2,1)}, bf16[256,512]{1,0:T(8,128)(2,1)S(1)}, u32[]{:S(2)}, u32[]{:S(2)}) collective-permute-start(bf16[256,512]{1,0:T(8,128)(2,1)} %first.3), channel_id=1, source_target_pairs={{0,24},{1,25},{2,26},{3,27},{4,28},{5,29},{6,30},{7,31},{8,0},{9,1... | collective-permute-start | bytes 786440 | tf_op jit(solution)/shard_map/ppermute | solution.py:24
  27.8 20.0 %collective-permute-start.10 = (bf16[224,1792]{1,0:T(8,128)(2,1)S(1)}, bf16[224,1792]{1,0:T(8,128)(2,1)S(1)}, u32[]{:S(2)}, u32[]{:S(2)}) collective-permute-start(bf16[224,1792]{1,0:T(8,128)(2,1)S(1)} %get-tuple-element.92), channel_id=1, source_target_pairs={{0,2},{1,3},{2,0},{3,1},{4,6},{5,7},{6,4},{7,5},{8,10},{9,11},{10,... | collective-permute-start | bytes 2408456 | tf_op jit(solution)/shard_map/ppermute | solution.py:24
  28.4 17.4 %collective-permute-start.7 = (bf16[144,1792]{1,0:T(8,128)(2,1)S(1)}, bf16[144,1792]{1,0:T(8,128)(2,1)S(1)}, u32[]{:S(2)}, u32[]{:S(2)}) collective-permute-start(bf16[144,1792]{1,0:T(8,128)(2,1)S(1)} %get-tuple-element.82), channel_id=1, source_target_pairs={{0,4},{1,5},{2,6},{3,7},{4,8},{5,9},{6,10},{7,11},{8,12},{9,13},{1... | collective-permute-start | bytes 1548296 | tf_op jit(solution)/shard_map/ppermute | solution.py:24
  29.9 15.6 %collective-permute-start.8 = (bf16[112,1792]{1,0:T(8,128)(2,1)S(1)}, bf16[112,1792]{1,0:T(8,128)(2,1)S(1)}, u32[]{:S(2)}, u32[]{:S(2)}) collective-permute-start(bf16[112,1792]{1,0:T(8,128)(2,1)S(1)} %collective-permute-done.2), channel_id=1, source_target_pairs={{0,8},{1,9},{2,10},{3,11},{4,4},{5,5},{6,6},{7,7},{8,16},{9,17},{1... | collective-permute-start | bytes 1204232 | tf_op jit(solution)/shard_map/ppermute | solution.py:24
  32.1 15.6 %collective-permute-start.9 = (bf16[32,1792]{1,0:T(8,128)(2,1)S(1)}, bf16[32,1792]{1,0:T(8,128)(2,1)S(1)}, u32[]{:S(2)}, u32[]{:S(2)}) collective-permute-start(bf16[32,1792]{1,0:T(8,128)(2,1)S(1)} %get-tuple-element.91), channel_id=1, source_target_pairs={{0,24},{1,25},{2,26},{3,27},{4,28},{5,29},{6,30},{7,31},{8,0},{9,1... | collective-permute-start | bytes 344072 | tf_op jit(solution)/shard_map/ppermute | solution.py:24
  45.8 3.4 %collective-permute-start.12 = (bf16[112,1792]{1,0:T(8,128)(2,1)S(1)}, bf16[112,1792]{1,0:T(8,128)(2,1)S(1)}, u32[]{:S(2)}, u32[]{:S(2)}) collective-permute-start(bf16[112,1792]{1,0:T(8,128)(2,1)S(1)} %collective-permute-done.8.refs_1_.refs_3_.refs_28_), channel_id=1, source_target_pairs={{0,1},{1,0},{2,3},{3,2},{4,5},{5,4},{6,7},{7,6},{8,9},{9,8},{10,11... | collective-permute-start | bytes 1204232 | tf_op jit(solution)/shard_map/ppermute | solution.py:24
  45.8 3.4 %collective-permute-start.11 = (bf16[144,1792]{1,0:T(8,128)(2,1)S(1)}, bf16[144,1792]{1,0:T(8,128)(2,1)S(1)}, u32[]{:S(2)}, u32[]{:S(2)}) collective-permute-start(bf16[144,1792]{1,0:T(8,128)(2,1)S(1)} %collective-permute-done.7.refs_0_.refs_2_.refs_27_), channel_id=1, source_target_pairs={{0,1},{1,0},{2,3},{3,2},{4,5},{5,4},{6,7},{7,6},{8,9},{9,8},{10,11... | collective-permute-start | bytes 1548296 | tf_op jit(solution)/shard_map/ppermute | solution.py:24
  51.0 3.9 %collective-permute-start.14 = (f32[8,1024]{1,0:T(8,128)S(1)}, f32[8,1024]{1,0:T(8,128)S(1)}, u32[]{:S(2)}, u32[]{:S(2)}) collective-permute-start(f32[8,1024]{1,0:T(8,128)S(1)} %get-tuple-element.108.refs_0_), channel_id=1, source_target_pairs={{0,2},{1,3},{2,0},{3,1},{4,6},{5,7},{6,4},{7,5},{8,10},{9,11},{10,... | collective-permute-start | bytes 98312 | tf_op jit(solution)/shard_map/ppermute | solution.py:24
  52.5 2.4 %collective-permute-start.13 = (f32[8,1024]{1,0:T(8,128)S(1)}, f32[8,1024]{1,0:T(8,128)S(1)}, u32[]{:S(2)}, u32[]{:S(2)}) collective-permute-start(f32[8,1024]{1,0:T(8,128)S(1)} %get-tuple-element.108.refs_0_), channel_id=1, source_target_pairs={{0,1},{1,0},{2,3},{3,2},{4,5},{5,4},{6,7},{7,6},{8,9},{9,8},{10,11... | collective-permute-start | bytes 98312 | tf_op jit(solution)/shard_map/ppermute | solution.py:24
  55.0 5.0 %collective-permute-start.15 = (f32[8,512]{1,0:T(8,128)S(1)}, f32[8,512]{1,0:T(8,128)S(1)}, u32[]{:S(2)}, u32[]{:S(2)}) collective-permute-start(f32[8,512]{1,0:T(8,128)S(1)} %get-tuple-element.110), channel_id=1, source_target_pairs={{0,4},{1,5},{2,6},{3,7},{4,0},{5,1},{6,2},{7,3},{8,12},{9,13},{10,... | collective-permute-start | bytes 49160 | tf_op jit(solution)/shard_map/ppermute | solution.py:24
  55.8 6.4 %collective-permute-start.16 = (f32[8,512]{1,0:T(8,128)S(1)}, f32[8,512]{1,0:T(8,128)S(1)}, u32[]{:S(2)}, u32[]{:S(2)}) collective-permute-start(f32[8,512]{1,0:T(8,128)S(1)} %get-tuple-element.111), channel_id=1, source_target_pairs={{0,28},{1,29},{2,30},{3,31},{4,8},{5,9},{6,10},{7,11},{8,4},{9,5},... | collective-permute-start | bytes 49160 | tf_op jit(solution)/shard_map/ppermute | solution.py:24
  59.9 3.7 %collective-permute-start.17 = (f32[8,512]{1,0:T(8,128)S(1)}, f32[8,512]{1,0:T(8,128)S(1)}, u32[]{:S(2)}, u32[]{:S(2)}) collective-permute-start(f32[8,512]{1,0:T(8,128)S(1)} %get-tuple-element.112), channel_id=1, source_target_pairs={{0,8},{1,9},{2,10},{3,11},{4,12},{5,13},{6,14},{7,15},{8,0},{9,1},... | collective-permute-start | bytes 49160 | tf_op jit(solution)/shard_map/ppermute | solution.py:24
  59.9 5.5 %collective-permute-start.18 = (f32[8,512]{1,0:T(8,128)S(1)}, f32[8,512]{1,0:T(8,128)S(1)}, u32[]{:S(2)}, u32[]{:S(2)}) collective-permute-start(f32[8,512]{1,0:T(8,128)S(1)} %get-tuple-element.113), channel_id=1, source_target_pairs={{0,24},{1,25},{2,26},{3,27},{4,28},{5,29},{6,30},{7,31},{8,16},{9,... | collective-permute-start | bytes 49160 | tf_op jit(solution)/shard_map/ppermute | solution.py:24
  68.2 2.2 %collective-permute-start.20 = (bf16[256,512]{1,0:T(8,128)(2,1)S(1)}, bf16[256,512]{1,0:T(8,128)(2,1)S(1)}, u32[]{:S(2)}, u32[]{:S(2)}) collective-permute-start(bf16[256,512]{1,0:T(8,128)(2,1)S(1)} %get-tuple-element.117), channel_id=1, source_target_pairs={{0,1},{1,0},{2,3},{3,2},{4,5},{5,4},{6,7},{7,6},{8,9},{9,8},{10,11... | collective-permute-start | bytes 786440 | tf_op jit(solution)/shard_map/ppermute | solution.py:24
  68.3 6.4 %collective-permute-start.19 = (bf16[256,256]{1,0:T(8,128)(2,1)S(1)}, bf16[256,256]{1,0:T(8,128)(2,1)S(1)}, u32[]{:S(2)}, u32[]{:S(2)}) collective-permute-start(bf16[256,256]{1,0:T(8,128)(2,1)S(1)} %get-tuple-element.115), channel_id=1, source_target_pairs={{0,2},{1,3},{2,0},{3,1},{4,6},{5,7},{6,4},{7,5},{8,10},{9,11},{10,... | collective-permute-start | bytes 393224 | tf_op jit(solution)/shard_map/ppermute | solution.py:24
  69.3 7.7 %collective-permute-start.22 = (bf16[256,256]{1,0:T(8,128)(2,1)S(1)}, bf16[256,256]{1,0:T(8,128)(2,1)S(1)}, u32[]{:S(2)}, u32[]{:S(2)}) collective-permute-start(bf16[256,256]{1,0:T(8,128)(2,1)S(1)} %get-tuple-element.124), channel_id=1, source_target_pairs={{0,2},{1,3},{2,0},{3,1},{4,6},{5,7},{6,4},{7,5},{8,10},{9,11},{10,... | collective-permute-start | bytes 393224 | tf_op jit(solution)/shard_map/ppermute | solution.py:24
  70.4 14.5 %collective-permute-start.26 = (bf16[256,512]{1,0:T(8,128)(2,1)S(1)}, bf16[256,512]{1,0:T(8,128)(2,1)S(1)}, u32[]{:S(2)}, u32[]{:S(2)}) collective-permute-start(bf16[256,512]{1,0:T(8,128)(2,1)S(1)} %add_convert_fusion), channel_id=1, source_target_pairs={{0,28},{1,29},{2,30},{3,31},{4,0},{5,1},{6,2},{7,3},{8,4},{9,5},{1... | collective-permute-start | bytes 786440 | tf_op jit(solution)/shard_map/ppermute | solution.py:24
  74.7 11.2 %collective-permute-start.21 = (bf16[256,256]{1,0:T(8,128)(2,1)S(1)}, bf16[256,256]{1,0:T(8,128)(2,1)S(1)}, u32[]{:S(2)}, u32[]{:S(2)}) collective-permute-start(bf16[256,256]{1,0:T(8,128)(2,1)S(1)} %add_text.2), channel_id=1, source_target_pairs={{0,8},{1,9},{2,10},{3,11},{4,12},{5,13},{6,14},{7,15},{8,16},{9,17... | collective-permute-start | bytes 393224 | tf_op jit(solution)/shard_map/ppermute | solution.py:24
  77.0 7.9 %collective-permute-start.24 = (bf16[512,256]{1,0:T(8,128)(2,1)S(1)}, bf16[512,256]{1,0:T(8,128)(2,1)S(1)}, u32[]{:S(2)}, u32[]{:S(2)}) collective-permute-start(bf16[512,256]{1,0:T(8,128)(2,1)S(1)} %get-tuple-element.127), channel_id=1, source_target_pairs={{0,2},{1,3},{2,0},{3,1},{4,6},{5,7},{6,4},{7,5},{8,10},{9,11},{10,... | collective-permute-start | bytes 786440 | tf_op jit(solution)/shard_map/ppermute | solution.py:24
  78.0 7.9 %collective-permute-start.23 = (bf16[256,256]{1,0:T(8,128)(2,1)S(1)}, bf16[256,256]{1,0:T(8,128)(2,1)S(1)}, u32[]{:S(2)}, u32[]{:S(2)}) collective-permute-start(bf16[256,256]{1,0:T(8,128)(2,1)S(1)} %add_text.3), channel_id=1, source_target_pairs={{0,8},{1,9},{2,10},{3,11},{4,12},{5,13},{6,14},{7,15},{8,16},{9,17... | collective-permute-start | bytes 393224 | tf_op jit(solution)/shard_map/ppermute | solution.py:24
  78.2 6.7 %collective-permute-start.25 = (bf16[256,512]{1,0:T(8,128)(2,1)S(1)}, bf16[256,512]{1,0:T(8,128)(2,1)S(1)}, u32[]{:S(2)}, u32[]{:S(2)}) collective-permute-start(bf16[256,512]{1,0:T(8,128)(2,1)S(1)} %get-tuple-element.129), channel_id=1, source_target_pairs={{0,1},{1,0},{2,3},{3,2},{4,5},{5,4},{6,7},{7,6},{8,9},{9,8},{10,11... | collective-permute-start | bytes 786440 | tf_op jit(solution)/shard_map/ppermute | solution.py:24

commit v5 on v4

--- a/solution.py
+++ b/solution.py
@@ -368,12 +368,12 @@
     out[...] = (total + home[...].astype(jnp.float32)) * scale
 
 
-def finish_text_kernel(scale, own, *refs):
+def finish_text_kernel(scale, own, x, *refs):
     homes, out = refs[:-1], refs[-1]
     width = homes[0].shape[0]
     for index, home in enumerate(homes):
         here = slice(index * width, (index + 1) * width)
-        total = own[here] + home[...].astype(jnp.float32)
+        total = own[here] + x[here].astype(jnp.float32) + home[...].astype(jnp.float32)
         out[:, here] = total.T * scale
 
 
@@ -562,21 +562,25 @@
     txt_home = [
         ahead(txt_sum, 2), ahead(add(txt_same[1], txt_cross[1], sent_half, "add_text"), 2)
     ]
-    txt_own = add(txt_own, to_other_x(txt_x), tall, "add_own_text")
-
-    def finish(kernel, *args, name):
+    txt_x = to_other_x(txt_x)
+
+    def finish(kernel, *args, name, cost=None):
         return pl.pallas_call(
             lambda *refs: kernel(scale_s, *refs),
             out_shape=wide,
             in_specs=[vmem] * len(args),
             out_specs=vmem,
             compiler_params=params(8),
+            cost_estimate=cost,
             name=name,
         )(*args)
 
-    grad_image = finish(finish_image_kernel, img_own, img_core, img_home, name="finish_image")
-    *txt_home, txt_own, grad_image = lax.optimization_barrier((*txt_home, txt_own, grad_image))
-    grad_text = finish(finish_text_kernel, txt_own, *txt_home, name="finish_text")
+    img_home, txt_x = lax.optimization_barrier((img_home, txt_x))
+    grad_image = finish(
+        finish_image_kernel, img_own, img_core, img_home, name="finish_image", cost=LIGHT
+    )
+    *txt_home, grad_image = lax.optimization_barrier((*txt_home, grad_image))
+    grad_text = finish(finish_text_kernel, txt_own, txt_x, *txt_home, name="finish_text")
     return (grad_image, grad_text)
 
 

time: 87.1 us -> 87 us (level)
  no operation moved by 1% of the time
where the time goes in v5:
time: 87 us; the launch traced here: 86.8 us
  waiting for transfers between devices  39 us (45%)
  starting transfers between devices  31.2 us (36%)
  Pallas kernels  13.8 us (16%)
  local copies, waits for them, and re-layouts  2.04 us (2%)
    ppermute x27, waiting for transfers between devices, send_to(): return lax.ppermute(value, AXES, pairs)  39 us
    ppermute x27, starting transfers between devices, send_to(): return lax.ppermute(value, AXES, pairs)  31.2 us
    pallas_call x3, Pallas kernels, part_scores(): pl.pallas_call(lambda *refs: part_kernel(shard, scales, spans, sizes, cou...  5.33 us
    pallas_call x1, Pallas kernels, on_device(): pl.pallas_call(lambda *refs: ahead_kernel(shard, spans[0], *refs), out_sh...  2.68 us
    unnamed x8, local copies, waits for them, and re-layouts  2.04 us
    pallas_call x2, Pallas kernels, finish(): pl.pallas_call(lambda *refs: kernel(scale_s, *refs), out_shape=wide, in_s...  1.9 us
    pallas_call x1, Pallas kernels, on_device(): pl.pallas_call(lambda *refs: far_kernel(shard, scales, spans, *refs), out...  1.84 us
  transfers between devices with their start and end apart: 27, of which 13 were waited for; matrix products, arithmetic and copies ran while one was open for 0% of the time, Pallas kernels for 9%

profile of v5, /device:TPU:0, one launch (start us, length us, event | category | flops | bytes accessed | tf_op | source)
XLA Modules:
  0.0 86.8 jit_solution(4719553077502081090)
XLA Ops:
  0.6 0.5 collective-permute-start.1
  1.2 2.6 %collective-permute-start.6 = (bf16[256,1280]{1,0:T(8,128)(2,1)}, bf16[256,1280]{1,0:T(8,128)(2,1)S(1)}, u32[]{:S(2)}, u32[]{:S(2)}) collective-permute-start(bf16[256,1280]{1,0:T(8,128)(2,1)} %second.3), channel_id=1, source_target_pairs={{0,2},{1,3},{2,0},{3,1},{4,6},{5,7},{6,4},{7,5},{8,10},{9,11},{10,... | collective-permute-start | bytes 1966088 | tf_op jit(solution)/shard_map/ppermute | solution.py:24
  3.7 3.6 %collective-permute-start.4 = (bf16[256,1280]{1,0:T(8,128)(2,1)}, bf16[256,1280]{1,0:T(8,128)(2,1)S(1)}, u32[]{:S(2)}, u32[]{:S(2)}) collective-permute-start(bf16[256,1280]{1,0:T(8,128)(2,1)} %second.3), channel_id=1, source_target_pairs={{0,24},{1,25},{2,26},{3,27},{4,28},{5,29},{6,30},{7,31},{8,0},{9,1... | collective-permute-start | bytes 1966088 | tf_op jit(solution)/shard_map/ppermute | solution.py:24
  7.3 1.1 %copy-done.1 = bf16[256,1280]{1,0:T(8,128)(2,1)S(1)} copy-done((bf16[256,1280]{1,0:T(8,128)(2,1)S(1)}, bf16[256,1280]{1,0:T(8,128)(2,1)}, u32[]{:S(2)}) %copy-start.1) | copy-done | bytes 655384
  8.4 0.9 %copy-done.2 = bf16[256,512]{1,0:T(8,128)(2,1)S(1)} copy-done((bf16[256,512]{1,0:T(8,128)(2,1)S(1)}, bf16[256,512]{1,0:T(8,128)(2,1)}, u32[]{:S(2)}) %copy-start.2) | copy-done | bytes 262168
  9.4 0.1 pack_images.1
  9.5 1.6 %collective-permute-start.2 = (bf16[112,1792]{1,0:T(8,128)(2,1)S(1)}, bf16[112,1792]{1,0:T(8,128)(2,1)S(1)}, u32[]{:S(2)}, u32[]{:S(2)}) collective-permute-start(bf16[112,1792]{1,0:T(8,128)(2,1)S(1)} %get-tuple-element.73), channel_id=1, source_target_pairs={{0,4},{1,5},{2,6},{3,7},{4,0},{5,1},{6,2},{7,3},{8,12},{9,13},{10,... | collective-permute-start | bytes 1204232 | tf_op jit(solution)/shard_map/ppermute | solution.py:24
  11.1 0.5 collective-permute-start.5
  11.6 0.4 collective-permute-start.3
  12.1 9.2 %collective-permute-done.2 = bf16[112,1792]{1,0:T(8,128)(2,1)S(1)} collective-permute-done((bf16[112,1792]{1,0:T(8,128)(2,1)S(1)}, bf16[112,1792]{1,0:T(8,128)(2,1)S(1)}, u32[]{:S(2)}, u32[]{:S(2)}) %collective-permute-start.2) | collective-permute-done | bytes 401440 | tf_op jit(solution)/shard_map/ppermute | solution.py:24
  21.3 1.5 %collective-permute-done.4.t_ahead = bf16[256,1280]{1,0:T(8,128)(2,1)S(1)} collective-permute-done((bf16[256,1280]{1,0:T(8,128)(2,1)}, bf16[256,1280]{1,0:T(8,128)(2,1)S(1)}, u32[]{:S(2)}, u32[]{:S(2)}) %collective-permute-start.4) | collective-permute-done | bytes 655392 | tf_op jit(solution)/shard_map/ppermute | solution.py:24
  22.7 2.1 %collective-permute-done.5.s_x = bf16[256,512]{1,0:T(8,128)(2,1)S(1)} collective-permute-done((bf16[256,512]{1,0:T(8,128)(2,1)}, bf16[256,512]{1,0:T(8,128)(2,1)S(1)}, u32[]{:S(2)}, u32[]{:S(2)}) %collective-permute-start.5) | collective-permute-done | bytes 262176 | tf_op jit(solution)/shard_map/ppermute | solution.py:24
  24.9 2.7 %collective-permute-done.3.s_ahead = bf16[256,512]{1,0:T(8,128)(2,1)S(1)} collective-permute-done((bf16[256,512]{1,0:T(8,128)(2,1)}, bf16[256,512]{1,0:T(8,128)(2,1)S(1)}, u32[]{:S(2)}, u32[]{:S(2)}) %collective-permute-start.3) | collective-permute-done | bytes 262176 | tf_op jit(solution)/shard_map/ppermute | solution.py:24
  27.6 0.2 pack_arrived.1
  27.8 0.6 collective-permute-start.10
  28.4 1.5 %collective-permute-start.7 = (bf16[144,1792]{1,0:T(8,128)(2,1)S(1)}, bf16[144,1792]{1,0:T(8,128)(2,1)S(1)}, u32[]{:S(2)}, u32[]{:S(2)}) collective-permute-start(bf16[144,1792]{1,0:T(8,128)(2,1)S(1)} %get-tuple-element.83), channel_id=1, source_target_pairs={{0,4},{1,5},{2,6},{3,7},{4,8},{5,9},{6,10},{7,11},{8,12},{9,13},{1... | collective-permute-start | bytes 1548296 | tf_op jit(solution)/shard_map/ppermute | solution.py:24
  29.9 2.2 %collective-permute-start.8 = (bf16[112,1792]{1,0:T(8,128)(2,1)S(1)}, bf16[112,1792]{1,0:T(8,128)(2,1)S(1)}, u32[]{:S(2)}, u32[]{:S(2)}) collective-permute-start(bf16[112,1792]{1,0:T(8,128)(2,1)S(1)} %collective-permute-done.2), channel_id=1, source_target_pairs={{0,8},{1,9},{2,10},{3,11},{4,4},{5,5},{6,6},{7,7},{8,16},{9,17},{1... | collective-permute-start | bytes 1204232 | tf_op jit(solution)/shard_map/ppermute | solution.py:24
  32.1 3.9 %collective-permute-start.9 = (bf16[32,1792]{1,0:T(8,128)(2,1)S(1)}, bf16[32,1792]{1,0:T(8,128)(2,1)S(1)}, u32[]{:S(2)}, u32[]{:S(2)}) collective-permute-start(bf16[32,1792]{1,0:T(8,128)(2,1)S(1)} %get-tuple-element.92), channel_id=1, source_target_pairs={{0,24},{1,25},{2,26},{3,27},{4,28},{5,29},{6,30},{7,31},{8,0},{9,1... | collective-permute-start | bytes 344072 | tf_op jit(solution)/shard_map/ppermute | solution.py:24
  36.1 0.1 pack_core.1.refs_1_.refs_26_.refs_8_
  36.2 2.5 %scores_home.1 = (f32[512,768]{1,0:T(8,128)S(1)}, f32[512,768]{1,0:T(8,128)S(1)}, f32[512,768]{1,0:T(8,128)S(1)}, f32[512,768]{1,0:T(8,128)S(1)}, f32[8,512]{1,0:T(8,128)S(1)}, /*index=5*/f32[8,768]{1,0:T(8,128)S(1)}) custom-call(bf16[256,1792]{1,0:T(8,128)(2,1)S(1)} %get-tuple-element.69.refs_0_.refs_25_.refs_7_, ...), custom_call_target="tpu_custom_call" | custom-call | tf_op jit(solution)/shard_map/scores_home/pallas_call | solution.py:448
  38.6 6.9 %collective-permute-done.8.refs_1_.refs_3_.refs_28_ = bf16[112,1792]{1,0:T(8,128)(2,1)S(1)} collective-permute-done((bf16[112,1792]{1,0:T(8,128)(2,1)S(1)}, bf16[112,1792]{1,0:T(8,128)(2,1)S(1)}, u32[]{:S(2)}, u32[]{:S(2)}) %collective-permute-start.8) | collective-permute-done | bytes 401440 | tf_op jit(solution)/shard_map/ppermute | solution.py:24
  45.5 0.3 collective-permute-done.7.refs_0_.refs_2_.refs_27_
  45.8 0.5 collective-permute-start.11
  46.3 1.5 %scores_near.1 = (f32[256,768]{1,0:T(8,128)S(1)}, f32[256,768]{1,0:T(8,128)S(1)}, f32[256,768]{1,0:T(8,128)S(1)}, f32[256,768]{1,0:T(8,128)S(1)}, f32[8,256]{1,0:T(8,128)S(1)}, /*index=5*/f32[4,768]{1,0:T(4,128)S(1)}) custom-call(bf16[144,1792]{1,0:T(8,128)(2,1)S(1)} %collective-permute-done.7.refs_0_.refs_2_.refs_27_, ...), custom_call_target="tpu_custom_call" | custom-call | tf_op jit(solution)/shard_map/scores_near/pallas_call | solution.py:448
  47.8 1.4 %scores_side.1 = (f32[768,256]{1,0:T(8,128)S(1)}, f32[768,256]{1,0:T(8,128)S(1)}, f32[768,256]{1,0:T(8,128)S(1)}, f32[768,256]{1,0:T(8,128)S(1)}, f32[8,768]{1,0:T(8,128)S(1)}, /*index=5*/f32[12,256]{1,0:T(8,128)S(1)}) custom-call(bf16[256,1792]{1,0:T(8,128)(2,1)S(1)} %get-tuple-element.69.refs_0_.refs_25_.refs_7_, ...), custom_call_target="tpu_custom_call" | custom-call | flops 99999997952 | bytes 1000000000 | tf_op jit(solution)/shard_map/scores_side/pallas_call | solution.py:448
  49.2 1.8 %scores_far.1 = (f32[256,1024]{1,0:T(8,128)S(1)}, f32[256,1024]{1,0:T(8,128)S(1)}, f32[256,1024]{1,0:T(8,128)S(1)}, f32[256,1024]{1,0:T(8,128)S(1)}, f32[8,256]{...) custom-call(bf16[144,1792]{1,0:T(8,128)(2,1)S(1)} %collective-permute-done.11.refs_0_.refs_29_, ...), custom_call_target="tpu_custom_call" | custom-call | tf_op jit(solution)/shard_map/scores_far/pallas_call | solution.py:470
  51.0 1.5 %collective-permute-start.14 = (f32[8,1024]{1,0:T(8,128)S(1)}, f32[8,1024]{1,0:T(8,128)S(1)}, u32[]{:S(2)}, u32[]{:S(2)}) collective-permute-start(f32[8,1024]{1,0:T(8,128)S(1)} %get-tuple-element.109.refs_0_), channel_id=1, source_target_pairs={{0,2},{1,3},{2,0},{3,1},{4,6},{5,7},{6,4},{7,5},{8,10},{9,11},{10,... | collective-permute-start | bytes 98312 | tf_op jit(solution)/shard_map/ppermute | solution.py:24
  52.5 2.4 %collective-permute-done.14.refs_2_ = f32[8,1024]{1,0:T(8,128)S(1)} collective-permute-done((f32[8,1024]{1,0:T(8,128)S(1)}, f32[8,1024]{1,0:T(8,128)S(1)}, u32[]{:S(2)}, u32[]{:S(2)}) %collective-permute-start.14) | collective-permute-done | bytes 32800 | tf_op jit(solution)/shard_map/ppermute | solution.py:24
  55.0 0.8 collective-permute-start.15
  55.8 4.1 %collective-permute-start.16 = (f32[8,512]{1,0:T(8,128)S(1)}, f32[8,512]{1,0:T(8,128)S(1)}, u32[]{:S(2)}, u32[]{:S(2)}) collective-permute-start(f32[8,512]{1,0:T(8,128)S(1)} %get-tuple-element.112), channel_id=1, source_target_pairs={{0,28},{1,29},{2,30},{3,31},{4,8},{5,9},{6,10},{7,11},{8,4},{9,5},... | collective-permute-start | bytes 49160 | tf_op jit(solution)/shard_map/ppermute | solution.py:24
  60.0 2.2 %collective-permute-done.16.refs_2_ = f32[8,512]{1,0:T(8,128)S(1)} collective-permute-done((f32[8,512]{1,0:T(8,128)S(1)}, f32[8,512]{1,0:T(8,128)S(1)}, u32[]{:S(2)}, u32[]{:S(2)}) %collective-permute-start.16) | collective-permute-done | bytes 16416 | tf_op jit(solution)/shard_map/ppermute | solution.py:24
  62.2 1.4 %collective-permute-done.17.refs_3_ = f32[8,512]{1,0:T(8,128)S(1)} collective-permute-done((f32[8,512]{1,0:T(8,128)S(1)}, f32[8,512]{1,0:T(8,128)S(1)}, u32[]{:S(2)}, u32[]{:S(2)}) %collective-permute-start.17) | collective-permute-done | bytes 16416 | tf_op jit(solution)/shard_map/ppermute | solution.py:24
  63.7 1.8 %collective-permute-done.18.refs_4_ = f32[8,512]{1,0:T(8,128)S(1)} collective-permute-done((f32[8,512]{1,0:T(8,128)S(1)}, f32[8,512]{1,0:T(8,128)S(1)}, u32[]{:S(2)}, u32[]{:S(2)}) %collective-permute-start.18) | collective-permute-done | bytes 16416 | tf_op jit(solution)/shard_map/ppermute | solution.py:24
  65.5 2.7 %gradients_ahead.1 = (f32[256,256]{1,0:T(8,128)S(1)}, f32[256,256]{1,0:T(8,128)S(1)}, bf16[256,256]{1,0:T(8,128)(2,1)S(1)}, bf16[256,256]{1,0:T(8,128)(2,1)S(1)}...) custom-call(f32[512,768]{1,0:T(8,128)S(1)} %get-tuple-element.79.ref, ...), custom_call_target="tpu_custom_call" | custom-call | tf_op jit(solution)/shard_map/gradients_ahead/pallas_call | solution.py:512
  68.2 0.1 collective-permute-start.20
  68.3 1.0 %collective-permute-start.19 = (bf16[256,256]{1,0:T(8,128)(2,1)S(1)}, bf16[256,256]{1,0:T(8,128)(2,1)S(1)}, u32[]{:S(2)}, u32[]{:S(2)}) collective-permute-start(bf16[256,256]{1,0:T(8,128)(2,1)S(1)} %get-tuple-element.116), channel_id=1, source_target_pairs={{0,2},{1,3},{2,0},{3,1},{4,6},{5,7},{6,4},{7,5},{8,10},{9,11},{10,... | collective-permute-start | bytes 393224 | tf_op jit(solution)/shard_map/ppermute | solution.py:24
  69.3 1.1 %collective-permute-start.22 = (bf16[256,256]{1,0:T(8,128)(2,1)S(1)}, bf16[256,256]{1,0:T(8,128)(2,1)S(1)}, u32[]{:S(2)}, u32[]{:S(2)}) collective-permute-start(bf16[256,256]{1,0:T(8,128)(2,1)S(1)} %get-tuple-element.125), channel_id=1, source_target_pairs={{0,2},{1,3},{2,0},{3,1},{4,6},{5,7},{6,4},{7,5},{8,10},{9,11},{10,... | collective-permute-start | bytes 393224 | tf_op jit(solution)/shard_map/ppermute | solution.py:24
  70.4 0.1 add_convert_fusion
  70.4 3.0 %collective-permute-start.25 = (bf16[256,512]{1,0:T(8,128)(2,1)S(1)}, bf16[256,512]{1,0:T(8,128)(2,1)S(1)}, u32[]{:S(2)}, u32[]{:S(2)}) collective-permute-start(bf16[256,512]{1,0:T(8,128)(2,1)S(1)} %add_convert_fusion), channel_id=1, source_target_pairs={{0,28},{1,29},{2,30},{3,31},{4,0},{5,1},{6,2},{7,3},{8,4},{9,5},{1... | collective-permute-start | bytes 786440 | tf_op jit(solution)/shard_map/ppermute | solution.py:24
  73.5 1.2 %collective-permute-done.19.second = bf16[256,256]{1,0:T(8,128)(2,1)S(1)} collective-permute-done((bf16[256,256]{1,0:T(8,128)(2,1)S(1)}, bf16[256,256]{1,0:T(8,128)(2,1)S(1)}, u32[]{:S(2)}, u32[]{:S(2)}) %collective-permute-start.19) | collective-permute-done | bytes 131104 | tf_op jit(solution)/shard_map/ppermute | solution.py:24
  74.7 0.3 collective-permute-start.21
  74.9 1.5 %gradients_home.1 = (f32[256,512]{1,0:T(8,128)S(1)}, bf16[256,512]{1,0:T(8,128)(2,1)S(1)}, f32[512,256]{1,0:T(8,128)S(1)}, bf16[512,256]{1,0:T(8,128)(2,1)S(1)}) custom-call(f32[512,768]{1,0:T(8,128)S(1)} %get-tuple-element.79.refs_0_, f32[512,768]{1,0:T(8,128)S(1)} %get-tuple-element.80.refs_1_, f32[512,768]{1,0:T(8,128)S(1)} %get-tuple-element.81.refs_2_, ...), custom_call_target="tpu_custom_call" | custom-call | tf_op jit(solution)/shard_map/gradients_home/pallas_call | solution.py:536
  76.4 0.6 collective-permute-done.22.second
  77.0 0.9 %collective-permute-start.26 = (bf16[512,256]{1,0:T(8,128)(2,1)S(1)}, bf16[512,256]{1,0:T(8,128)(2,1)S(1)}, u32[]{:S(2)}, u32[]{:S(2)}) collective-permute-start(bf16[512,256]{1,0:T(8,128)(2,1)S(1)} %get-tuple-element.129), channel_id=1, source_target_pairs={{0,2},{1,3},{2,0},{3,1},{4,6},{5,7},{6,4},{7,5},{8,10},{9,11},{10,... | collective-permute-start | bytes 786440 | tf_op jit(solution)/shard_map/ppermute | solution.py:24
  78.0 0.3 collective-permute-start.23
  78.3 6.6 %collective-permute-done.26.refs_1_ = bf16[512,256]{1,0:T(8,128)(2,1)S(1)} collective-permute-done((bf16[512,256]{1,0:T(8,128)(2,1)S(1)}, bf16[512,256]{1,0:T(8,128)(2,1)S(1)}, u32[]{:S(2)}, u32[]{:S(2)}) %collective-permute-start.26) | collective-permute-done | bytes 262176 | tf_op jit(solution)/shard_map/ppermute | solution.py:24
  84.9 0.9 %finish_image.1 = f32[256,512]{1,0:T(8,128)} custom-call(f32[256,512]{1,0:T(8,128)S(1)} %get-tuple-element.127.refs_0_, bf16[256,512]{1,0:T(8,128)(2,1)S(1)} %collective-permute-done.24.refs_1_, bf16[256,512]{1,0:T(8,128)(2,1)S(1)} %collective-permute-done.25.refs_2_), custom_call_target="tpu_custom_call" | custom-call | flops 3000000000 | bytes 30000000 | tf_op jit(solution)/shard_map/finish_image/pallas_call | solution.py:568
  85.8 1.0 %finish_text.1 = f32[256,512]{1,0:T(8,128)} custom-call(f32[512,256]{1,0:T(8,128)S(1)} %get-tuple-element.132.refs_0_, bf16[512,256]{1,0:T(8,128)(2,1)S(1)} %collective-permute-done.26.refs_1_, bf16[256,256]{1,0:T(8,128)(2,1)S(1)} %collective-permute-done.21.refs_2_, bf16[256,256]{1,0:T(8,128)(2,1)S(1)} %collective-permute-done.23.refs_3_), custom_call_target="tpu_custom_call" | custom-call | tf_op jit(solution)/shard_map/finish_text/pallas_call | solution.py:568
  (31 shorter events, 0.3 us)
Async XLA Ops:
  0.6 35.4 %copy-start = (bf16[256,1280]{1,0:T(8,128)(2,1)S(1)}, bf16[256,1280]{1,0:T(8,128)(2,1)}, u32[]{:S(2)}) copy-start(bf16[256,1280]{1,0:T(8,128)(2,1)} %second.3) | copy-start | bytes 1966084
  0.6 10.4 %collective-permute-start.1 = (bf16[256,1280]{1,0:T(8,128)(2,1)}, bf16[256,1280]{1,0:T(8,128)(2,1)S(1)}, u32[]{:S(2)}, u32[]{:S(2)}) collective-permute-start(bf16[256,1280]{1,0:T(8,128)(2,1)} %second.2), channel_id=1, source_target_pairs={{0,1},{1,0},{2,3},{3,2},{4,5},{5,4},{6,7},{7,6},{8,9},{9,8},{10,11... | collective-permute-start | bytes 1966088 | tf_op jit(solution)/shard_map/ppermute | solution.py:24
  1.2 20.1 %collective-permute-start.6 = (bf16[256,1280]{1,0:T(8,128)(2,1)}, bf16[256,1280]{1,0:T(8,128)(2,1)S(1)}, u32[]{:S(2)}, u32[]{:S(2)}) collective-permute-start(bf16[256,1280]{1,0:T(8,128)(2,1)} %second.3), channel_id=1, source_target_pairs={{0,2},{1,3},{2,0},{3,1},{4,6},{5,7},{6,4},{7,5},{8,10},{9,11},{10,... | collective-permute-start | bytes 1966088 | tf_op jit(solution)/shard_map/ppermute | solution.py:24
  3.7 19.0 %collective-permute-start.4 = (bf16[256,1280]{1,0:T(8,128)(2,1)}, bf16[256,1280]{1,0:T(8,128)(2,1)S(1)}, u32[]{:S(2)}, u32[]{:S(2)}) collective-permute-start(bf16[256,1280]{1,0:T(8,128)(2,1)} %second.3), channel_id=1, source_target_pairs={{0,24},{1,25},{2,26},{3,27},{4,28},{5,29},{6,30},{7,31},{8,0},{9,1... | collective-permute-start | bytes 1966088 | tf_op jit(solution)/shard_map/ppermute | solution.py:24
  7.3 3.8 %collective-permute-start = (bf16[256,512]{1,0:T(8,128)(2,1)}, bf16[256,512]{1,0:T(8,128)(2,1)S(1)}, u32[]{:S(2)}, u32[]{:S(2)}) collective-permute-start(bf16[256,512]{1,0:T(8,128)(2,1)} %first.2), channel_id=1, source_target_pairs={{0,1},{1,0},{2,3},{3,2},{4,5},{5,4},{6,7},{7,6},{8,9},{9,8},{10,11... | collective-permute-start | bytes 786440 | tf_op jit(solution)/shard_map/ppermute | solution.py:24
  7.3 1.1 %copy-start.1 = (bf16[256,1280]{1,0:T(8,128)(2,1)S(1)}, bf16[256,1280]{1,0:T(8,128)(2,1)}, u32[]{:S(2)}) copy-start(bf16[256,1280]{1,0:T(8,128)(2,1)} %second.2) | copy-start | bytes 1966084
  8.4 0.9 %copy-start.2 = (bf16[256,512]{1,0:T(8,128)(2,1)S(1)}, bf16[256,512]{1,0:T(8,128)(2,1)}, u32[]{:S(2)}) copy-start(bf16[256,512]{1,0:T(8,128)(2,1)} %first.2) | copy-start | bytes 786436
  9.4 26.7 %copy-start.3 = (bf16[256,512]{1,0:T(8,128)(2,1)S(1)}, bf16[256,512]{1,0:T(8,128)(2,1)}, u32[]{:S(2)}) copy-start(bf16[256,512]{1,0:T(8,128)(2,1)} %first.3) | copy-start | bytes 786436
  9.5 11.8 %collective-permute-start.2 = (bf16[112,1792]{1,0:T(8,128)(2,1)S(1)}, bf16[112,1792]{1,0:T(8,128)(2,1)S(1)}, u32[]{:S(2)}, u32[]{:S(2)}) collective-permute-start(bf16[112,1792]{1,0:T(8,128)(2,1)S(1)} %get-tuple-element.73), channel_id=1, source_target_pairs={{0,4},{1,5},{2,6},{3,7},{4,0},{5,1},{6,2},{7,3},{8,12},{9,13},{10,... | collective-permute-start | bytes 1204232 | tf_op jit(solution)/shard_map/ppermute | solution.py:24
  11.1 13.8 %collective-permute-start.5 = (bf16[256,512]{1,0:T(8,128)(2,1)}, bf16[256,512]{1,0:T(8,128)(2,1)S(1)}, u32[]{:S(2)}, u32[]{:S(2)}) collective-permute-start(bf16[256,512]{1,0:T(8,128)(2,1)} %first.3), channel_id=1, source_target_pairs={{0,2},{1,3},{2,0},{3,1},{4,6},{5,7},{6,4},{7,5},{8,10},{9,11},{10,... | collective-permute-start | bytes 786440 | tf_op jit(solution)/shard_map/ppermute | solution.py:24
  11.6 16.0 %collective-permute-start.3 = (bf16[256,512]{1,0:T(8,128)(2,1)}, bf16[256,512]{1,0:T(8,128)(2,1)S(1)}, u32[]{:S(2)}, u32[]{:S(2)}) collective-permute-start(bf16[256,512]{1,0:T(8,128)(2,1)} %first.3), channel_id=1, source_target_pairs={{0,24},{1,25},{2,26},{3,27},{4,28},{5,29},{6,30},{7,31},{8,0},{9,1... | collective-permute-start | bytes 786440 | tf_op jit(solution)/shard_map/ppermute | solution.py:24
  27.8 20.0 %collective-permute-start.10 = (bf16[224,1792]{1,0:T(8,128)(2,1)S(1)}, bf16[224,1792]{1,0:T(8,128)(2,1)S(1)}, u32[]{:S(2)}, u32[]{:S(2)}) collective-permute-start(bf16[224,1792]{1,0:T(8,128)(2,1)S(1)} %get-tuple-element.93), channel_id=1, source_target_pairs={{0,2},{1,3},{2,0},{3,1},{4,6},{5,7},{6,4},{7,5},{8,10},{9,11},{10,... | collective-permute-start | bytes 2408456 | tf_op jit(solution)/shard_map/ppermute | solution.py:24
  28.4 17.4 %collective-permute-start.7 = (bf16[144,1792]{1,0:T(8,128)(2,1)S(1)}, bf16[144,1792]{1,0:T(8,128)(2,1)S(1)}, u32[]{:S(2)}, u32[]{:S(2)}) collective-permute-start(bf16[144,1792]{1,0:T(8,128)(2,1)S(1)} %get-tuple-element.83), channel_id=1, source_target_pairs={{0,4},{1,5},{2,6},{3,7},{4,8},{5,9},{6,10},{7,11},{8,12},{9,13},{1... | collective-permute-start | bytes 1548296 | tf_op jit(solution)/shard_map/ppermute | solution.py:24
  29.9 15.6 %collective-permute-start.8 = (bf16[112,1792]{1,0:T(8,128)(2,1)S(1)}, bf16[112,1792]{1,0:T(8,128)(2,1)S(1)}, u32[]{:S(2)}, u32[]{:S(2)}) collective-permute-start(bf16[112,1792]{1,0:T(8,128)(2,1)S(1)} %collective-permute-done.2), channel_id=1, source_target_pairs={{0,8},{1,9},{2,10},{3,11},{4,4},{5,5},{6,6},{7,7},{8,16},{9,17},{1... | collective-permute-start | bytes 1204232 | tf_op jit(solution)/shard_map/ppermute | solution.py:24
  32.1 15.6 %collective-permute-start.9 = (bf16[32,1792]{1,0:T(8,128)(2,1)S(1)}, bf16[32,1792]{1,0:T(8,128)(2,1)S(1)}, u32[]{:S(2)}, u32[]{:S(2)}) collective-permute-start(bf16[32,1792]{1,0:T(8,128)(2,1)S(1)} %get-tuple-element.92), channel_id=1, source_target_pairs={{0,24},{1,25},{2,26},{3,27},{4,28},{5,29},{6,30},{7,31},{8,0},{9,1... | collective-permute-start | bytes 344072 | tf_op jit(solution)/shard_map/ppermute | solution.py:24
  45.8 3.4 %collective-permute-start.12 = (bf16[112,1792]{1,0:T(8,128)(2,1)S(1)}, bf16[112,1792]{1,0:T(8,128)(2,1)S(1)}, u32[]{:S(2)}, u32[]{:S(2)}) collective-permute-start(bf16[112,1792]{1,0:T(8,128)(2,1)S(1)} %collective-permute-done.8.refs_1_.refs_3_.refs_28_), channel_id=1, source_target_pairs={{0,1},{1,0},{2,3},{3,2},{4,5},{5,4},{6,7},{7,6},{8,9},{9,8},{10,11... | collective-permute-start | bytes 1204232 | tf_op jit(solution)/shard_map/ppermute | solution.py:24
  45.8 3.4 %collective-permute-start.11 = (bf16[144,1792]{1,0:T(8,128)(2,1)S(1)}, bf16[144,1792]{1,0:T(8,128)(2,1)S(1)}, u32[]{:S(2)}, u32[]{:S(2)}) collective-permute-start(bf16[144,1792]{1,0:T(8,128)(2,1)S(1)} %collective-permute-done.7.refs_0_.refs_2_.refs_27_), channel_id=1, source_target_pairs={{0,1},{1,0},{2,3},{3,2},{4,5},{5,4},{6,7},{7,6},{8,9},{9,8},{10,11... | collective-permute-start | bytes 1548296 | tf_op jit(solution)/shard_map/ppermute | solution.py:24
  51.0 3.9 %collective-permute-start.14 = (f32[8,1024]{1,0:T(8,128)S(1)}, f32[8,1024]{1,0:T(8,128)S(1)}, u32[]{:S(2)}, u32[]{:S(2)}) collective-permute-start(f32[8,1024]{1,0:T(8,128)S(1)} %get-tuple-element.109.refs_0_), channel_id=1, source_target_pairs={{0,2},{1,3},{2,0},{3,1},{4,6},{5,7},{6,4},{7,5},{8,10},{9,11},{10,... | collective-permute-start | bytes 98312 | tf_op jit(solution)/shard_map/ppermute | solution.py:24
  52.5 2.4 %collective-permute-start.13 = (f32[8,1024]{1,0:T(8,128)S(1)}, f32[8,1024]{1,0:T(8,128)S(1)}, u32[]{:S(2)}, u32[]{:S(2)}) collective-permute-start(f32[8,1024]{1,0:T(8,128)S(1)} %get-tuple-element.109.refs_0_), channel_id=1, source_target_pairs={{0,1},{1,0},{2,3},{3,2},{4,5},{5,4},{6,7},{7,6},{8,9},{9,8},{10,11... | collective-permute-start | bytes 98312 | tf_op jit(solution)/shard_map/ppermute | solution.py:24
  55.0 5.0 %collective-permute-start.15 = (f32[8,512]{1,0:T(8,128)S(1)}, f32[8,512]{1,0:T(8,128)S(1)}, u32[]{:S(2)}, u32[]{:S(2)}) collective-permute-start(f32[8,512]{1,0:T(8,128)S(1)} %get-tuple-element.111), channel_id=1, source_target_pairs={{0,4},{1,5},{2,6},{3,7},{4,0},{5,1},{6,2},{7,3},{8,12},{9,13},{10,... | collective-permute-start | bytes 49160 | tf_op jit(solution)/shard_map/ppermute | solution.py:24
  55.8 6.4 %collective-permute-start.16 = (f32[8,512]{1,0:T(8,128)S(1)}, f32[8,512]{1,0:T(8,128)S(1)}, u32[]{:S(2)}, u32[]{:S(2)}) collective-permute-start(f32[8,512]{1,0:T(8,128)S(1)} %get-tuple-element.112), channel_id=1, source_target_pairs={{0,28},{1,29},{2,30},{3,31},{4,8},{5,9},{6,10},{7,11},{8,4},{9,5},... | collective-permute-start | bytes 49160 | tf_op jit(solution)/shard_map/ppermute | solution.py:24
  59.9 3.7 %collective-permute-start.17 = (f32[8,512]{1,0:T(8,128)S(1)}, f32[8,512]{1,0:T(8,128)S(1)}, u32[]{:S(2)}, u32[]{:S(2)}) collective-permute-start(f32[8,512]{1,0:T(8,128)S(1)} %get-tuple-element.113), channel_id=1, source_target_pairs={{0,8},{1,9},{2,10},{3,11},{4,12},{5,13},{6,14},{7,15},{8,0},{9,1},... | collective-permute-start | bytes 49160 | tf_op jit(solution)/shard_map/ppermute | solution.py:24
  59.9 5.5 %collective-permute-start.18 = (f32[8,512]{1,0:T(8,128)S(1)}, f32[8,512]{1,0:T(8,128)S(1)}, u32[]{:S(2)}, u32[]{:S(2)}) collective-permute-start(f32[8,512]{1,0:T(8,128)S(1)} %get-tuple-element.114), channel_id=1, source_target_pairs={{0,24},{1,25},{2,26},{3,27},{4,28},{5,29},{6,30},{7,31},{8,16},{9,... | collective-permute-start | bytes 49160 | tf_op jit(solution)/shard_map/ppermute | solution.py:24
  68.2 2.2 %collective-permute-start.20 = (bf16[256,512]{1,0:T(8,128)(2,1)S(1)}, bf16[256,512]{1,0:T(8,128)(2,1)S(1)}, u32[]{:S(2)}, u32[]{:S(2)}) collective-permute-start(bf16[256,512]{1,0:T(8,128)(2,1)S(1)} %get-tuple-element.118), channel_id=1, source_target_pairs={{0,1},{1,0},{2,3},{3,2},{4,5},{5,4},{6,7},{7,6},{8,9},{9,8},{10,11... | collective-permute-start | bytes 786440 | tf_op jit(solution)/shard_map/ppermute | solution.py:24
  68.3 6.4 %collective-permute-start.19 = (bf16[256,256]{1,0:T(8,128)(2,1)S(1)}, bf16[256,256]{1,0:T(8,128)(2,1)S(1)}, u32[]{:S(2)}, u32[]{:S(2)}) collective-permute-start(bf16[256,256]{1,0:T(8,128)(2,1)S(1)} %get-tuple-element.116), channel_id=1, source_target_pairs={{0,2},{1,3},{2,0},{3,1},{4,6},{5,7},{6,4},{7,5},{8,10},{9,11},{10,... | collective-permute-start | bytes 393224 | tf_op jit(solution)/shard_map/ppermute | solution.py:24
  69.3 7.7 %collective-permute-start.22 = (bf16[256,256]{1,0:T(8,128)(2,1)S(1)}, bf16[256,256]{1,0:T(8,128)(2,1)S(1)}, u32[]{:S(2)}, u32[]{:S(2)}) collective-permute-start(bf16[256,256]{1,0:T(8,128)(2,1)S(1)} %get-tuple-element.125), channel_id=1, source_target_pairs={{0,2},{1,3},{2,0},{3,1},{4,6},{5,7},{6,4},{7,5},{8,10},{9,11},{10,... | collective-permute-start | bytes 393224 | tf_op jit(solution)/shard_map/ppermute | solution.py:24
  70.4 14.4 %collective-permute-start.25 = (bf16[256,512]{1,0:T(8,128)(2,1)S(1)}, bf16[256,512]{1,0:T(8,128)(2,1)S(1)}, u32[]{:S(2)}, u32[]{:S(2)}) collective-permute-start(bf16[256,512]{1,0:T(8,128)(2,1)S(1)} %add_convert_fusion), channel_id=1, source_target_pairs={{0,28},{1,29},{2,30},{3,31},{4,0},{5,1},{6,2},{7,3},{8,4},{9,5},{1... | collective-permute-start | bytes 786440 | tf_op jit(solution)/shard_map/ppermute | solution.py:24
  74.7 11.1 %collective-permute-start.21 = (bf16[256,256]{1,0:T(8,128)(2,1)S(1)}, bf16[256,256]{1,0:T(8,128)(2,1)S(1)}, u32[]{:S(2)}, u32[]{:S(2)}) collective-permute-start(bf16[256,256]{1,0:T(8,128)(2,1)S(1)} %add_text.2), channel_id=1, source_target_pairs={{0,8},{1,9},{2,10},{3,11},{4,12},{5,13},{6,14},{7,15},{8,16},{9,17... | collective-permute-start | bytes 393224 | tf_op jit(solution)/shard_map/ppermute | solution.py:24
  77.0 7.9 %collective-permute-start.26 = (bf16[512,256]{1,0:T(8,128)(2,1)S(1)}, bf16[512,256]{1,0:T(8,128)(2,1)S(1)}, u32[]{:S(2)}, u32[]{:S(2)}) collective-permute-start(bf16[512,256]{1,0:T(8,128)(2,1)S(1)} %get-tuple-element.129), channel_id=1, source_target_pairs={{0,2},{1,3},{2,0},{3,1},{4,6},{5,7},{6,4},{7,5},{8,10},{9,11},{10,... | collective-permute-start | bytes 786440 | tf_op jit(solution)/shard_map/ppermute | solution.py:24
  77.9 6.9 %collective-permute-start.24 = (bf16[256,512]{1,0:T(8,128)(2,1)S(1)}, bf16[256,512]{1,0:T(8,128)(2,1)S(1)}, u32[]{:S(2)}, u32[]{:S(2)}) collective-permute-start(bf16[256,512]{1,0:T(8,128)(2,1)S(1)} %get-tuple-element.128), channel_id=1, source_target_pairs={{0,1},{1,0},{2,3},{3,2},{4,5},{5,4},{6,7},{7,6},{8,9},{9,8},{10,11... | collective-permute-start | bytes 786440 | tf_op jit(solution)/shard_map/ppermute | solution.py:24
  78.0 7.8 %collective-permute-start.23 = (bf16[256,256]{1,0:T(8,128)(2,1)S(1)}, bf16[256,256]{1,0:T(8,128)(2,1)S(1)}, u32[]{:S(2)}, u32[]{:S(2)}) collective-permute-start(bf16[256,256]{1,0:T(8,128)(2,1)S(1)} %add_text.3), channel_id=1, source_target_pairs={{0,8},{1,9},{2,10},{3,11},{4,12},{5,13},{6,14},{7,15},{8,16},{9,17... | collective-permute-start | bytes 393224 | tf_op jit(solution)/shard_map/ppermute | solution.py:24

commit v6 on v5

--- a/solution.py
+++ b/solution.py
@@ -224,7 +224,7 @@
 def join_blocks_kernel(shard, home_ref, *refs):
     ins, out = refs[:4], refs[4]
     for kind, upward in enumerate(block_parities()):
-        first, second = (rows4(ref, 0) for ref in ins[2 * kind : 2 * kind + 2])
+        first, second = (rows4(ref, 0) for ref in ins[kind::2])
         above = [jnp.where(upward, x, y) for x, y in zip(first, second)]
         below = [jnp.where(upward, y, x) for x, y in zip(first, second)]
         for half in range(2):
@@ -489,10 +489,10 @@
         name="join_group",
     )(partial, to_other_core(partial), to_other_x(partial))
     away = [
-        send_to(part, lambda block, x, core, step=step, first=first: (
+        send_to(away[index], lambda block, x, core, step=step, first=first: (
             block + (step if (block // step) % 2 == first else -step), x, core
         ))
-        for part, step, first in zip(away, (1, 1, 2, 2), (0, 1, 0, 1))
+        for index, step, first in ((0, 1, 0), (2, 2, 0), (1, 1, 1), (3, 2, 1))
     ]
     stats = pl.pallas_call(
         lambda *refs: join_blocks_kernel(shard, *refs),

time: 87 us -> 87 us (level)
  transfers between devices with their start and end apart: 27 -> 27, of which waited for: 13 -> 12; matrix products, arithmetic and copies ran while one was open for 0% -> 0% of each run, Pallas kernels for 9% -> 9%
where the time goes in v6:
time: 87 us; the launch traced here: 86.8 us
  waiting for transfers between devices  39.4 us (45%)
  starting transfers between devices  30.7 us (35%)
  Pallas kernels  13.8 us (16%)
  local copies, waits for them, and re-layouts  2.04 us (2%)
    ppermute x27, waiting for transfers between devices, send_to(): return lax.ppermute(value, AXES, pairs)  39.4 us
    ppermute x27, starting transfers between devices, send_to(): return lax.ppermute(value, AXES, pairs)  30.7 us
    pallas_call x3, Pallas kernels, part_scores(): pl.pallas_call(lambda *refs: part_kernel(shard, scales, spans, sizes, cou...  5.33 us
    pallas_call x1, Pallas kernels, on_device(): pl.pallas_call(lambda *refs: ahead_kernel(shard, spans[0], *refs), out_sh...  2.68 us
    unnamed x8, local copies, waits for them, and re-layouts  2.04 us
    pallas_call x2, Pallas kernels, finish(): pl.pallas_call(lambda *refs: kernel(scale_s, *refs), out_shape=wide, in_s...  1.9 us
    pallas_call x1, Pallas kernels, on_device(): pl.pallas_call(lambda *refs: far_kernel(shard, scales, spans, *refs), out...  1.84 us
  transfers between devices with their start and end apart: 27, of which 12 were waited for; matrix products, arithmetic and copies ran while one was open for 0% of the time, Pallas kernels for 9%

profile of v6, /device:TPU:0, one launch (start us, length us, event | category | flops | bytes accessed | tf_op | source)
XLA Modules:
  0.0 86.8 jit_solution(5044455190463182542)
XLA Ops:
  0.6 0.5 collective-permute-start.1
  1.2 2.6 %collective-permute-start.6 = (bf16[256,1280]{1,0:T(8,128)(2,1)}, bf16[256,1280]{1,0:T(8,128)(2,1)S(1)}, u32[]{:S(2)}, u32[]{:S(2)}) collective-permute-start(bf16[256,1280]{1,0:T(8,128)(2,1)} %second.3), channel_id=1, source_target_pairs={{0,2},{1,3},{2,0},{3,1},{4,6},{5,7},{6,4},{7,5},{8,10},{9,11},{10,... | collective-permute-start | bytes 1966088 | tf_op jit(solution)/shard_map/ppermute | solution.py:24
  3.7 3.6 %collective-permute-start.4 = (bf16[256,1280]{1,0:T(8,128)(2,1)}, bf16[256,1280]{1,0:T(8,128)(2,1)S(1)}, u32[]{:S(2)}, u32[]{:S(2)}) collective-permute-start(bf16[256,1280]{1,0:T(8,128)(2,1)} %second.3), channel_id=1, source_target_pairs={{0,24},{1,25},{2,26},{3,27},{4,28},{5,29},{6,30},{7,31},{8,0},{9,1... | collective-permute-start | bytes 1966088 | tf_op jit(solution)/shard_map/ppermute | solution.py:24
  7.3 1.1 %copy-done.1 = bf16[256,1280]{1,0:T(8,128)(2,1)S(1)} copy-done((bf16[256,1280]{1,0:T(8,128)(2,1)S(1)}, bf16[256,1280]{1,0:T(8,128)(2,1)}, u32[]{:S(2)}) %copy-start.1) | copy-done | bytes 655384
  8.4 0.9 %copy-done.2 = bf16[256,512]{1,0:T(8,128)(2,1)S(1)} copy-done((bf16[256,512]{1,0:T(8,128)(2,1)S(1)}, bf16[256,512]{1,0:T(8,128)(2,1)}, u32[]{:S(2)}) %copy-start.2) | copy-done | bytes 262168
  9.4 0.1 pack_images.1
  9.5 1.6 %collective-permute-start.2 = (bf16[112,1792]{1,0:T(8,128)(2,1)S(1)}, bf16[112,1792]{1,0:T(8,128)(2,1)S(1)}, u32[]{:S(2)}, u32[]{:S(2)}) collective-permute-start(bf16[112,1792]{1,0:T(8,128)(2,1)S(1)} %get-tuple-element.73), channel_id=1, source_target_pairs={{0,4},{1,5},{2,6},{3,7},{4,0},{5,1},{6,2},{7,3},{8,12},{9,13},{10,... | collective-permute-start | bytes 1204232 | tf_op jit(solution)/shard_map/ppermute | solution.py:24
  11.1 0.5 collective-permute-start.5
  11.6 0.4 collective-permute-start.3
  12.1 9.2 %collective-permute-done.2 = bf16[112,1792]{1,0:T(8,128)(2,1)S(1)} collective-permute-done((bf16[112,1792]{1,0:T(8,128)(2,1)S(1)}, bf16[112,1792]{1,0:T(8,128)(2,1)S(1)}, u32[]{:S(2)}, u32[]{:S(2)}) %collective-permute-start.2) | collective-permute-done | bytes 401440 | tf_op jit(solution)/shard_map/ppermute | solution.py:24
  21.3 1.5 %collective-permute-done.4.t_ahead = bf16[256,1280]{1,0:T(8,128)(2,1)S(1)} collective-permute-done((bf16[256,1280]{1,0:T(8,128)(2,1)}, bf16[256,1280]{1,0:T(8,128)(2,1)S(1)}, u32[]{:S(2)}, u32[]{:S(2)}) %collective-permute-start.4) | collective-permute-done | bytes 655392 | tf_op jit(solution)/shard_map/ppermute | solution.py:24
  22.7 2.1 %collective-permute-done.5.s_x = bf16[256,512]{1,0:T(8,128)(2,1)S(1)} collective-permute-done((bf16[256,512]{1,0:T(8,128)(2,1)}, bf16[256,512]{1,0:T(8,128)(2,1)S(1)}, u32[]{:S(2)}, u32[]{:S(2)}) %collective-permute-start.5) | collective-permute-done | bytes 262176 | tf_op jit(solution)/shard_map/ppermute | solution.py:24
  24.9 2.7 %collective-permute-done.3.s_ahead = bf16[256,512]{1,0:T(8,128)(2,1)S(1)} collective-permute-done((bf16[256,512]{1,0:T(8,128)(2,1)}, bf16[256,512]{1,0:T(8,128)(2,1)S(1)}, u32[]{:S(2)}, u32[]{:S(2)}) %collective-permute-start.3) | collective-permute-done | bytes 262176 | tf_op jit(solution)/shard_map/ppermute | solution.py:24
  27.6 0.2 pack_arrived.1
  27.8 0.6 collective-permute-start.10
  28.4 1.5 %collective-permute-start.7 = (bf16[144,1792]{1,0:T(8,128)(2,1)S(1)}, bf16[144,1792]{1,0:T(8,128)(2,1)S(1)}, u32[]{:S(2)}, u32[]{:S(2)}) collective-permute-start(bf16[144,1792]{1,0:T(8,128)(2,1)S(1)} %get-tuple-element.83), channel_id=1, source_target_pairs={{0,4},{1,5},{2,6},{3,7},{4,8},{5,9},{6,10},{7,11},{8,12},{9,13},{1... | collective-permute-start | bytes 1548296 | tf_op jit(solution)/shard_map/ppermute | solution.py:24
  29.9 2.2 %collective-permute-start.8 = (bf16[112,1792]{1,0:T(8,128)(2,1)S(1)}, bf16[112,1792]{1,0:T(8,128)(2,1)S(1)}, u32[]{:S(2)}, u32[]{:S(2)}) collective-permute-start(bf16[112,1792]{1,0:T(8,128)(2,1)S(1)} %collective-permute-done.2), channel_id=1, source_target_pairs={{0,8},{1,9},{2,10},{3,11},{4,4},{5,5},{6,6},{7,7},{8,16},{9,17},{1... | collective-permute-start | bytes 1204232 | tf_op jit(solution)/shard_map/ppermute | solution.py:24
  32.1 3.9 %collective-permute-start.9 = (bf16[32,1792]{1,0:T(8,128)(2,1)S(1)}, bf16[32,1792]{1,0:T(8,128)(2,1)S(1)}, u32[]{:S(2)}, u32[]{:S(2)}) collective-permute-start(bf16[32,1792]{1,0:T(8,128)(2,1)S(1)} %get-tuple-element.92), channel_id=1, source_target_pairs={{0,24},{1,25},{2,26},{3,27},{4,28},{5,29},{6,30},{7,31},{8,0},{9,1... | collective-permute-start | bytes 344072 | tf_op jit(solution)/shard_map/ppermute | solution.py:24
  36.0 0.1 pack_own.1.refs_2_.refs_31_.refs_9_
  36.1 0.1 pack_core.1.refs_1_.refs_26_.refs_8_
  36.2 2.5 %scores_home.1 = (f32[512,768]{1,0:T(8,128)S(1)}, f32[512,768]{1,0:T(8,128)S(1)}, f32[512,768]{1,0:T(8,128)S(1)}, f32[512,768]{1,0:T(8,128)S(1)}, f32[8,512]{1,0:T(8,128)S(1)}, /*index=5*/f32[8,768]{1,0:T(8,128)S(1)}) custom-call(bf16[256,1792]{1,0:T(8,128)(2,1)S(1)} %get-tuple-element.69.refs_0_.refs_25_.refs_7_, ...), custom_call_target="tpu_custom_call" | custom-call | tf_op jit(solution)/shard_map/scores_home/pallas_call | solution.py:448
  38.6 6.9 %collective-permute-done.8.refs_1_.refs_3_.refs_28_ = bf16[112,1792]{1,0:T(8,128)(2,1)S(1)} collective-permute-done((bf16[112,1792]{1,0:T(8,128)(2,1)S(1)}, bf16[112,1792]{1,0:T(8,128)(2,1)S(1)}, u32[]{:S(2)}, u32[]{:S(2)}) %collective-permute-start.8) | collective-permute-done | bytes 401440 | tf_op jit(solution)/shard_map/ppermute | solution.py:24
  45.5 0.3 collective-permute-done.7.refs_0_.refs_2_.refs_27_
  45.8 0.5 collective-permute-start.11
  46.3 1.5 %scores_near.1 = (f32[256,768]{1,0:T(8,128)S(1)}, f32[256,768]{1,0:T(8,128)S(1)}, f32[256,768]{1,0:T(8,128)S(1)}, f32[256,768]{1,0:T(8,128)S(1)}, f32[8,256]{1,0:T(8,128)S(1)}, /*index=5*/f32[4,768]{1,0:T(4,128)S(1)}) custom-call(bf16[144,1792]{1,0:T(8,128)(2,1)S(1)} %collective-permute-done.7.refs_0_.refs_2_.refs_27_, ...), custom_call_target="tpu_custom_call" | custom-call | tf_op jit(solution)/shard_map/scores_near/pallas_call | solution.py:448
  47.8 1.4 %scores_side.1 = (f32[768,256]{1,0:T(8,128)S(1)}, f32[768,256]{1,0:T(8,128)S(1)}, f32[768,256]{1,0:T(8,128)S(1)}, f32[768,256]{1,0:T(8,128)S(1)}, f32[8,768]{1,0:T(8,128)S(1)}, /*index=5*/f32[12,256]{1,0:T(8,128)S(1)}) custom-call(bf16[256,1792]{1,0:T(8,128)(2,1)S(1)} %get-tuple-element.69.refs_0_.refs_25_.refs_7_, ...), custom_call_target="tpu_custom_call" | custom-call | flops 99999997952 | bytes 1000000000 | tf_op jit(solution)/shard_map/scores_side/pallas_call | solution.py:448
  49.2 1.8 %scores_far.1 = (f32[256,1024]{1,0:T(8,128)S(1)}, f32[256,1024]{1,0:T(8,128)S(1)}, f32[256,1024]{1,0:T(8,128)S(1)}, f32[256,1024]{1,0:T(8,128)S(1)}, f32[8,256]{...) custom-call(bf16[144,1792]{1,0:T(8,128)(2,1)S(1)} %collective-permute-done.11.refs_0_.refs_29_, ...), custom_call_target="tpu_custom_call" | custom-call | tf_op jit(solution)/shard_map/scores_far/pallas_call | solution.py:470
  51.0 1.5 %collective-permute-start.14 = (f32[8,1024]{1,0:T(8,128)S(1)}, f32[8,1024]{1,0:T(8,128)S(1)}, u32[]{:S(2)}, u32[]{:S(2)}) collective-permute-start(f32[8,1024]{1,0:T(8,128)S(1)} %get-tuple-element.109.refs_0_), channel_id=1, source_target_pairs={{0,2},{1,3},{2,0},{3,1},{4,6},{5,7},{6,4},{7,5},{8,10},{9,11},{10,... | collective-permute-start | bytes 98312 | tf_op jit(solution)/shard_map/ppermute | solution.py:24
  52.5 2.4 %collective-permute-done.14.refs_2_ = f32[8,1024]{1,0:T(8,128)S(1)} collective-permute-done((f32[8,1024]{1,0:T(8,128)S(1)}, f32[8,1024]{1,0:T(8,128)S(1)}, u32[]{:S(2)}, u32[]{:S(2)}) %collective-permute-start.14) | collective-permute-done | bytes 32800 | tf_op jit(solution)/shard_map/ppermute | solution.py:24
  55.0 0.8 collective-permute-start.15
  55.8 0.4 collective-permute-start.16
  56.2 3.8 %collective-permute-start.17 = (f32[8,512]{1,0:T(8,128)S(1)}, f32[8,512]{1,0:T(8,128)S(1)}, u32[]{:S(2)}, u32[]{:S(2)}) collective-permute-start(f32[8,512]{1,0:T(8,128)S(1)} %get-tuple-element.113), channel_id=1, source_target_pairs={{0,28},{1,29},{2,30},{3,31},{4,8},{5,9},{6,10},{7,11},{8,4},{9,5},... | collective-permute-start | bytes 49160 | tf_op jit(solution)/shard_map/ppermute | solution.py:24
  59.9 2.0 %collective-permute-start.18 = (f32[8,512]{1,0:T(8,128)S(1)}, f32[8,512]{1,0:T(8,128)S(1)}, u32[]{:S(2)}, u32[]{:S(2)}) collective-permute-start(f32[8,512]{1,0:T(8,128)S(1)} %get-tuple-element.114), channel_id=1, source_target_pairs={{0,24},{1,25},{2,26},{3,27},{4,28},{5,29},{6,30},{7,31},{8,16},{9,... | collective-permute-start | bytes 49160 | tf_op jit(solution)/shard_map/ppermute | solution.py:24
  61.9 0.6 collective-permute-done.17.refs_3_
  62.6 2.9 %collective-permute-done.18.refs_4_ = f32[8,512]{1,0:T(8,128)S(1)} collective-permute-done((f32[8,512]{1,0:T(8,128)S(1)}, f32[8,512]{1,0:T(8,128)S(1)}, u32[]{:S(2)}, u32[]{:S(2)}) %collective-permute-start.18) | collective-permute-done | bytes 16416 | tf_op jit(solution)/shard_map/ppermute | solution.py:24
  65.5 2.7 %gradients_ahead.1 = (f32[256,256]{1,0:T(8,128)S(1)}, f32[256,256]{1,0:T(8,128)S(1)}, bf16[256,256]{1,0:T(8,128)(2,1)S(1)}, bf16[256,256]{1,0:T(8,128)(2,1)S(1)}...) custom-call(f32[512,768]{1,0:T(8,128)S(1)} %get-tuple-element.79.ref, ...), custom_call_target="tpu_custom_call" | custom-call | tf_op jit(solution)/shard_map/gradients_ahead/pallas_call | solution.py:512
  68.2 0.1 collective-permute-start.20
  68.3 1.0 %collective-permute-start.19 = (bf16[256,256]{1,0:T(8,128)(2,1)S(1)}, bf16[256,256]{1,0:T(8,128)(2,1)S(1)}, u32[]{:S(2)}, u32[]{:S(2)}) collective-permute-start(bf16[256,256]{1,0:T(8,128)(2,1)S(1)} %get-tuple-element.116), channel_id=1, source_target_pairs={{0,2},{1,3},{2,0},{3,1},{4,6},{5,7},{6,4},{7,5},{8,10},{9,11},{10,... | collective-permute-start | bytes 393224 | tf_op jit(solution)/shard_map/ppermute | solution.py:24
  69.3 1.1 %collective-permute-start.22 = (bf16[256,256]{1,0:T(8,128)(2,1)S(1)}, bf16[256,256]{1,0:T(8,128)(2,1)S(1)}, u32[]{:S(2)}, u32[]{:S(2)}) collective-permute-start(bf16[256,256]{1,0:T(8,128)(2,1)S(1)} %get-tuple-element.125), channel_id=1, source_target_pairs={{0,2},{1,3},{2,0},{3,1},{4,6},{5,7},{6,4},{7,5},{8,10},{9,11},{10,... | collective-permute-start | bytes 393224 | tf_op jit(solution)/shard_map/ppermute | solution.py:24
  70.4 0.1 add_convert_fusion
  70.4 1.0 %collective-permute-start.25 = (bf16[256,512]{1,0:T(8,128)(2,1)S(1)}, bf16[256,512]{1,0:T(8,128)(2,1)S(1)}, u32[]{:S(2)}, u32[]{:S(2)}) collective-permute-start(bf16[256,512]{1,0:T(8,128)(2,1)S(1)} %add_convert_fusion), channel_id=1, source_target_pairs={{0,28},{1,29},{2,30},{3,31},{4,0},{5,1},{6,2},{7,3},{8,4},{9,5},{1... | collective-permute-start | bytes 786440 | tf_op jit(solution)/shard_map/ppermute | solution.py:24
  71.5 3.2 %collective-permute-done.19.second = bf16[256,256]{1,0:T(8,128)(2,1)S(1)} collective-permute-done((bf16[256,256]{1,0:T(8,128)(2,1)S(1)}, bf16[256,256]{1,0:T(8,128)(2,1)S(1)}, u32[]{:S(2)}, u32[]{:S(2)}) %collective-permute-start.19) | collective-permute-done | bytes 131104 | tf_op jit(solution)/shard_map/ppermute | solution.py:24
  74.7 1.5 %gradients_home.1 = (f32[256,512]{1,0:T(8,128)S(1)}, bf16[256,512]{1,0:T(8,128)(2,1)S(1)}, f32[512,256]{1,0:T(8,128)S(1)}, bf16[512,256]{1,0:T(8,128)(2,1)S(1)}) custom-call(f32[512,768]{1,0:T(8,128)S(1)} %get-tuple-element.79.refs_0_, f32[512,768]{1,0:T(8,128)S(1)} %get-tuple-element.80.refs_1_, f32[512,768]{1,0:T(8,128)S(1)} %get-tuple-element.81.refs_2_, ...), custom_call_target="tpu_custom_call" | custom-call | tf_op jit(solution)/shard_map/gradients_home/pallas_call | solution.py:536
  76.2 0.8 collective-permute-done.22.second
  77.0 0.9 %collective-permute-start.26 = (bf16[512,256]{1,0:T(8,128)(2,1)S(1)}, bf16[512,256]{1,0:T(8,128)(2,1)S(1)}, u32[]{:S(2)}, u32[]{:S(2)}) collective-permute-start(bf16[512,256]{1,0:T(8,128)(2,1)S(1)} %get-tuple-element.129), channel_id=1, source_target_pairs={{0,2},{1,3},{2,0},{3,1},{4,6},{5,7},{6,4},{7,5},{8,10},{9,11},{10,... | collective-permute-start | bytes 786440 | tf_op jit(solution)/shard_map/ppermute | solution.py:24
  78.0 6.8 %collective-permute-done.26.refs_1_ = bf16[512,256]{1,0:T(8,128)(2,1)S(1)} collective-permute-done((bf16[512,256]{1,0:T(8,128)(2,1)S(1)}, bf16[512,256]{1,0:T(8,128)(2,1)S(1)}, u32[]{:S(2)}, u32[]{:S(2)}) %collective-permute-start.26) | collective-permute-done | bytes 262176 | tf_op jit(solution)/shard_map/ppermute | solution.py:24
  84.9 0.9 %finish_image.1 = f32[256,512]{1,0:T(8,128)} custom-call(f32[256,512]{1,0:T(8,128)S(1)} %get-tuple-element.127.refs_0_, bf16[256,512]{1,0:T(8,128)(2,1)S(1)} %collective-permute-done.24.refs_1_, bf16[256,512]{1,0:T(8,128)(2,1)S(1)} %collective-permute-done.25.refs_2_), custom_call_target="tpu_custom_call" | custom-call | flops 3000000000 | bytes 30000000 | tf_op jit(solution)/shard_map/finish_image/pallas_call | solution.py:568
  85.8 1.0 %finish_text.1 = f32[256,512]{1,0:T(8,128)} custom-call(f32[512,256]{1,0:T(8,128)S(1)} %get-tuple-element.132.refs_0_, bf16[512,256]{1,0:T(8,128)(2,1)S(1)} %collective-permute-done.26.refs_1_, bf16[256,256]{1,0:T(8,128)(2,1)S(1)} %collective-permute-done.21.refs_2_, bf16[256,256]{1,0:T(8,128)(2,1)S(1)} %collective-permute-done.23.refs_3_), custom_call_target="tpu_custom_call" | custom-call | tf_op jit(solution)/shard_map/finish_text/pallas_call | solution.py:568
  (31 shorter events, 0.3 us)
Async XLA Ops:
  0.6 35.4 %copy-start = (bf16[256,1280]{1,0:T(8,128)(2,1)S(1)}, bf16[256,1280]{1,0:T(8,128)(2,1)}, u32[]{:S(2)}) copy-start(bf16[256,1280]{1,0:T(8,128)(2,1)} %second.3) | copy-start | bytes 1966084
  0.6 10.4 %collective-permute-start.1 = (bf16[256,1280]{1,0:T(8,128)(2,1)}, bf16[256,1280]{1,0:T(8,128)(2,1)S(1)}, u32[]{:S(2)}, u32[]{:S(2)}) collective-permute-start(bf16[256,1280]{1,0:T(8,128)(2,1)} %second.2), channel_id=1, source_target_pairs={{0,1},{1,0},{2,3},{3,2},{4,5},{5,4},{6,7},{7,6},{8,9},{9,8},{10,11... | collective-permute-start | bytes 1966088 | tf_op jit(solution)/shard_map/ppermute | solution.py:24
  1.2 20.1 %collective-permute-start.6 = (bf16[256,1280]{1,0:T(8,128)(2,1)}, bf16[256,1280]{1,0:T(8,128)(2,1)S(1)}, u32[]{:S(2)}, u32[]{:S(2)}) collective-permute-start(bf16[256,1280]{1,0:T(8,128)(2,1)} %second.3), channel_id=1, source_target_pairs={{0,2},{1,3},{2,0},{3,1},{4,6},{5,7},{6,4},{7,5},{8,10},{9,11},{10,... | collective-permute-start | bytes 1966088 | tf_op jit(solution)/shard_map/ppermute | solution.py:24
  3.7 19.0 %collective-permute-start.4 = (bf16[256,1280]{1,0:T(8,128)(2,1)}, bf16[256,1280]{1,0:T(8,128)(2,1)S(1)}, u32[]{:S(2)}, u32[]{:S(2)}) collective-permute-start(bf16[256,1280]{1,0:T(8,128)(2,1)} %second.3), channel_id=1, source_target_pairs={{0,24},{1,25},{2,26},{3,27},{4,28},{5,29},{6,30},{7,31},{8,0},{9,1... | collective-permute-start | bytes 1966088 | tf_op jit(solution)/shard_map/ppermute | solution.py:24
  7.3 3.8 %collective-permute-start = (bf16[256,512]{1,0:T(8,128)(2,1)}, bf16[256,512]{1,0:T(8,128)(2,1)S(1)}, u32[]{:S(2)}, u32[]{:S(2)}) collective-permute-start(bf16[256,512]{1,0:T(8,128)(2,1)} %first.2), channel_id=1, source_target_pairs={{0,1},{1,0},{2,3},{3,2},{4,5},{5,4},{6,7},{7,6},{8,9},{9,8},{10,11... | collective-permute-start | bytes 786440 | tf_op jit(solution)/shard_map/ppermute | solution.py:24
  7.3 1.1 %copy-start.1 = (bf16[256,1280]{1,0:T(8,128)(2,1)S(1)}, bf16[256,1280]{1,0:T(8,128)(2,1)}, u32[]{:S(2)}) copy-start(bf16[256,1280]{1,0:T(8,128)(2,1)} %second.2) | copy-start | bytes 1966084
  8.4 0.9 %copy-start.2 = (bf16[256,512]{1,0:T(8,128)(2,1)S(1)}, bf16[256,512]{1,0:T(8,128)(2,1)}, u32[]{:S(2)}) copy-start(bf16[256,512]{1,0:T(8,128)(2,1)} %first.2) | copy-start | bytes 786436
  9.4 26.7 %copy-start.3 = (bf16[256,512]{1,0:T(8,128)(2,1)S(1)}, bf16[256,512]{1,0:T(8,128)(2,1)}, u32[]{:S(2)}) copy-start(bf16[256,512]{1,0:T(8,128)(2,1)} %first.3) | copy-start | bytes 786436
  9.5 11.8 %collective-permute-start.2 = (bf16[112,1792]{1,0:T(8,128)(2,1)S(1)}, bf16[112,1792]{1,0:T(8,128)(2,1)S(1)}, u32[]{:S(2)}, u32[]{:S(2)}) collective-permute-start(bf16[112,1792]{1,0:T(8,128)(2,1)S(1)} %get-tuple-element.73), channel_id=1, source_target_pairs={{0,4},{1,5},{2,6},{3,7},{4,0},{5,1},{6,2},{7,3},{8,12},{9,13},{10,... | collective-permute-start | bytes 1204232 | tf_op jit(solution)/shard_map/ppermute | solution.py:24
  11.1 13.8 %collective-permute-start.5 = (bf16[256,512]{1,0:T(8,128)(2,1)}, bf16[256,512]{1,0:T(8,128)(2,1)S(1)}, u32[]{:S(2)}, u32[]{:S(2)}) collective-permute-start(bf16[256,512]{1,0:T(8,128)(2,1)} %first.3), channel_id=1, source_target_pairs={{0,2},{1,3},{2,0},{3,1},{4,6},{5,7},{6,4},{7,5},{8,10},{9,11},{10,... | collective-permute-start | bytes 786440 | tf_op jit(solution)/shard_map/ppermute | solution.py:24
  11.6 16.0 %collective-permute-start.3 = (bf16[256,512]{1,0:T(8,128)(2,1)}, bf16[256,512]{1,0:T(8,128)(2,1)S(1)}, u32[]{:S(2)}, u32[]{:S(2)}) collective-permute-start(bf16[256,512]{1,0:T(8,128)(2,1)} %first.3), channel_id=1, source_target_pairs={{0,24},{1,25},{2,26},{3,27},{4,28},{5,29},{6,30},{7,31},{8,0},{9,1... | collective-permute-start | bytes 786440 | tf_op jit(solution)/shard_map/ppermute | solution.py:24
  27.8 20.0 %collective-permute-start.10 = (bf16[224,1792]{1,0:T(8,128)(2,1)S(1)}, bf16[224,1792]{1,0:T(8,128)(2,1)S(1)}, u32[]{:S(2)}, u32[]{:S(2)}) collective-permute-start(bf16[224,1792]{1,0:T(8,128)(2,1)S(1)} %get-tuple-element.93), channel_id=1, source_target_pairs={{0,2},{1,3},{2,0},{3,1},{4,6},{5,7},{6,4},{7,5},{8,10},{9,11},{10,... | collective-permute-start | bytes 2408456 | tf_op jit(solution)/shard_map/ppermute | solution.py:24
  28.4 17.4 %collective-permute-start.7 = (bf16[144,1792]{1,0:T(8,128)(2,1)S(1)}, bf16[144,1792]{1,0:T(8,128)(2,1)S(1)}, u32[]{:S(2)}, u32[]{:S(2)}) collective-permute-start(bf16[144,1792]{1,0:T(8,128)(2,1)S(1)} %get-tuple-element.83), channel_id=1, source_target_pairs={{0,4},{1,5},{2,6},{3,7},{4,8},{5,9},{6,10},{7,11},{8,12},{9,13},{1... | collective-permute-start | bytes 1548296 | tf_op jit(solution)/shard_map/ppermute | solution.py:24
  29.9 15.6 %collective-permute-start.8 = (bf16[112,1792]{1,0:T(8,128)(2,1)S(1)}, bf16[112,1792]{1,0:T(8,128)(2,1)S(1)}, u32[]{:S(2)}, u32[]{:S(2)}) collective-permute-start(bf16[112,1792]{1,0:T(8,128)(2,1)S(1)} %collective-permute-done.2), channel_id=1, source_target_pairs={{0,8},{1,9},{2,10},{3,11},{4,4},{5,5},{6,6},{7,7},{8,16},{9,17},{1... | collective-permute-start | bytes 1204232 | tf_op jit(solution)/shard_map/ppermute | solution.py:24
  32.1 15.6 %collective-permute-start.9 = (bf16[32,1792]{1,0:T(8,128)(2,1)S(1)}, bf16[32,1792]{1,0:T(8,128)(2,1)S(1)}, u32[]{:S(2)}, u32[]{:S(2)}) collective-permute-start(bf16[32,1792]{1,0:T(8,128)(2,1)S(1)} %get-tuple-element.92), channel_id=1, source_target_pairs={{0,24},{1,25},{2,26},{3,27},{4,28},{5,29},{6,30},{7,31},{8,0},{9,1... | collective-permute-start | bytes 344072 | tf_op jit(solution)/shard_map/ppermute | solution.py:24
  45.8 3.4 %collective-permute-start.12 = (bf16[112,1792]{1,0:T(8,128)(2,1)S(1)}, bf16[112,1792]{1,0:T(8,128)(2,1)S(1)}, u32[]{:S(2)}, u32[]{:S(2)}) collective-permute-start(bf16[112,1792]{1,0:T(8,128)(2,1)S(1)} %collective-permute-done.8.refs_1_.refs_3_.refs_28_), channel_id=1, source_target_pairs={{0,1},{1,0},{2,3},{3,2},{4,5},{5,4},{6,7},{7,6},{8,9},{9,8},{10,11... | collective-permute-start | bytes 1204232 | tf_op jit(solution)/shard_map/ppermute | solution.py:24
  45.8 3.4 %collective-permute-start.11 = (bf16[144,1792]{1,0:T(8,128)(2,1)S(1)}, bf16[144,1792]{1,0:T(8,128)(2,1)S(1)}, u32[]{:S(2)}, u32[]{:S(2)}) collective-permute-start(bf16[144,1792]{1,0:T(8,128)(2,1)S(1)} %collective-permute-done.7.refs_0_.refs_2_.refs_27_), channel_id=1, source_target_pairs={{0,1},{1,0},{2,3},{3,2},{4,5},{5,4},{6,7},{7,6},{8,9},{9,8},{10,11... | collective-permute-start | bytes 1548296 | tf_op jit(solution)/shard_map/ppermute | solution.py:24
  51.0 3.9 %collective-permute-start.14 = (f32[8,1024]{1,0:T(8,128)S(1)}, f32[8,1024]{1,0:T(8,128)S(1)}, u32[]{:S(2)}, u32[]{:S(2)}) collective-permute-start(f32[8,1024]{1,0:T(8,128)S(1)} %get-tuple-element.109.refs_0_), channel_id=1, source_target_pairs={{0,2},{1,3},{2,0},{3,1},{4,6},{5,7},{6,4},{7,5},{8,10},{9,11},{10,... | collective-permute-start | bytes 98312 | tf_op jit(solution)/shard_map/ppermute | solution.py:24
  52.5 2.4 %collective-permute-start.13 = (f32[8,1024]{1,0:T(8,128)S(1)}, f32[8,1024]{1,0:T(8,128)S(1)}, u32[]{:S(2)}, u32[]{:S(2)}) collective-permute-start(f32[8,1024]{1,0:T(8,128)S(1)} %get-tuple-element.109.refs_0_), channel_id=1, source_target_pairs={{0,1},{1,0},{2,3},{3,2},{4,5},{5,4},{6,7},{7,6},{8,9},{9,8},{10,11... | collective-permute-start | bytes 98312 | tf_op jit(solution)/shard_map/ppermute | solution.py:24
  55.0 6.9 %collective-permute-start.15 = (f32[8,512]{1,0:T(8,128)S(1)}, f32[8,512]{1,0:T(8,128)S(1)}, u32[]{:S(2)}, u32[]{:S(2)}) collective-permute-start(f32[8,512]{1,0:T(8,128)S(1)} %get-tuple-element.111), channel_id=1, source_target_pairs={{0,4},{1,5},{2,6},{3,7},{4,0},{5,1},{6,2},{7,3},{8,12},{9,13},{10,... | collective-permute-start | bytes 49160 | tf_op jit(solution)/shard_map/ppermute | solution.py:24
  55.8 6.2 %collective-permute-start.16 = (f32[8,512]{1,0:T(8,128)S(1)}, f32[8,512]{1,0:T(8,128)S(1)}, u32[]{:S(2)}, u32[]{:S(2)}) collective-permute-start(f32[8,512]{1,0:T(8,128)S(1)} %get-tuple-element.112), channel_id=1, source_target_pairs={{0,8},{1,9},{2,10},{3,11},{4,12},{5,13},{6,14},{7,15},{8,0},{9,1},... | collective-permute-start | bytes 49160 | tf_op jit(solution)/shard_map/ppermute | solution.py:24
  56.2 6.4 %collective-permute-start.17 = (f32[8,512]{1,0:T(8,128)S(1)}, f32[8,512]{1,0:T(8,128)S(1)}, u32[]{:S(2)}, u32[]{:S(2)}) collective-permute-start(f32[8,512]{1,0:T(8,128)S(1)} %get-tuple-element.113), channel_id=1, source_target_pairs={{0,28},{1,29},{2,30},{3,31},{4,8},{5,9},{6,10},{7,11},{8,4},{9,5},... | collective-permute-start | bytes 49160 | tf_op jit(solution)/shard_map/ppermute | solution.py:24
  59.9 5.5 %collective-permute-start.18 = (f32[8,512]{1,0:T(8,128)S(1)}, f32[8,512]{1,0:T(8,128)S(1)}, u32[]{:S(2)}, u32[]{:S(2)}) collective-permute-start(f32[8,512]{1,0:T(8,128)S(1)} %get-tuple-element.114), channel_id=1, source_target_pairs={{0,24},{1,25},{2,26},{3,27},{4,28},{5,29},{6,30},{7,31},{8,16},{9,... | collective-permute-start | bytes 49160 | tf_op jit(solution)/shard_map/ppermute | solution.py:24
  68.2 2.2 %collective-permute-start.20 = (bf16[256,512]{1,0:T(8,128)(2,1)S(1)}, bf16[256,512]{1,0:T(8,128)(2,1)S(1)}, u32[]{:S(2)}, u32[]{:S(2)}) collective-permute-start(bf16[256,512]{1,0:T(8,128)(2,1)S(1)} %get-tuple-element.118), channel_id=1, source_target_pairs={{0,1},{1,0},{2,3},{3,2},{4,5},{5,4},{6,7},{7,6},{8,9},{9,8},{10,11... | collective-permute-start | bytes 786440 | tf_op jit(solution)/shard_map/ppermute | solution.py:24
  68.3 6.4 %collective-permute-start.19 = (bf16[256,256]{1,0:T(8,128)(2,1)S(1)}, bf16[256,256]{1,0:T(8,128)(2,1)S(1)}, u32[]{:S(2)}, u32[]{:S(2)}) collective-permute-start(bf16[256,256]{1,0:T(8,128)(2,1)S(1)} %get-tuple-element.116), channel_id=1, source_target_pairs={{0,2},{1,3},{2,0},{3,1},{4,6},{5,7},{6,4},{7,5},{8,10},{9,11},{10,... | collective-permute-start | bytes 393224 | tf_op jit(solution)/shard_map/ppermute | solution.py:24
  69.3 7.7 %collective-permute-start.22 = (bf16[256,256]{1,0:T(8,128)(2,1)S(1)}, bf16[256,256]{1,0:T(8,128)(2,1)S(1)}, u32[]{:S(2)}, u32[]{:S(2)}) collective-permute-start(bf16[256,256]{1,0:T(8,128)(2,1)S(1)} %get-tuple-element.125), channel_id=1, source_target_pairs={{0,2},{1,3},{2,0},{3,1},{4,6},{5,7},{6,4},{7,5},{8,10},{9,11},{10,... | collective-permute-start | bytes 393224 | tf_op jit(solution)/shard_map/ppermute | solution.py:24
  70.4 14.4 %collective-permute-start.25 = (bf16[256,512]{1,0:T(8,128)(2,1)S(1)}, bf16[256,512]{1,0:T(8,128)(2,1)S(1)}, u32[]{:S(2)}, u32[]{:S(2)}) collective-permute-start(bf16[256,512]{1,0:T(8,128)(2,1)S(1)} %add_convert_fusion), channel_id=1, source_target_pairs={{0,28},{1,29},{2,30},{3,31},{4,0},{5,1},{6,2},{7,3},{8,4},{9,5},{1... | collective-permute-start | bytes 786440 | tf_op jit(solution)/shard_map/ppermute | solution.py:24
  74.7 11.1 %collective-permute-start.21 = (bf16[256,256]{1,0:T(8,128)(2,1)S(1)}, bf16[256,256]{1,0:T(8,128)(2,1)S(1)}, u32[]{:S(2)}, u32[]{:S(2)}) collective-permute-start(bf16[256,256]{1,0:T(8,128)(2,1)S(1)} %add_text.2), channel_id=1, source_target_pairs={{0,8},{1,9},{2,10},{3,11},{4,12},{5,13},{6,14},{7,15},{8,16},{9,17... | collective-permute-start | bytes 393224 | tf_op jit(solution)/shard_map/ppermute | solution.py:24
  77.0 7.9 %collective-permute-start.26 = (bf16[512,256]{1,0:T(8,128)(2,1)S(1)}, bf16[512,256]{1,0:T(8,128)(2,1)S(1)}, u32[]{:S(2)}, u32[]{:S(2)}) collective-permute-start(bf16[512,256]{1,0:T(8,128)(2,1)S(1)} %get-tuple-element.129), channel_id=1, source_target_pairs={{0,2},{1,3},{2,0},{3,1},{4,6},{5,7},{6,4},{7,5},{8,10},{9,11},{10,... | collective-permute-start | bytes 786440 | tf_op jit(solution)/shard_map/ppermute | solution.py:24
  77.9 6.9 %collective-permute-start.24 = (bf16[256,512]{1,0:T(8,128)(2,1)S(1)}, bf16[256,512]{1,0:T(8,128)(2,1)S(1)}, u32[]{:S(2)}, u32[]{:S(2)}) collective-permute-start(bf16[256,512]{1,0:T(8,128)(2,1)S(1)} %get-tuple-element.128), channel_id=1, source_target_pairs={{0,1},{1,0},{2,3},{3,2},{4,5},{5,4},{6,7},{7,6},{8,9},{9,8},{10,11... | collective-permute-start | bytes 786440 | tf_op jit(solution)/shard_map/ppermute | solution.py:24
  78.0 7.8 %collective-permute-start.23 = (bf16[256,256]{1,0:T(8,128)(2,1)S(1)}, bf16[256,256]{1,0:T(8,128)(2,1)S(1)}, u32[]{:S(2)}, u32[]{:S(2)}) collective-permute-start(bf16[256,256]{1,0:T(8,128)(2,1)S(1)} %add_text.3), channel_id=1, source_target_pairs={{0,8},{1,9},{2,10},{3,11},{4,12},{5,13},{6,14},{7,15},{8,16},{9,17... | collective-permute-start | bytes 393224 | tf_op jit(solution)/shard_map/ppermute | solution.py:24

commit v7 on v6

--- a/solution.py
+++ b/solution.py
@@ -277,14 +277,15 @@
     return total
 
 
-def ahead_kernel(shard, span, *refs):
+def ahead_kernel(shard, span, behind, *refs):
     below, refs = (refs[0:4], refs[4:8], refs[8:12], refs[12:16]), refs[16:]
     rows_in, cols_in, stat_ref = refs[0:8:2], refs[1:8:2], refs[8]
     images = (refs[9:10], refs[10:11], refs[11:13], refs[13:15])
     texts, refs = text_parts(refs[15:], 4)
-    same_out, cross_out, weights_out, img_out, both_out = (
-        refs[0:2], refs[2:4], refs[4], refs[5:7], refs[7]
-    )
+    if behind:
+        total_out, img_out, both_out = refs[0], refs[1:3], refs[3]
+    else:
+        total_in, same_out, cross_out, weights_out = refs[0], refs[1:3], refs[3:5], refs[5]
     home, third = slice(0, 2 * shard), slice(2 * shard, 3 * shard)
     fourth, far = slice(3 * shard, 4 * shard), slice(2 * shard, 4 * shard)
     col_home, col_third, col_last, col_far = (
@@ -314,15 +315,13 @@
             near = weigh(below[call], here, home, row[:2], seen, col_home)
         return jnp.concatenate(weights, axis=1), near
 
-    total = both = None
-    ready = weights_of(0)
-    for index in range(4):
-        weights, near = ready
-        if index < 3:
-            ready = weights_of(index + 1)
+    both = None
+    total = None if behind else total_in[...]
+    for index in (2, 3) if behind else (0, 1):
+        weights, near = weights_of(index)
         image = rows_of(images[index], span)
         term = text_term(image, weights)
-        total = total + term if index else term
+        total = term if total is None else total + term
         if index < 2:
             weights_out[pl.ds(index * shard, shard)] = weights
             continue
@@ -330,12 +329,15 @@
         both = term if index == 2 else both + term
         out = img_out[index - 2]
         out[...] = image_term((near, weights), texts, span).astype(out.dtype)
+    if behind:
+        total_out[...] = total
+        both_out[...] = both
+        return
     height = total.shape[0] // 2
     for index in range(2):
         part = total[index * height : (index + 1) * height]
         same_out[index][...] = part[:, :shard]
         cross_out[index][...] = part[:, shard:].astype(jnp.bfloat16)
-    both_out[...] = both
 
 
 def home_kernel(shard, span, *refs):
@@ -509,25 +511,30 @@
     flat = jax.ShapeDtypeStruct((shard, width_s), bf16)
     tall_half = jax.ShapeDtypeStruct((width_s // 2, shard), f32)
     sent_half = jax.ShapeDtypeStruct((width_s // 2, shard), bf16)
-    *txt_ahead, weights, img_back, img_cross, txt_both = pl.pallas_call(
-        lambda *refs: ahead_kernel(shard, spans[0], *refs),
-        out_shape=(
-            tall_half,
-            tall_half,
-            sent_half,
-            sent_half,
-            jax.ShapeDtypeStruct((2 * shard, 2 * shard), bf16),
-            wide,
-            flat,
-            jax.ShapeDtypeStruct((width_s, 2 * shard), f32),
-        ),
-        in_specs=[vmem] * 36,
-        out_specs=(vmem,) * 8,
-        compiler_params=params(24),
+    square = jax.ShapeDtypeStruct((width_s, 2 * shard), f32)
+
+    def gradients(behind, outs, *more, name):
+        args = (
+            *home, *near, *side, *far, *calls_stats, stats, *images, *texts, *more
+        )
+        return pl.pallas_call(
+            lambda *refs: ahead_kernel(shard, spans[0], behind, *refs),
+            out_shape=outs,
+            in_specs=[vmem] * len(args),
+            out_specs=(vmem,) * len(outs),
+            compiler_params=params(24),
+            name=name,
+        )(*args)
+
+    txt_part, img_back, img_cross, txt_both = gradients(
+        True, (square, wide, flat, square), name="gradients_behind"
+    )
+    *txt_ahead, weights = gradients(
+        False,
+        (tall_half, tall_half, sent_half, sent_half)
+        + (jax.ShapeDtypeStruct((2 * shard, 2 * shard), bf16),),
+        txt_part,
         name="gradients_ahead",
-    )(
-        *home, *near, *side, *far, *calls_stats, stats,
-        *images, *texts,
     )
     img_cross = to_other_core(img_cross)
     img_sum = (img_back + img_cross.astype(f32)).astype(bf16)

time: 87 us -> 87.8 us (level)
    pallas_call x1 -> x2, Pallas kernels: 2.68 us -> 3.08 us  [gradients(): pl.pallas_call(lambda *refs: ahead_kernel(shard, spans[0], behind, *refs)...]
  transfers between devices with their start and end apart: 27 -> 27, of which waited for: 12 -> 13; matrix products, arithmetic and copies ran while one was open for 0% -> 0% of each run, Pallas kernels for 9% -> 10%
where the time goes in v7:
time: 87.8 us; the launch traced here: 87.5 us
  waiting for transfers between devices  39.4 us (45%)
  starting transfers between devices  31 us (35%)
  Pallas kernels  14.3 us (16%)
  local copies, waits for them, and re-layouts  2.04 us (2%)
    ppermute x27, waiting for transfers between devices, send_to(): return lax.ppermute(value, AXES, pairs)  39.4 us
    ppermute x27, starting transfers between devices, send_to(): return lax.ppermute(value, AXES, pairs)  31 us
    pallas_call x3, Pallas kernels, part_scores(): pl.pallas_call(lambda *refs: part_kernel(shard, scales, spans, sizes, cou...  5.34 us
    pallas_call x2, Pallas kernels, gradients(): pl.pallas_call(lambda *refs: ahead_kernel(shard, spans[0], behind, *refs)...  3.08 us
    unnamed x8, local copies, waits for them, and re-layouts  2.04 us
    pallas_call x2, Pallas kernels, finish(): pl.pallas_call(lambda *refs: kernel(scale_s, *refs), out_shape=wide, in_s...  1.91 us
    pallas_call x1, Pallas kernels, on_device(): pl.pallas_call(lambda *refs: far_kernel(shard, scales, spans, *refs), out...  1.85 us
  transfers between devices with their start and end apart: 27, of which 13 were waited for; matrix products, arithmetic and copies ran while one was open for 0% of the time, Pallas kernels for 10%

profile of v7, /device:TPU:0, one launch (start us, length us, event | category | flops | bytes accessed | tf_op | source)
XLA Modules:
  0.0 87.5 jit_solution(17850376567937302217)
XLA Ops:
  0.6 0.5 collective-permute-start.1
  1.2 2.6 %collective-permute-start.6 = (bf16[256,1280]{1,0:T(8,128)(2,1)}, bf16[256,1280]{1,0:T(8,128)(2,1)S(1)}, u32[]{:S(2)}, u32[]{:S(2)}) collective-permute-start(bf16[256,1280]{1,0:T(8,128)(2,1)} %second.3), channel_id=1, source_target_pairs={{0,2},{1,3},{2,0},{3,1},{4,6},{5,7},{6,4},{7,5},{8,10},{9,11},{10,... | collective-permute-start | bytes 1966088 | tf_op jit(solution)/shard_map/ppermute | solution.py:24
  3.7 3.6 %collective-permute-start.4 = (bf16[256,1280]{1,0:T(8,128)(2,1)}, bf16[256,1280]{1,0:T(8,128)(2,1)S(1)}, u32[]{:S(2)}, u32[]{:S(2)}) collective-permute-start(bf16[256,1280]{1,0:T(8,128)(2,1)} %second.3), channel_id=1, source_target_pairs={{0,24},{1,25},{2,26},{3,27},{4,28},{5,29},{6,30},{7,31},{8,0},{9,1... | collective-permute-start | bytes 1966088 | tf_op jit(solution)/shard_map/ppermute | solution.py:24
  7.3 1.1 %copy-done.1 = bf16[256,1280]{1,0:T(8,128)(2,1)S(1)} copy-done((bf16[256,1280]{1,0:T(8,128)(2,1)S(1)}, bf16[256,1280]{1,0:T(8,128)(2,1)}, u32[]{:S(2)}) %copy-start.1) | copy-done | bytes 655384
  8.4 0.9 %copy-done.2 = bf16[256,512]{1,0:T(8,128)(2,1)S(1)} copy-done((bf16[256,512]{1,0:T(8,128)(2,1)S(1)}, bf16[256,512]{1,0:T(8,128)(2,1)}, u32[]{:S(2)}) %copy-start.2) | copy-done | bytes 262168
  9.4 0.1 pack_images.1
  9.5 1.6 %collective-permute-start.2 = (bf16[112,1792]{1,0:T(8,128)(2,1)S(1)}, bf16[112,1792]{1,0:T(8,128)(2,1)S(1)}, u32[]{:S(2)}, u32[]{:S(2)}) collective-permute-start(bf16[112,1792]{1,0:T(8,128)(2,1)S(1)} %get-tuple-element.74), channel_id=1, source_target_pairs={{0,4},{1,5},{2,6},{3,7},{4,0},{5,1},{6,2},{7,3},{8,12},{9,13},{10,... | collective-permute-start | bytes 1204232 | tf_op jit(solution)/shard_map/ppermute | solution.py:24
  11.1 0.5 collective-permute-start.5
  11.6 0.4 collective-permute-start.3
  12.1 9.2 %collective-permute-done.2 = bf16[112,1792]{1,0:T(8,128)(2,1)S(1)} collective-permute-done((bf16[112,1792]{1,0:T(8,128)(2,1)S(1)}, bf16[112,1792]{1,0:T(8,128)(2,1)S(1)}, u32[]{:S(2)}, u32[]{:S(2)}) %collective-permute-start.2) | collective-permute-done | bytes 401440 | tf_op jit(solution)/shard_map/ppermute | solution.py:24
  21.3 1.5 %collective-permute-done.4.t_ahead = bf16[256,1280]{1,0:T(8,128)(2,1)S(1)} collective-permute-done((bf16[256,1280]{1,0:T(8,128)(2,1)}, bf16[256,1280]{1,0:T(8,128)(2,1)S(1)}, u32[]{:S(2)}, u32[]{:S(2)}) %collective-permute-start.4) | collective-permute-done | bytes 655392 | tf_op jit(solution)/shard_map/ppermute | solution.py:24
  22.7 2.1 %collective-permute-done.5.s_x = bf16[256,512]{1,0:T(8,128)(2,1)S(1)} collective-permute-done((bf16[256,512]{1,0:T(8,128)(2,1)}, bf16[256,512]{1,0:T(8,128)(2,1)S(1)}, u32[]{:S(2)}, u32[]{:S(2)}) %collective-permute-start.5) | collective-permute-done | bytes 262176 | tf_op jit(solution)/shard_map/ppermute | solution.py:24
  24.9 2.7 %collective-permute-done.3.s_ahead = bf16[256,512]{1,0:T(8,128)(2,1)S(1)} collective-permute-done((bf16[256,512]{1,0:T(8,128)(2,1)}, bf16[256,512]{1,0:T(8,128)(2,1)S(1)}, u32[]{:S(2)}, u32[]{:S(2)}) %collective-permute-start.3) | collective-permute-done | bytes 262176 | tf_op jit(solution)/shard_map/ppermute | solution.py:24
  27.6 0.2 pack_arrived.1
  27.8 0.6 collective-permute-start.10
  28.4 1.5 %collective-permute-start.7 = (bf16[144,1792]{1,0:T(8,128)(2,1)S(1)}, bf16[144,1792]{1,0:T(8,128)(2,1)S(1)}, u32[]{:S(2)}, u32[]{:S(2)}) collective-permute-start(bf16[144,1792]{1,0:T(8,128)(2,1)S(1)} %get-tuple-element.84), channel_id=1, source_target_pairs={{0,4},{1,5},{2,6},{3,7},{4,8},{5,9},{6,10},{7,11},{8,12},{9,13},{1... | collective-permute-start | bytes 1548296 | tf_op jit(solution)/shard_map/ppermute | solution.py:24
  29.9 2.2 %collective-permute-start.8 = (bf16[112,1792]{1,0:T(8,128)(2,1)S(1)}, bf16[112,1792]{1,0:T(8,128)(2,1)S(1)}, u32[]{:S(2)}, u32[]{:S(2)}) collective-permute-start(bf16[112,1792]{1,0:T(8,128)(2,1)S(1)} %collective-permute-done.2), channel_id=1, source_target_pairs={{0,8},{1,9},{2,10},{3,11},{4,4},{5,5},{6,6},{7,7},{8,16},{9,17},{1... | collective-permute-start | bytes 1204232 | tf_op jit(solution)/shard_map/ppermute | solution.py:24
  32.1 3.9 %collective-permute-start.9 = (bf16[32,1792]{1,0:T(8,128)(2,1)S(1)}, bf16[32,1792]{1,0:T(8,128)(2,1)S(1)}, u32[]{:S(2)}, u32[]{:S(2)}) collective-permute-start(bf16[32,1792]{1,0:T(8,128)(2,1)S(1)} %get-tuple-element.93), channel_id=1, source_target_pairs={{0,24},{1,25},{2,26},{3,27},{4,28},{5,29},{6,30},{7,31},{8,0},{9,1... | collective-permute-start | bytes 344072 | tf_op jit(solution)/shard_map/ppermute | solution.py:24
  36.2 2.5 %scores_home.1 = (f32[512,768]{1,0:T(8,128)S(1)}, f32[512,768]{1,0:T(8,128)S(1)}, f32[512,768]{1,0:T(8,128)S(1)}, f32[512,768]{1,0:T(8,128)S(1)}, f32[8,512]{1,0:T(8,128)S(1)}, /*index=5*/f32[8,768]{1,0:T(8,128)S(1)}) custom-call(bf16[256,1792]{1,0:T(8,128)(2,1)S(1)} %get-tuple-element.70.refs_0_.refs_25_.refs_7_, ...), custom_call_target="tpu_custom_call" | custom-call | tf_op jit(solution)/shard_map/scores_home/pallas_call | solution.py:450
  38.6 6.9 %collective-permute-done.8.refs_1_.refs_3_.refs_28_ = bf16[112,1792]{1,0:T(8,128)(2,1)S(1)} collective-permute-done((bf16[112,1792]{1,0:T(8,128)(2,1)S(1)}, bf16[112,1792]{1,0:T(8,128)(2,1)S(1)}, u32[]{:S(2)}, u32[]{:S(2)}) %collective-permute-start.8) | collective-permute-done | bytes 401440 | tf_op jit(solution)/shard_map/ppermute | solution.py:24
  45.5 0.3 collective-permute-done.7.refs_0_.refs_2_.refs_27_
  45.8 1.5 %scores_near.1 = (f32[256,768]{1,0:T(8,128)S(1)}, f32[256,768]{1,0:T(8,128)S(1)}, f32[256,768]{1,0:T(8,128)S(1)}, f32[256,768]{1,0:T(8,128)S(1)}, f32[8,256]{1,0:T(8,128)S(1)}, /*index=5*/f32[4,768]{1,0:T(4,128)S(1)}) custom-call(bf16[144,1792]{1,0:T(8,128)(2,1)S(1)} %collective-permute-done.7.refs_0_.refs_2_.refs_27_, ...), custom_call_target="tpu_custom_call" | custom-call | tf_op jit(solution)/shard_map/scores_near/pallas_call | solution.py:450
  47.2 0.5 collective-permute-start.12
  47.8 1.4 %scores_side.1 = (f32[768,256]{1,0:T(8,128)S(1)}, f32[768,256]{1,0:T(8,128)S(1)}, f32[768,256]{1,0:T(8,128)S(1)}, f32[768,256]{1,0:T(8,128)S(1)}, f32[8,768]{1,0:T(8,128)S(1)}, /*index=5*/f32[12,256]{1,0:T(8,128)S(1)}) custom-call(bf16[256,1792]{1,0:T(8,128)(2,1)S(1)} %get-tuple-element.70.refs_0_.refs_25_.refs_7_, ...), custom_call_target="tpu_custom_call" | custom-call | flops 99999997952 | bytes 1000000000 | tf_op jit(solution)/shard_map/scores_side/pallas_call | solution.py:450
  49.2 1.8 %scores_far.1 = (f32[256,1024]{1,0:T(8,128)S(1)}, f32[256,1024]{1,0:T(8,128)S(1)}, f32[256,1024]{1,0:T(8,128)S(1)}, f32[256,1024]{1,0:T(8,128)S(1)}, f32[8,256]{...) custom-call(bf16[144,1792]{1,0:T(8,128)(2,1)S(1)} %collective-permute-done.11.refs_0_.refs_29_, ...), custom_call_target="tpu_custom_call" | custom-call | tf_op jit(solution)/shard_map/scores_far/pallas_call | solution.py:472
  51.1 0.3 collective-permute-start.13
  51.4 1.5 %collective-permute-start.14 = (f32[8,1024]{1,0:T(8,128)S(1)}, f32[8,1024]{1,0:T(8,128)S(1)}, u32[]{:S(2)}, u32[]{:S(2)}) collective-permute-start(f32[8,1024]{1,0:T(8,128)S(1)} %get-tuple-element.110.refs_0_), channel_id=1, source_target_pairs={{0,2},{1,3},{2,0},{3,1},{4,6},{5,7},{6,4},{7,5},{8,10},{9,11},{10,... | collective-permute-start | bytes 98312 | tf_op jit(solution)/shard_map/ppermute | solution.py:24
  52.9 2.4 %collective-permute-done.14.refs_2_ = f32[8,1024]{1,0:T(8,128)S(1)} collective-permute-done((f32[8,1024]{1,0:T(8,128)S(1)}, f32[8,1024]{1,0:T(8,128)S(1)}, u32[]{:S(2)}, u32[]{:S(2)}) %collective-permute-start.14) | collective-permute-done | bytes 32800 | tf_op jit(solution)/shard_map/ppermute | solution.py:24
  55.4 0.5 collective-permute-start.15
  55.9 0.4 collective-permute-start.16
  56.3 3.8 %collective-permute-start.17 = (f32[8,512]{1,0:T(8,128)S(1)}, f32[8,512]{1,0:T(8,128)S(1)}, u32[]{:S(2)}, u32[]{:S(2)}) collective-permute-start(f32[8,512]{1,0:T(8,128)S(1)} %get-tuple-element.114), channel_id=1, source_target_pairs={{0,28},{1,29},{2,30},{3,31},{4,8},{5,9},{6,10},{7,11},{8,4},{9,5},... | collective-permute-start | bytes 49160 | tf_op jit(solution)/shard_map/ppermute | solution.py:24
  60.0 2.0 %collective-permute-start.18 = (f32[8,512]{1,0:T(8,128)S(1)}, f32[8,512]{1,0:T(8,128)S(1)}, u32[]{:S(2)}, u32[]{:S(2)}) collective-permute-start(f32[8,512]{1,0:T(8,128)S(1)} %get-tuple-element.115), channel_id=1, source_target_pairs={{0,24},{1,25},{2,26},{3,27},{4,28},{5,29},{6,30},{7,31},{8,16},{9,... | collective-permute-start | bytes 49160 | tf_op jit(solution)/shard_map/ppermute | solution.py:24
  62.1 0.6 collective-permute-done.17.refs_3_
  62.7 2.9 %collective-permute-done.18.refs_4_ = f32[8,512]{1,0:T(8,128)S(1)} collective-permute-done((f32[8,512]{1,0:T(8,128)S(1)}, f32[8,512]{1,0:T(8,128)S(1)}, u32[]{:S(2)}, u32[]{:S(2)}) %collective-permute-start.18) | collective-permute-done | bytes 16416 | tf_op jit(solution)/shard_map/ppermute | solution.py:24
  65.6 1.9 %gradients_behind.1 = (f32[512,512]{1,0:T(8,128)S(1)}, f32[256,512]{1,0:T(8,128)S(1)}, bf16[256,512]{1,0:T(8,128)(2,1)S(1)}, f32[512,512]{1,0:T(8,128)S(1)}) custom-call(f32[512,768]{1,0:T(8,128)S(1)} %get-tuple-element.80.refs_0_, f32[512,768]{1,0:T(8,128)S(1)} %get-tuple-element.81.refs_1_, f32[512,768]{1,0:T(8,128)S(1)} %get-tuple-element.82.refs_2_, ...), custom_call_target="tpu_custom_call" | custom-call | tf_op jit(solution)/shard_map/gradients_behind/pallas_call | solution.py:520
  67.6 1.2 %gradients_ahead.1 = (f32[256,256]{1,0:T(8,128)S(1)}, f32[256,256]{1,0:T(8,128)S(1)}, bf16[256,256]{1,0:T(8,128)(2,1)S(1)}, bf16[256,256]{1,0:T(8,128)(2,1)S(1)}, bf16[512,512]{1,0:T(8,128)(2,1)S(1)}) custom-call(f32[512,768]{1,0:T(8,128)S(1)} %get-tuple-element.80.refs_0_, f32[512,768]{1,0:T(8,128)S(1)} %get-tuple-element.81.refs_1_, ...), custom_call_target="tpu_custom_call" | custom-call | tf_op jit(solution)/shard_map/gradients_ahead/pallas_call | solution.py:520
  68.8 1.2 %collective-permute-start.19 = (bf16[256,256]{1,0:T(8,128)(2,1)S(1)}, bf16[256,256]{1,0:T(8,128)(2,1)S(1)}, u32[]{:S(2)}, u32[]{:S(2)}) collective-permute-start(bf16[256,256]{1,0:T(8,128)(2,1)S(1)} %get-tuple-element.118), channel_id=1, source_target_pairs={{0,2},{1,3},{2,0},{3,1},{4,6},{5,7},{6,4},{7,5},{8,10},{9,11},{10,... | collective-permute-start | bytes 393224 | tf_op jit(solution)/shard_map/ppermute | solution.py:24
  70.0 0.8 collective-permute-start.22
  70.9 0.1 add_convert_fusion
  71.0 1.0 %collective-permute-start.25 = (bf16[256,512]{1,0:T(8,128)(2,1)S(1)}, bf16[256,512]{1,0:T(8,128)(2,1)S(1)}, u32[]{:S(2)}, u32[]{:S(2)}) collective-permute-start(bf16[256,512]{1,0:T(8,128)(2,1)S(1)} %add_convert_fusion), channel_id=1, source_target_pairs={{0,28},{1,29},{2,30},{3,31},{4,0},{5,1},{6,2},{7,3},{8,4},{9,5},{1... | collective-permute-start | bytes 786440 | tf_op jit(solution)/shard_map/ppermute | solution.py:24
  72.0 3.2 %collective-permute-done.19.second = bf16[256,256]{1,0:T(8,128)(2,1)S(1)} collective-permute-done((bf16[256,256]{1,0:T(8,128)(2,1)S(1)}, bf16[256,256]{1,0:T(8,128)(2,1)S(1)}, u32[]{:S(2)}, u32[]{:S(2)}) %collective-permute-start.19) | collective-permute-done | bytes 131104 | tf_op jit(solution)/shard_map/ppermute | solution.py:24
  75.3 1.5 %gradients_home.1 = (f32[256,512]{1,0:T(8,128)S(1)}, bf16[256,512]{1,0:T(8,128)(2,1)S(1)}, f32[512,256]{1,0:T(8,128)S(1)}, bf16[512,256]{1,0:T(8,128)(2,1)S(1)}) custom-call(f32[512,768]{1,0:T(8,128)S(1)} %get-tuple-element.80.refs_0_, f32[512,768]{1,0:T(8,128)S(1)} %get-tuple-element.81.refs_1_, f32[512,768]{1,0:T(8,128)S(1)} %get-tuple-element.82.refs_2_, ...), custom_call_target="tpu_custom_call" | custom-call | tf_op jit(solution)/shard_map/gradients_home/pallas_call | solution.py:543
  76.7 0.8 collective-permute-done.22.second
  77.5 1.2 %collective-permute-start.26 = (bf16[512,256]{1,0:T(8,128)(2,1)S(1)}, bf16[512,256]{1,0:T(8,128)(2,1)S(1)}, u32[]{:S(2)}, u32[]{:S(2)}) collective-permute-start(bf16[512,256]{1,0:T(8,128)(2,1)S(1)} %get-tuple-element.131), channel_id=1, source_target_pairs={{0,2},{1,3},{2,0},{3,1},{4,6},{5,7},{6,4},{7,5},{8,10},{9,11},{10,... | collective-permute-start | bytes 786440 | tf_op jit(solution)/shard_map/ppermute | solution.py:24
  78.8 6.6 %collective-permute-done.26.refs_1_ = bf16[512,256]{1,0:T(8,128)(2,1)S(1)} collective-permute-done((bf16[512,256]{1,0:T(8,128)(2,1)S(1)}, bf16[512,256]{1,0:T(8,128)(2,1)S(1)}, u32[]{:S(2)}, u32[]{:S(2)}) %collective-permute-start.26) | collective-permute-done | bytes 262176 | tf_op jit(solution)/shard_map/ppermute | solution.py:24
  85.4 0.9 %finish_image.1 = f32[256,512]{1,0:T(8,128)} custom-call(f32[256,512]{1,0:T(8,128)S(1)} %get-tuple-element.129.refs_0_, bf16[256,512]{1,0:T(8,128)(2,1)S(1)} %collective-permute-done.24.refs_1_, bf16[256,512]{1,0:T(8,128)(2,1)S(1)} %collective-permute-done.25.refs_2_), custom_call_target="tpu_custom_call" | custom-call | flops 3000000000 | bytes 30000000 | tf_op jit(solution)/shard_map/finish_image/pallas_call | solution.py:575
  86.3 0.2 collective-permute-done.23.refs_3_
  86.5 1.0 %finish_text.1 = f32[256,512]{1,0:T(8,128)} custom-call(f32[512,256]{1,0:T(8,128)S(1)} %get-tuple-element.134.refs_0_, bf16[512,256]{1,0:T(8,128)(2,1)S(1)} %collective-permute-done.26.refs_1_, bf16[256,256]{1,0:T(8,128)(2,1)S(1)} %collective-permute-done.21.refs_2_, bf16[256,256]{1,0:T(8,128)(2,1)S(1)} %collective-permute-done.23.refs_3_), custom_call_target="tpu_custom_call" | custom-call | tf_op jit(solution)/shard_map/finish_text/pallas_call | solution.py:575
  (32 shorter events, 0.5 us)
Async XLA Ops:
  0.6 35.4 %copy-start = (bf16[256,1280]{1,0:T(8,128)(2,1)S(1)}, bf16[256,1280]{1,0:T(8,128)(2,1)}, u32[]{:S(2)}) copy-start(bf16[256,1280]{1,0:T(8,128)(2,1)} %second.3) | copy-start | bytes 1966084
  0.6 10.4 %collective-permute-start.1 = (bf16[256,1280]{1,0:T(8,128)(2,1)}, bf16[256,1280]{1,0:T(8,128)(2,1)S(1)}, u32[]{:S(2)}, u32[]{:S(2)}) collective-permute-start(bf16[256,1280]{1,0:T(8,128)(2,1)} %second.2), channel_id=1, source_target_pairs={{0,1},{1,0},{2,3},{3,2},{4,5},{5,4},{6,7},{7,6},{8,9},{9,8},{10,11... | collective-permute-start | bytes 1966088 | tf_op jit(solution)/shard_map/ppermute | solution.py:24
  1.2 20.1 %collective-permute-start.6 = (bf16[256,1280]{1,0:T(8,128)(2,1)}, bf16[256,1280]{1,0:T(8,128)(2,1)S(1)}, u32[]{:S(2)}, u32[]{:S(2)}) collective-permute-start(bf16[256,1280]{1,0:T(8,128)(2,1)} %second.3), channel_id=1, source_target_pairs={{0,2},{1,3},{2,0},{3,1},{4,6},{5,7},{6,4},{7,5},{8,10},{9,11},{10,... | collective-permute-start | bytes 1966088 | tf_op jit(solution)/shard_map/ppermute | solution.py:24
  3.7 19.0 %collective-permute-start.4 = (bf16[256,1280]{1,0:T(8,128)(2,1)}, bf16[256,1280]{1,0:T(8,128)(2,1)S(1)}, u32[]{:S(2)}, u32[]{:S(2)}) collective-permute-start(bf16[256,1280]{1,0:T(8,128)(2,1)} %second.3), channel_id=1, source_target_pairs={{0,24},{1,25},{2,26},{3,27},{4,28},{5,29},{6,30},{7,31},{8,0},{9,1... | collective-permute-start | bytes 1966088 | tf_op jit(solution)/shard_map/ppermute | solution.py:24
  7.3 3.8 %collective-permute-start = (bf16[256,512]{1,0:T(8,128)(2,1)}, bf16[256,512]{1,0:T(8,128)(2,1)S(1)}, u32[]{:S(2)}, u32[]{:S(2)}) collective-permute-start(bf16[256,512]{1,0:T(8,128)(2,1)} %first.2), channel_id=1, source_target_pairs={{0,1},{1,0},{2,3},{3,2},{4,5},{5,4},{6,7},{7,6},{8,9},{9,8},{10,11... | collective-permute-start | bytes 786440 | tf_op jit(solution)/shard_map/ppermute | solution.py:24
  7.3 1.1 %copy-start.1 = (bf16[256,1280]{1,0:T(8,128)(2,1)S(1)}, bf16[256,1280]{1,0:T(8,128)(2,1)}, u32[]{:S(2)}) copy-start(bf16[256,1280]{1,0:T(8,128)(2,1)} %second.2) | copy-start | bytes 1966084
  8.4 0.9 %copy-start.2 = (bf16[256,512]{1,0:T(8,128)(2,1)S(1)}, bf16[256,512]{1,0:T(8,128)(2,1)}, u32[]{:S(2)}) copy-start(bf16[256,512]{1,0:T(8,128)(2,1)} %first.2) | copy-start | bytes 786436
  9.4 26.7 %copy-start.3 = (bf16[256,512]{1,0:T(8,128)(2,1)S(1)}, bf16[256,512]{1,0:T(8,128)(2,1)}, u32[]{:S(2)}) copy-start(bf16[256,512]{1,0:T(8,128)(2,1)} %first.3) | copy-start | bytes 786436
  9.5 11.8 %collective-permute-start.2 = (bf16[112,1792]{1,0:T(8,128)(2,1)S(1)}, bf16[112,1792]{1,0:T(8,128)(2,1)S(1)}, u32[]{:S(2)}, u32[]{:S(2)}) collective-permute-start(bf16[112,1792]{1,0:T(8,128)(2,1)S(1)} %get-tuple-element.74), channel_id=1, source_target_pairs={{0,4},{1,5},{2,6},{3,7},{4,0},{5,1},{6,2},{7,3},{8,12},{9,13},{10,... | collective-permute-start | bytes 1204232 | tf_op jit(solution)/shard_map/ppermute | solution.py:24
  11.1 13.8 %collective-permute-start.5 = (bf16[256,512]{1,0:T(8,128)(2,1)}, bf16[256,512]{1,0:T(8,128)(2,1)S(1)}, u32[]{:S(2)}, u32[]{:S(2)}) collective-permute-start(bf16[256,512]{1,0:T(8,128)(2,1)} %first.3), channel_id=1, source_target_pairs={{0,2},{1,3},{2,0},{3,1},{4,6},{5,7},{6,4},{7,5},{8,10},{9,11},{10,... | collective-permute-start | bytes 786440 | tf_op jit(solution)/shard_map/ppermute | solution.py:24
  11.6 16.0 %collective-permute-start.3 = (bf16[256,512]{1,0:T(8,128)(2,1)}, bf16[256,512]{1,0:T(8,128)(2,1)S(1)}, u32[]{:S(2)}, u32[]{:S(2)}) collective-permute-start(bf16[256,512]{1,0:T(8,128)(2,1)} %first.3), channel_id=1, source_target_pairs={{0,24},{1,25},{2,26},{3,27},{4,28},{5,29},{6,30},{7,31},{8,0},{9,1... | collective-permute-start | bytes 786440 | tf_op jit(solution)/shard_map/ppermute | solution.py:24
  27.8 20.0 %collective-permute-start.10 = (bf16[224,1792]{1,0:T(8,128)(2,1)S(1)}, bf16[224,1792]{1,0:T(8,128)(2,1)S(1)}, u32[]{:S(2)}, u32[]{:S(2)}) collective-permute-start(bf16[224,1792]{1,0:T(8,128)(2,1)S(1)} %get-tuple-element.94), channel_id=1, source_target_pairs={{0,2},{1,3},{2,0},{3,1},{4,6},{5,7},{6,4},{7,5},{8,10},{9,11},{10,... | collective-permute-start | bytes 2408456 | tf_op jit(solution)/shard_map/ppermute | solution.py:24
  28.4 17.4 %collective-permute-start.7 = (bf16[144,1792]{1,0:T(8,128)(2,1)S(1)}, bf16[144,1792]{1,0:T(8,128)(2,1)S(1)}, u32[]{:S(2)}, u32[]{:S(2)}) collective-permute-start(bf16[144,1792]{1,0:T(8,128)(2,1)S(1)} %get-tuple-element.84), channel_id=1, source_target_pairs={{0,4},{1,5},{2,6},{3,7},{4,8},{5,9},{6,10},{7,11},{8,12},{9,13},{1... | collective-permute-start | bytes 1548296 | tf_op jit(solution)/shard_map/ppermute | solution.py:24
  29.9 15.6 %collective-permute-start.8 = (bf16[112,1792]{1,0:T(8,128)(2,1)S(1)}, bf16[112,1792]{1,0:T(8,128)(2,1)S(1)}, u32[]{:S(2)}, u32[]{:S(2)}) collective-permute-start(bf16[112,1792]{1,0:T(8,128)(2,1)S(1)} %collective-permute-done.2), channel_id=1, source_target_pairs={{0,8},{1,9},{2,10},{3,11},{4,4},{5,5},{6,6},{7,7},{8,16},{9,17},{1... | collective-permute-start | bytes 1204232 | tf_op jit(solution)/shard_map/ppermute | solution.py:24
  32.1 15.6 %collective-permute-start.9 = (bf16[32,1792]{1,0:T(8,128)(2,1)S(1)}, bf16[32,1792]{1,0:T(8,128)(2,1)S(1)}, u32[]{:S(2)}, u32[]{:S(2)}) collective-permute-start(bf16[32,1792]{1,0:T(8,128)(2,1)S(1)} %get-tuple-element.93), channel_id=1, source_target_pairs={{0,24},{1,25},{2,26},{3,27},{4,28},{5,29},{6,30},{7,31},{8,0},{9,1... | collective-permute-start | bytes 344072 | tf_op jit(solution)/shard_map/ppermute | solution.py:24
  45.8 3.4 %collective-permute-start.11 = (bf16[144,1792]{1,0:T(8,128)(2,1)S(1)}, bf16[144,1792]{1,0:T(8,128)(2,1)S(1)}, u32[]{:S(2)}, u32[]{:S(2)}) collective-permute-start(bf16[144,1792]{1,0:T(8,128)(2,1)S(1)} %collective-permute-done.7.refs_0_.refs_2_.refs_27_), channel_id=1, source_target_pairs={{0,1},{1,0},{2,3},{3,2},{4,5},{5,4},{6,7},{7,6},{8,9},{9,8},{10,11... | collective-permute-start | bytes 1548296 | tf_op jit(solution)/shard_map/ppermute | solution.py:24
  47.2 2.0 %collective-permute-start.12 = (bf16[112,1792]{1,0:T(8,128)(2,1)S(1)}, bf16[112,1792]{1,0:T(8,128)(2,1)S(1)}, u32[]{:S(2)}, u32[]{:S(2)}) collective-permute-start(bf16[112,1792]{1,0:T(8,128)(2,1)S(1)} %collective-permute-done.8.refs_1_.refs_3_.refs_28_), channel_id=1, source_target_pairs={{0,1},{1,0},{2,3},{3,2},{4,5},{5,4},{6,7},{7,6},{8,9},{9,8},{10,11... | collective-permute-start | bytes 1204232 | tf_op jit(solution)/shard_map/ppermute | solution.py:24
  51.1 1.8 %collective-permute-start.13 = (f32[8,1024]{1,0:T(8,128)S(1)}, f32[8,1024]{1,0:T(8,128)S(1)}, u32[]{:S(2)}, u32[]{:S(2)}) collective-permute-start(f32[8,1024]{1,0:T(8,128)S(1)} %get-tuple-element.110.refs_0_), channel_id=1, source_target_pairs={{0,1},{1,0},{2,3},{3,2},{4,5},{5,4},{6,7},{7,6},{8,9},{9,8},{10,11... | collective-permute-start | bytes 98312 | tf_op jit(solution)/shard_map/ppermute | solution.py:24
  51.4 3.9 %collective-permute-start.14 = (f32[8,1024]{1,0:T(8,128)S(1)}, f32[8,1024]{1,0:T(8,128)S(1)}, u32[]{:S(2)}, u32[]{:S(2)}) collective-permute-start(f32[8,1024]{1,0:T(8,128)S(1)} %get-tuple-element.110.refs_0_), channel_id=1, source_target_pairs={{0,2},{1,3},{2,0},{3,1},{4,6},{5,7},{6,4},{7,5},{8,10},{9,11},{10,... | collective-permute-start | bytes 98312 | tf_op jit(solution)/shard_map/ppermute | solution.py:24
  55.4 6.7 %collective-permute-start.15 = (f32[8,512]{1,0:T(8,128)S(1)}, f32[8,512]{1,0:T(8,128)S(1)}, u32[]{:S(2)}, u32[]{:S(2)}) collective-permute-start(f32[8,512]{1,0:T(8,128)S(1)} %get-tuple-element.112), channel_id=1, source_target_pairs={{0,4},{1,5},{2,6},{3,7},{4,0},{5,1},{6,2},{7,3},{8,12},{9,13},{10,... | collective-permute-start | bytes 49160 | tf_op jit(solution)/shard_map/ppermute | solution.py:24
  55.9 6.2 %collective-permute-start.16 = (f32[8,512]{1,0:T(8,128)S(1)}, f32[8,512]{1,0:T(8,128)S(1)}, u32[]{:S(2)}, u32[]{:S(2)}) collective-permute-start(f32[8,512]{1,0:T(8,128)S(1)} %get-tuple-element.113), channel_id=1, source_target_pairs={{0,8},{1,9},{2,10},{3,11},{4,12},{5,13},{6,14},{7,15},{8,0},{9,1},... | collective-permute-start | bytes 49160 | tf_op jit(solution)/shard_map/ppermute | solution.py:24
  56.3 6.4 %collective-permute-start.17 = (f32[8,512]{1,0:T(8,128)S(1)}, f32[8,512]{1,0:T(8,128)S(1)}, u32[]{:S(2)}, u32[]{:S(2)}) collective-permute-start(f32[8,512]{1,0:T(8,128)S(1)} %get-tuple-element.114), channel_id=1, source_target_pairs={{0,28},{1,29},{2,30},{3,31},{4,8},{5,9},{6,10},{7,11},{8,4},{9,5},... | collective-permute-start | bytes 49160 | tf_op jit(solution)/shard_map/ppermute | solution.py:24
  60.0 5.5 %collective-permute-start.18 = (f32[8,512]{1,0:T(8,128)S(1)}, f32[8,512]{1,0:T(8,128)S(1)}, u32[]{:S(2)}, u32[]{:S(2)}) collective-permute-start(f32[8,512]{1,0:T(8,128)S(1)} %get-tuple-element.115), channel_id=1, source_target_pairs={{0,24},{1,25},{2,26},{3,27},{4,28},{5,29},{6,30},{7,31},{8,16},{9,... | collective-permute-start | bytes 49160 | tf_op jit(solution)/shard_map/ppermute | solution.py:24
  67.5 3.3 %collective-permute-start.20 = (bf16[256,512]{1,0:T(8,128)(2,1)S(1)}, bf16[256,512]{1,0:T(8,128)(2,1)S(1)}, u32[]{:S(2)}, u32[]{:S(2)}) collective-permute-start(bf16[256,512]{1,0:T(8,128)(2,1)S(1)} %get-tuple-element.120), channel_id=1, source_target_pairs={{0,1},{1,0},{2,3},{3,2},{4,5},{5,4},{6,7},{7,6},{8,9},{9,8},{10,11... | collective-permute-start | bytes 786440 | tf_op jit(solution)/shard_map/ppermute | solution.py:24
  68.8 6.4 %collective-permute-start.19 = (bf16[256,256]{1,0:T(8,128)(2,1)S(1)}, bf16[256,256]{1,0:T(8,128)(2,1)S(1)}, u32[]{:S(2)}, u32[]{:S(2)}) collective-permute-start(bf16[256,256]{1,0:T(8,128)(2,1)S(1)} %get-tuple-element.118), channel_id=1, source_target_pairs={{0,2},{1,3},{2,0},{3,1},{4,6},{5,7},{6,4},{7,5},{8,10},{9,11},{10,... | collective-permute-start | bytes 393224 | tf_op jit(solution)/shard_map/ppermute | solution.py:24
  70.0 7.5 %collective-permute-start.22 = (bf16[256,256]{1,0:T(8,128)(2,1)S(1)}, bf16[256,256]{1,0:T(8,128)(2,1)S(1)}, u32[]{:S(2)}, u32[]{:S(2)}) collective-permute-start(bf16[256,256]{1,0:T(8,128)(2,1)S(1)} %get-tuple-element.127), channel_id=1, source_target_pairs={{0,2},{1,3},{2,0},{3,1},{4,6},{5,7},{6,4},{7,5},{8,10},{9,11},{10,... | collective-permute-start | bytes 393224 | tf_op jit(solution)/shard_map/ppermute | solution.py:24
  71.0 14.5 %collective-permute-start.25 = (bf16[256,512]{1,0:T(8,128)(2,1)S(1)}, bf16[256,512]{1,0:T(8,128)(2,1)S(1)}, u32[]{:S(2)}, u32[]{:S(2)}) collective-permute-start(bf16[256,512]{1,0:T(8,128)(2,1)S(1)} %add_convert_fusion), channel_id=1, source_target_pairs={{0,28},{1,29},{2,30},{3,31},{4,0},{5,1},{6,2},{7,3},{8,4},{9,5},{1... | collective-permute-start | bytes 786440 | tf_op jit(solution)/shard_map/ppermute | solution.py:24
  75.2 11.3 %collective-permute-start.21 = (bf16[256,256]{1,0:T(8,128)(2,1)S(1)}, bf16[256,256]{1,0:T(8,128)(2,1)S(1)}, u32[]{:S(2)}, u32[]{:S(2)}) collective-permute-start(bf16[256,256]{1,0:T(8,128)(2,1)S(1)} %add_text.2), channel_id=1, source_target_pairs={{0,8},{1,9},{2,10},{3,11},{4,12},{5,13},{6,14},{7,15},{8,16},{9,17... | collective-permute-start | bytes 393224 | tf_op jit(solution)/shard_map/ppermute | solution.py:24
  77.5 7.9 %collective-permute-start.26 = (bf16[512,256]{1,0:T(8,128)(2,1)S(1)}, bf16[512,256]{1,0:T(8,128)(2,1)S(1)}, u32[]{:S(2)}, u32[]{:S(2)}) collective-permute-start(bf16[512,256]{1,0:T(8,128)(2,1)S(1)} %get-tuple-element.131), channel_id=1, source_target_pairs={{0,2},{1,3},{2,0},{3,1},{4,6},{5,7},{6,4},{7,5},{8,10},{9,11},{10,... | collective-permute-start | bytes 786440 | tf_op jit(solution)/shard_map/ppermute | solution.py:24
  78.7 6.7 %collective-permute-start.24 = (bf16[256,512]{1,0:T(8,128)(2,1)S(1)}, bf16[256,512]{1,0:T(8,128)(2,1)S(1)}, u32[]{:S(2)}, u32[]{:S(2)}) collective-permute-start(bf16[256,512]{1,0:T(8,128)(2,1)S(1)} %get-tuple-element.130), channel_id=1, source_target_pairs={{0,1},{1,0},{2,3},{3,2},{4,5},{5,4},{6,7},{7,6},{8,9},{9,8},{10,11... | collective-permute-start | bytes 786440 | tf_op jit(solution)/shard_map/ppermute | solution.py:24
  78.8 7.8 %collective-permute-start.23 = (bf16[256,256]{1,0:T(8,128)(2,1)S(1)}, bf16[256,256]{1,0:T(8,128)(2,1)S(1)}, u32[]{:S(2)}, u32[]{:S(2)}) collective-permute-start(bf16[256,256]{1,0:T(8,128)(2,1)S(1)} %add_text.3), channel_id=1, source_target_pairs={{0,8},{1,9},{2,10},{3,11},{4,12},{5,13},{6,14},{7,15},{8,16},{9,17... | collective-permute-start | bytes 393224 | tf_op jit(solution)/shard_map/ppermute | solution.py:24

commit v8 on v6

--- a/solution.py
+++ b/solution.py
@@ -154,7 +154,7 @@
 def far_kernel(shard, scales, spans, *refs):
     outs = refs[13:]
     part_kernel(shard, scales, spans, (2,), 4, *refs[:7], *outs[:6])
-    total_kernel(shard, *refs[7:13], outs[4], outs[5], outs[6])
+    total_kernel(shard, *refs[7:13], *outs[4:])
 
 
 HOME, NEAR, SIDE, FAR = range(4)
@@ -179,12 +179,12 @@
 
 def total_kernel(shard, *refs):
     rows, seen, last = join_calls(refs[0:8:2], refs[1:8:2], shard)
-    out = refs[8]
+    row_out, col_out = refs[8:]
     for k in range(4):
         for index in range(4):
-            out[k : k + 1, index * shard : (index + 1) * shard] = rows[index][k]
-        out[4 + k : 5 + k, : 3 * shard] = seen[k]
-        out[4 + k : 5 + k, 3 * shard :] = last[k]
+            row_out[k : k + 1, index * shard : (index + 1) * shard] = rows[index][k]
+        col_out[k : k + 1, : 3 * shard] = seen[k]
+        col_out[k : k + 1, 3 * shard :] = last[k]
 
 
 def piece_stats(ref, kind, piece, shard):
@@ -197,15 +197,15 @@
     return lax.rem(block, 2) == 0, lax.rem(block // 2, 2) == 0
 
 
-def join_group_kernel(shard, mine_ref, core_ref, x_ref, home_ref, *outs):
+def join_group_kernel(shard, row_ref, col_ref, core_ref, x_ref, home_ref, *outs):
     halves = []
-    for kind, other_ref in enumerate((core_ref, x_ref)):
+    for kind, (mine_ref, other_ref) in enumerate(((row_ref, core_ref), (col_ref, x_ref))):
         for half in range(2):
             joint = []
             for piece in (2 * half, 2 * half + 1):
                 total = joined(
-                    piece_stats(mine_ref, kind, piece, shard),
-                    piece_stats(other_ref, kind, piece ^ 1, shard),
+                    piece_stats(mine_ref, 0, piece, shard),
+                    piece_stats(other_ref, 0, piece ^ 1, shard),
                 )
                 for k, value in enumerate(total):
                     at = 4 * kind + k
@@ -217,8 +217,6 @@
         for k in range(4):
             outs[2 * kind][k : k + 1] = jnp.where(upward, up[k], down[k])
             outs[2 * kind + 1][k : k + 1] = jnp.where(upward, down[k], up[k])
-        for out in outs[2 * kind : 2 * kind + 2]:
-            out[4:8] = jnp.zeros((4, 2 * shard), jnp.float32)
 
 
 def join_blocks_kernel(shard, home_ref, *refs):
@@ -467,27 +465,27 @@
     near, near_stats = part_scores(behind[:1], texts[:3], "scores_near")
     side, side_stats = part_scores((*own, behind[0]), texts[3:], "scores_side", HEAVY)
     others = (*home_stats, *near_stats, *side_stats)
-    *far, far_row, far_col, partial = pl.pallas_call(
+    *far, far_row, far_col, partial_row, partial_col = pl.pallas_call(
         lambda *refs: far_kernel(shard, scales, spans, *refs),
         out_shape=(score(1, 4),) * 4
-        + (stat(1), jax.ShapeDtypeStruct((4, 4 * shard), f32), stat(4)),
+        + (stat(1),) + (jax.ShapeDtypeStruct((4, 4 * shard), f32),) * 3,
         in_specs=[vmem] * 13,
-        out_specs=(vmem,) * 7,
+        out_specs=(vmem,) * 8,
         compiler_params=params(16),
         name="scores_far",
     )(*behind[1], *texts, *others)
     images = (image, image_core, *behind[0], *behind[1])
     calls_stats = (*others, far_row, far_col)
 
-    shared = jax.ShapeDtypeStruct((8, 2 * shard), f32)
+    shared = jax.ShapeDtypeStruct((4, 2 * shard), f32)
     group, *away = pl.pallas_call(
         lambda *refs: join_group_kernel(shard, *refs),
         out_shape=(stat(4),) + (shared,) * 4,
-        in_specs=[vmem] * 3,
+        in_specs=[vmem] * 4,
         out_specs=(vmem,) * 5,
         compiler_params=params(8),
         name="join_group",
-    )(partial, to_other_core(partial), to_other_x(partial))
+    )(partial_row, partial_col, to_other_core(partial_row), to_other_x(partial_col))
     away = [
         send_to(away[index], lambda block, x, core, step=step, first=first: (
             block + (step if (block // step) % 2 == first else -step), x, core

time: 87 us -> 86.8 us (level)
  no operation moved by 1% of the time
where the time goes in v8:
time: 86.8 us; the launch traced here: 86.6 us
  waiting for transfers between devices  39.1 us (45%)
  starting transfers between devices  30.8 us (35%)
  Pallas kernels  13.8 us (16%)
  local copies, waits for them, and re-layouts  2.04 us (2%)
    ppermute x27, waiting for transfers between devices, send_to(): return lax.ppermute(value, AXES, pairs)  39.1 us
    ppermute x27, starting transfers between devices, send_to(): return lax.ppermute(value, AXES, pairs)  30.8 us
    pallas_call x3, Pallas kernels, part_scores(): pl.pallas_call(lambda *refs: part_kernel(shard, scales, spans, sizes, cou...  5.33 us
    pallas_call x1, Pallas kernels, on_device(): pl.pallas_call(lambda *refs: ahead_kernel(shard, spans[0], *refs), out_sh...  2.68 us
    unnamed x8, local copies, waits for them, and re-layouts  2.04 us
    pallas_call x2, Pallas kernels, finish(): pl.pallas_call(lambda *refs: kernel(scale_s, *refs), out_shape=wide, in_s...  1.9 us
    pallas_call x1, Pallas kernels, on_device(): pl.pallas_call(lambda *refs: far_kernel(shard, scales, spans, *refs), out...  1.83 us
  transfers between devices with their start and end apart: 27, of which 12 were waited for; matrix products, arithmetic and copies ran while one was open for 0% of the time, Pallas kernels for 9%

profile of v8, /device:TPU:0, one launch (start us, length us, event | category | flops | bytes accessed | tf_op | source)
XLA Modules:
  0.0 86.6 jit_solution(1153261303089792847)
XLA Ops:
  0.6 0.5 collective-permute-start.1
  1.2 2.6 %collective-permute-start.6 = (bf16[256,1280]{1,0:T(8,128)(2,1)}, bf16[256,1280]{1,0:T(8,128)(2,1)S(1)}, u32[]{:S(2)}, u32[]{:S(2)}) collective-permute-start(bf16[256,1280]{1,0:T(8,128)(2,1)} %second.3), channel_id=1, source_target_pairs={{0,2},{1,3},{2,0},{3,1},{4,6},{5,7},{6,4},{7,5},{8,10},{9,11},{10,... | collective-permute-start | bytes 1966088 | tf_op jit(solution)/shard_map/ppermute | solution.py:24
  3.7 3.6 %collective-permute-start.4 = (bf16[256,1280]{1,0:T(8,128)(2,1)}, bf16[256,1280]{1,0:T(8,128)(2,1)S(1)}, u32[]{:S(2)}, u32[]{:S(2)}) collective-permute-start(bf16[256,1280]{1,0:T(8,128)(2,1)} %second.3), channel_id=1, source_target_pairs={{0,24},{1,25},{2,26},{3,27},{4,28},{5,29},{6,30},{7,31},{8,0},{9,1... | collective-permute-start | bytes 1966088 | tf_op jit(solution)/shard_map/ppermute | solution.py:24
  7.3 1.1 %copy-done.1 = bf16[256,1280]{1,0:T(8,128)(2,1)S(1)} copy-done((bf16[256,1280]{1,0:T(8,128)(2,1)S(1)}, bf16[256,1280]{1,0:T(8,128)(2,1)}, u32[]{:S(2)}) %copy-start.1) | copy-done | bytes 655384
  8.4 0.9 %copy-done.2 = bf16[256,512]{1,0:T(8,128)(2,1)S(1)} copy-done((bf16[256,512]{1,0:T(8,128)(2,1)S(1)}, bf16[256,512]{1,0:T(8,128)(2,1)}, u32[]{:S(2)}) %copy-start.2) | copy-done | bytes 262168
  9.4 0.1 pack_images.1
  9.5 1.6 %collective-permute-start.2 = (bf16[112,1792]{1,0:T(8,128)(2,1)S(1)}, bf16[112,1792]{1,0:T(8,128)(2,1)S(1)}, u32[]{:S(2)}, u32[]{:S(2)}) collective-permute-start(bf16[112,1792]{1,0:T(8,128)(2,1)S(1)} %get-tuple-element.74), channel_id=1, source_target_pairs={{0,4},{1,5},{2,6},{3,7},{4,0},{5,1},{6,2},{7,3},{8,12},{9,13},{10,... | collective-permute-start | bytes 1204232 | tf_op jit(solution)/shard_map/ppermute | solution.py:24
  11.1 0.5 collective-permute-start.5
  11.6 0.4 collective-permute-start.3
  12.1 9.2 %collective-permute-done.2 = bf16[112,1792]{1,0:T(8,128)(2,1)S(1)} collective-permute-done((bf16[112,1792]{1,0:T(8,128)(2,1)S(1)}, bf16[112,1792]{1,0:T(8,128)(2,1)S(1)}, u32[]{:S(2)}, u32[]{:S(2)}) %collective-permute-start.2) | collective-permute-done | bytes 401440 | tf_op jit(solution)/shard_map/ppermute | solution.py:24
  21.3 1.5 %collective-permute-done.4.t_ahead = bf16[256,1280]{1,0:T(8,128)(2,1)S(1)} collective-permute-done((bf16[256,1280]{1,0:T(8,128)(2,1)}, bf16[256,1280]{1,0:T(8,128)(2,1)S(1)}, u32[]{:S(2)}, u32[]{:S(2)}) %collective-permute-start.4) | collective-permute-done | bytes 655392 | tf_op jit(solution)/shard_map/ppermute | solution.py:24
  22.7 2.1 %collective-permute-done.5.s_x = bf16[256,512]{1,0:T(8,128)(2,1)S(1)} collective-permute-done((bf16[256,512]{1,0:T(8,128)(2,1)}, bf16[256,512]{1,0:T(8,128)(2,1)S(1)}, u32[]{:S(2)}, u32[]{:S(2)}) %collective-permute-start.5) | collective-permute-done | bytes 262176 | tf_op jit(solution)/shard_map/ppermute | solution.py:24
  24.9 2.7 %collective-permute-done.3.s_ahead = bf16[256,512]{1,0:T(8,128)(2,1)S(1)} collective-permute-done((bf16[256,512]{1,0:T(8,128)(2,1)}, bf16[256,512]{1,0:T(8,128)(2,1)S(1)}, u32[]{:S(2)}, u32[]{:S(2)}) %collective-permute-start.3) | collective-permute-done | bytes 262176 | tf_op jit(solution)/shard_map/ppermute | solution.py:24
  27.6 0.2 pack_arrived.1
  27.8 0.6 collective-permute-start.10
  28.4 1.5 %collective-permute-start.7 = (bf16[144,1792]{1,0:T(8,128)(2,1)S(1)}, bf16[144,1792]{1,0:T(8,128)(2,1)S(1)}, u32[]{:S(2)}, u32[]{:S(2)}) collective-permute-start(bf16[144,1792]{1,0:T(8,128)(2,1)S(1)} %get-tuple-element.84), channel_id=1, source_target_pairs={{0,4},{1,5},{2,6},{3,7},{4,8},{5,9},{6,10},{7,11},{8,12},{9,13},{1... | collective-permute-start | bytes 1548296 | tf_op jit(solution)/shard_map/ppermute | solution.py:24
  29.9 2.2 %collective-permute-start.8 = (bf16[112,1792]{1,0:T(8,128)(2,1)S(1)}, bf16[112,1792]{1,0:T(8,128)(2,1)S(1)}, u32[]{:S(2)}, u32[]{:S(2)}) collective-permute-start(bf16[112,1792]{1,0:T(8,128)(2,1)S(1)} %collective-permute-done.2), channel_id=1, source_target_pairs={{0,8},{1,9},{2,10},{3,11},{4,4},{5,5},{6,6},{7,7},{8,16},{9,17},{1... | collective-permute-start | bytes 1204232 | tf_op jit(solution)/shard_map/ppermute | solution.py:24
  32.1 3.9 %collective-permute-start.9 = (bf16[32,1792]{1,0:T(8,128)(2,1)S(1)}, bf16[32,1792]{1,0:T(8,128)(2,1)S(1)}, u32[]{:S(2)}, u32[]{:S(2)}) collective-permute-start(bf16[32,1792]{1,0:T(8,128)(2,1)S(1)} %get-tuple-element.93), channel_id=1, source_target_pairs={{0,24},{1,25},{2,26},{3,27},{4,28},{5,29},{6,30},{7,31},{8,0},{9,1... | collective-permute-start | bytes 344072 | tf_op jit(solution)/shard_map/ppermute | solution.py:24
  36.1 0.1 pack_core.1.refs_1_.refs_26_.refs_8_
  36.2 2.5 %scores_home.1 = (f32[512,768]{1,0:T(8,128)S(1)}, f32[512,768]{1,0:T(8,128)S(1)}, f32[512,768]{1,0:T(8,128)S(1)}, f32[512,768]{1,0:T(8,128)S(1)}, f32[8,512]{1,0:T(8,128)S(1)}, /*index=5*/f32[8,768]{1,0:T(8,128)S(1)}) custom-call(bf16[256,1792]{1,0:T(8,128)(2,1)S(1)} %get-tuple-element.70.refs_0_.refs_25_.refs_7_, ...), custom_call_target="tpu_custom_call" | custom-call | tf_op jit(solution)/shard_map/scores_home/pallas_call | solution.py:446
  38.6 6.9 %collective-permute-done.8.refs_1_.refs_3_.refs_28_ = bf16[112,1792]{1,0:T(8,128)(2,1)S(1)} collective-permute-done((bf16[112,1792]{1,0:T(8,128)(2,1)S(1)}, bf16[112,1792]{1,0:T(8,128)(2,1)S(1)}, u32[]{:S(2)}, u32[]{:S(2)}) %collective-permute-start.8) | collective-permute-done | bytes 401440 | tf_op jit(solution)/shard_map/ppermute | solution.py:24
  45.5 0.3 collective-permute-done.7.refs_0_.refs_2_.refs_27_
  45.8 0.5 collective-permute-start.11
  46.3 1.5 %scores_near.1 = (f32[256,768]{1,0:T(8,128)S(1)}, f32[256,768]{1,0:T(8,128)S(1)}, f32[256,768]{1,0:T(8,128)S(1)}, f32[256,768]{1,0:T(8,128)S(1)}, f32[8,256]{1,0:T(8,128)S(1)}, /*index=5*/f32[4,768]{1,0:T(4,128)S(1)}) custom-call(bf16[144,1792]{1,0:T(8,128)(2,1)S(1)} %collective-permute-done.7.refs_0_.refs_2_.refs_27_, ...), custom_call_target="tpu_custom_call" | custom-call | tf_op jit(solution)/shard_map/scores_near/pallas_call | solution.py:446
  47.8 1.4 %scores_side.1 = (f32[768,256]{1,0:T(8,128)S(1)}, f32[768,256]{1,0:T(8,128)S(1)}, f32[768,256]{1,0:T(8,128)S(1)}, f32[768,256]{1,0:T(8,128)S(1)}, f32[8,768]{1,0:T(8,128)S(1)}, /*index=5*/f32[12,256]{1,0:T(8,128)S(1)}) custom-call(bf16[256,1792]{1,0:T(8,128)(2,1)S(1)} %get-tuple-element.70.refs_0_.refs_25_.refs_7_, ...), custom_call_target="tpu_custom_call" | custom-call | flops 99999997952 | bytes 1000000000 | tf_op jit(solution)/shard_map/scores_side/pallas_call | solution.py:446
  49.2 1.8 %scores_far.1 = (f32[256,1024]{1,0:T(8,128)S(1)}, f32[256,1024]{1,0:T(8,128)S(1)}, f32[256,1024]{1,0:T(8,128)S(1)}, f32[256,1024]{1,0:T(8,128)S(1)}, f32[8,256]{...) custom-call(bf16[144,1792]{1,0:T(8,128)(2,1)S(1)} %collective-permute-done.11.refs_0_.refs_29_, ...), custom_call_target="tpu_custom_call" | custom-call | tf_op jit(solution)/shard_map/scores_far/pallas_call | solution.py:468
  51.0 1.6 %collective-permute-start.14 = (f32[4,1024]{1,0:T(4,128)S(1)}, f32[4,1024]{1,0:T(4,128)S(1)}, u32[]{:S(2)}, u32[]{:S(2)}) collective-permute-start(f32[4,1024]{1,0:T(4,128)S(1)} %get-tuple-element.111.refs_1_), channel_id=1, source_target_pairs={{0,2},{1,3},{2,0},{3,1},{4,6},{5,7},{6,4},{7,5},{8,10},{9,11},{10,... | collective-permute-start | bytes 49160 | tf_op jit(solution)/shard_map/ppermute | solution.py:24
  52.6 2.2 %collective-permute-done.14.refs_3_ = f32[4,1024]{1,0:T(4,128)S(1)} collective-permute-done((f32[4,1024]{1,0:T(4,128)S(1)}, f32[4,1024]{1,0:T(4,128)S(1)}, u32[]{:S(2)}, u32[]{:S(2)}) %collective-permute-start.14) | collective-permute-done | bytes 16416 | tf_op jit(solution)/shard_map/ppermute | solution.py:24
  54.9 0.8 collective-permute-start.15
  55.7 0.4 collective-permute-start.16
  56.0 3.8 %collective-permute-start.17 = (f32[4,512]{1,0:T(4,128)S(1)}, f32[4,512]{1,0:T(4,128)S(1)}, u32[]{:S(2)}, u32[]{:S(2)}) collective-permute-start(f32[4,512]{1,0:T(4,128)S(1)} %get-tuple-element.115), channel_id=1, source_target_pairs={{0,28},{1,29},{2,30},{3,31},{4,8},{5,9},{6,10},{7,11},{8,4},{9,5},... | collective-permute-start | bytes 24584 | tf_op jit(solution)/shard_map/ppermute | solution.py:24
  59.8 2.0 %collective-permute-start.18 = (f32[4,512]{1,0:T(4,128)S(1)}, f32[4,512]{1,0:T(4,128)S(1)}, u32[]{:S(2)}, u32[]{:S(2)}) collective-permute-start(f32[4,512]{1,0:T(4,128)S(1)} %get-tuple-element.116), channel_id=1, source_target_pairs={{0,24},{1,25},{2,26},{3,27},{4,28},{5,29},{6,30},{7,31},{8,16},{9,... | collective-permute-start | bytes 24584 | tf_op jit(solution)/shard_map/ppermute | solution.py:24
  61.8 0.6 collective-permute-done.17.refs_3_
  62.4 2.9 %collective-permute-done.18.refs_4_ = f32[4,512]{1,0:T(4,128)S(1)} collective-permute-done((f32[4,512]{1,0:T(4,128)S(1)}, f32[4,512]{1,0:T(4,128)S(1)}, u32[]{:S(2)}, u32[]{:S(2)}) %collective-permute-start.18) | collective-permute-done | bytes 8224 | tf_op jit(solution)/shard_map/ppermute | solution.py:24
  65.3 0.1 join_blocks.1.refs_24_.refs_6_
  65.3 2.7 %gradients_ahead.1 = (f32[256,256]{1,0:T(8,128)S(1)}, f32[256,256]{1,0:T(8,128)S(1)}, bf16[256,256]{1,0:T(8,128)(2,1)S(1)}, bf16[256,256]{1,0:T(8,128)(2,1)S(1)}...) custom-call(f32[512,768]{1,0:T(8,128)S(1)} %get-tuple-element.80.ref, ...), custom_call_target="tpu_custom_call" | custom-call | tf_op jit(solution)/shard_map/gradients_ahead/pallas_call | solution.py:510
  68.0 0.1 collective-permute-start.20
  68.1 1.0 %collective-permute-start.19 = (bf16[256,256]{1,0:T(8,128)(2,1)S(1)}, bf16[256,256]{1,0:T(8,128)(2,1)S(1)}, u32[]{:S(2)}, u32[]{:S(2)}) collective-permute-start(bf16[256,256]{1,0:T(8,128)(2,1)S(1)} %get-tuple-element.118), channel_id=1, source_target_pairs={{0,2},{1,3},{2,0},{3,1},{4,6},{5,7},{6,4},{7,5},{8,10},{9,11},{10,... | collective-permute-start | bytes 393224 | tf_op jit(solution)/shard_map/ppermute | solution.py:24
  69.1 1.1 %collective-permute-start.22 = (bf16[256,256]{1,0:T(8,128)(2,1)S(1)}, bf16[256,256]{1,0:T(8,128)(2,1)S(1)}, u32[]{:S(2)}, u32[]{:S(2)}) collective-permute-start(bf16[256,256]{1,0:T(8,128)(2,1)S(1)} %get-tuple-element.127), channel_id=1, source_target_pairs={{0,2},{1,3},{2,0},{3,1},{4,6},{5,7},{6,4},{7,5},{8,10},{9,11},{10,... | collective-permute-start | bytes 393224 | tf_op jit(solution)/shard_map/ppermute | solution.py:24
  70.2 0.1 add_convert_fusion
  70.3 1.0 %collective-permute-start.25 = (bf16[256,512]{1,0:T(8,128)(2,1)S(1)}, bf16[256,512]{1,0:T(8,128)(2,1)S(1)}, u32[]{:S(2)}, u32[]{:S(2)}) collective-permute-start(bf16[256,512]{1,0:T(8,128)(2,1)S(1)} %add_convert_fusion), channel_id=1, source_target_pairs={{0,28},{1,29},{2,30},{3,31},{4,0},{5,1},{6,2},{7,3},{8,4},{9,5},{1... | collective-permute-start | bytes 786440 | tf_op jit(solution)/shard_map/ppermute | solution.py:24
  71.3 3.2 %collective-permute-done.19.second = bf16[256,256]{1,0:T(8,128)(2,1)S(1)} collective-permute-done((bf16[256,256]{1,0:T(8,128)(2,1)S(1)}, bf16[256,256]{1,0:T(8,128)(2,1)S(1)}, u32[]{:S(2)}, u32[]{:S(2)}) %collective-permute-start.19) | collective-permute-done | bytes 131104 | tf_op jit(solution)/shard_map/ppermute | solution.py:24
  74.6 1.5 %gradients_home.1 = (f32[256,512]{1,0:T(8,128)S(1)}, bf16[256,512]{1,0:T(8,128)(2,1)S(1)}, f32[512,256]{1,0:T(8,128)S(1)}, bf16[512,256]{1,0:T(8,128)(2,1)S(1)}) custom-call(f32[512,768]{1,0:T(8,128)S(1)} %get-tuple-element.80.refs_0_, f32[512,768]{1,0:T(8,128)S(1)} %get-tuple-element.81.refs_1_, f32[512,768]{1,0:T(8,128)S(1)} %get-tuple-element.82.refs_2_, ...), custom_call_target="tpu_custom_call" | custom-call | tf_op jit(solution)/shard_map/gradients_home/pallas_call | solution.py:534
  76.0 0.8 collective-permute-done.22.second
  76.8 0.9 %collective-permute-start.26 = (bf16[512,256]{1,0:T(8,128)(2,1)S(1)}, bf16[512,256]{1,0:T(8,128)(2,1)S(1)}, u32[]{:S(2)}, u32[]{:S(2)}) collective-permute-start(bf16[512,256]{1,0:T(8,128)(2,1)S(1)} %get-tuple-element.131), channel_id=1, source_target_pairs={{0,2},{1,3},{2,0},{3,1},{4,6},{5,7},{6,4},{7,5},{8,10},{9,11},{10,... | collective-permute-start | bytes 786440 | tf_op jit(solution)/shard_map/ppermute | solution.py:24
  77.9 6.8 %collective-permute-done.26.refs_1_ = bf16[512,256]{1,0:T(8,128)(2,1)S(1)} collective-permute-done((bf16[512,256]{1,0:T(8,128)(2,1)S(1)}, bf16[512,256]{1,0:T(8,128)(2,1)S(1)}, u32[]{:S(2)}, u32[]{:S(2)}) %collective-permute-start.26) | collective-permute-done | bytes 262176 | tf_op jit(solution)/shard_map/ppermute | solution.py:24
  84.7 0.9 %finish_image.1 = f32[256,512]{1,0:T(8,128)} custom-call(f32[256,512]{1,0:T(8,128)S(1)} %get-tuple-element.129.refs_0_, bf16[256,512]{1,0:T(8,128)(2,1)S(1)} %collective-permute-done.24.refs_1_, bf16[256,512]{1,0:T(8,128)(2,1)S(1)} %collective-permute-done.25.refs_2_), custom_call_target="tpu_custom_call" | custom-call | flops 3000000000 | bytes 30000000 | tf_op jit(solution)/shard_map/finish_image/pallas_call | solution.py:566
  85.6 1.0 %finish_text.1 = f32[256,512]{1,0:T(8,128)} custom-call(f32[512,256]{1,0:T(8,128)S(1)} %get-tuple-element.134.refs_0_, bf16[512,256]{1,0:T(8,128)(2,1)S(1)} %collective-permute-done.26.refs_1_, bf16[256,256]{1,0:T(8,128)(2,1)S(1)} %collective-permute-done.21.refs_2_, bf16[256,256]{1,0:T(8,128)(2,1)S(1)} %collective-permute-done.23.refs_3_), custom_call_target="tpu_custom_call" | custom-call | tf_op jit(solution)/shard_map/finish_text/pallas_call | solution.py:566
  (31 shorter events, 0.4 us)
Async XLA Ops:
  0.6 35.4 %copy-start = (bf16[256,1280]{1,0:T(8,128)(2,1)S(1)}, bf16[256,1280]{1,0:T(8,128)(2,1)}, u32[]{:S(2)}) copy-start(bf16[256,1280]{1,0:T(8,128)(2,1)} %second.3) | copy-start | bytes 1966084
  0.6 10.4 %collective-permute-start.1 = (bf16[256,1280]{1,0:T(8,128)(2,1)}, bf16[256,1280]{1,0:T(8,128)(2,1)S(1)}, u32[]{:S(2)}, u32[]{:S(2)}) collective-permute-start(bf16[256,1280]{1,0:T(8,128)(2,1)} %second.2), channel_id=1, source_target_pairs={{0,1},{1,0},{2,3},{3,2},{4,5},{5,4},{6,7},{7,6},{8,9},{9,8},{10,11... | collective-permute-start | bytes 1966088 | tf_op jit(solution)/shard_map/ppermute | solution.py:24
  1.2 20.1 %collective-permute-start.6 = (bf16[256,1280]{1,0:T(8,128)(2,1)}, bf16[256,1280]{1,0:T(8,128)(2,1)S(1)}, u32[]{:S(2)}, u32[]{:S(2)}) collective-permute-start(bf16[256,1280]{1,0:T(8,128)(2,1)} %second.3), channel_id=1, source_target_pairs={{0,2},{1,3},{2,0},{3,1},{4,6},{5,7},{6,4},{7,5},{8,10},{9,11},{10,... | collective-permute-start | bytes 1966088 | tf_op jit(solution)/shard_map/ppermute | solution.py:24
  3.7 19.0 %collective-permute-start.4 = (bf16[256,1280]{1,0:T(8,128)(2,1)}, bf16[256,1280]{1,0:T(8,128)(2,1)S(1)}, u32[]{:S(2)}, u32[]{:S(2)}) collective-permute-start(bf16[256,1280]{1,0:T(8,128)(2,1)} %second.3), channel_id=1, source_target_pairs={{0,24},{1,25},{2,26},{3,27},{4,28},{5,29},{6,30},{7,31},{8,0},{9,1... | collective-permute-start | bytes 1966088 | tf_op jit(solution)/shard_map/ppermute | solution.py:24
  7.3 3.8 %collective-permute-start = (bf16[256,512]{1,0:T(8,128)(2,1)}, bf16[256,512]{1,0:T(8,128)(2,1)S(1)}, u32[]{:S(2)}, u32[]{:S(2)}) collective-permute-start(bf16[256,512]{1,0:T(8,128)(2,1)} %first.2), channel_id=1, source_target_pairs={{0,1},{1,0},{2,3},{3,2},{4,5},{5,4},{6,7},{7,6},{8,9},{9,8},{10,11... | collective-permute-start | bytes 786440 | tf_op jit(solution)/shard_map/ppermute | solution.py:24
  7.3 1.1 %copy-start.1 = (bf16[256,1280]{1,0:T(8,128)(2,1)S(1)}, bf16[256,1280]{1,0:T(8,128)(2,1)}, u32[]{:S(2)}) copy-start(bf16[256,1280]{1,0:T(8,128)(2,1)} %second.2) | copy-start | bytes 1966084
  8.4 0.9 %copy-start.2 = (bf16[256,512]{1,0:T(8,128)(2,1)S(1)}, bf16[256,512]{1,0:T(8,128)(2,1)}, u32[]{:S(2)}) copy-start(bf16[256,512]{1,0:T(8,128)(2,1)} %first.2) | copy-start | bytes 786436
  9.4 26.7 %copy-start.3 = (bf16[256,512]{1,0:T(8,128)(2,1)S(1)}, bf16[256,512]{1,0:T(8,128)(2,1)}, u32[]{:S(2)}) copy-start(bf16[256,512]{1,0:T(8,128)(2,1)} %first.3) | copy-start | bytes 786436
  9.5 11.8 %collective-permute-start.2 = (bf16[112,1792]{1,0:T(8,128)(2,1)S(1)}, bf16[112,1792]{1,0:T(8,128)(2,1)S(1)}, u32[]{:S(2)}, u32[]{:S(2)}) collective-permute-start(bf16[112,1792]{1,0:T(8,128)(2,1)S(1)} %get-tuple-element.74), channel_id=1, source_target_pairs={{0,4},{1,5},{2,6},{3,7},{4,0},{5,1},{6,2},{7,3},{8,12},{9,13},{10,... | collective-permute-start | bytes 1204232 | tf_op jit(solution)/shard_map/ppermute | solution.py:24
  11.1 13.8 %collective-permute-start.5 = (bf16[256,512]{1,0:T(8,128)(2,1)}, bf16[256,512]{1,0:T(8,128)(2,1)S(1)}, u32[]{:S(2)}, u32[]{:S(2)}) collective-permute-start(bf16[256,512]{1,0:T(8,128)(2,1)} %first.3), channel_id=1, source_target_pairs={{0,2},{1,3},{2,0},{3,1},{4,6},{5,7},{6,4},{7,5},{8,10},{9,11},{10,... | collective-permute-start | bytes 786440 | tf_op jit(solution)/shard_map/ppermute | solution.py:24
  11.6 16.0 %collective-permute-start.3 = (bf16[256,512]{1,0:T(8,128)(2,1)}, bf16[256,512]{1,0:T(8,128)(2,1)S(1)}, u32[]{:S(2)}, u32[]{:S(2)}) collective-permute-start(bf16[256,512]{1,0:T(8,128)(2,1)} %first.3), channel_id=1, source_target_pairs={{0,24},{1,25},{2,26},{3,27},{4,28},{5,29},{6,30},{7,31},{8,0},{9,1... | collective-permute-start | bytes 786440 | tf_op jit(solution)/shard_map/ppermute | solution.py:24
  27.8 20.0 %collective-permute-start.10 = (bf16[224,1792]{1,0:T(8,128)(2,1)S(1)}, bf16[224,1792]{1,0:T(8,128)(2,1)S(1)}, u32[]{:S(2)}, u32[]{:S(2)}) collective-permute-start(bf16[224,1792]{1,0:T(8,128)(2,1)S(1)} %get-tuple-element.94), channel_id=1, source_target_pairs={{0,2},{1,3},{2,0},{3,1},{4,6},{5,7},{6,4},{7,5},{8,10},{9,11},{10,... | collective-permute-start | bytes 2408456 | tf_op jit(solution)/shard_map/ppermute | solution.py:24
  28.4 17.4 %collective-permute-start.7 = (bf16[144,1792]{1,0:T(8,128)(2,1)S(1)}, bf16[144,1792]{1,0:T(8,128)(2,1)S(1)}, u32[]{:S(2)}, u32[]{:S(2)}) collective-permute-start(bf16[144,1792]{1,0:T(8,128)(2,1)S(1)} %get-tuple-element.84), channel_id=1, source_target_pairs={{0,4},{1,5},{2,6},{3,7},{4,8},{5,9},{6,10},{7,11},{8,12},{9,13},{1... | collective-permute-start | bytes 1548296 | tf_op jit(solution)/shard_map/ppermute | solution.py:24
  29.9 15.6 %collective-permute-start.8 = (bf16[112,1792]{1,0:T(8,128)(2,1)S(1)}, bf16[112,1792]{1,0:T(8,128)(2,1)S(1)}, u32[]{:S(2)}, u32[]{:S(2)}) collective-permute-start(bf16[112,1792]{1,0:T(8,128)(2,1)S(1)} %collective-permute-done.2), channel_id=1, source_target_pairs={{0,8},{1,9},{2,10},{3,11},{4,4},{5,5},{6,6},{7,7},{8,16},{9,17},{1... | collective-permute-start | bytes 1204232 | tf_op jit(solution)/shard_map/ppermute | solution.py:24
  32.1 15.6 %collective-permute-start.9 = (bf16[32,1792]{1,0:T(8,128)(2,1)S(1)}, bf16[32,1792]{1,0:T(8,128)(2,1)S(1)}, u32[]{:S(2)}, u32[]{:S(2)}) collective-permute-start(bf16[32,1792]{1,0:T(8,128)(2,1)S(1)} %get-tuple-element.93), channel_id=1, source_target_pairs={{0,24},{1,25},{2,26},{3,27},{4,28},{5,29},{6,30},{7,31},{8,0},{9,1... | collective-permute-start | bytes 344072 | tf_op jit(solution)/shard_map/ppermute | solution.py:24
  45.8 3.4 %collective-permute-start.12 = (bf16[112,1792]{1,0:T(8,128)(2,1)S(1)}, bf16[112,1792]{1,0:T(8,128)(2,1)S(1)}, u32[]{:S(2)}, u32[]{:S(2)}) collective-permute-start(bf16[112,1792]{1,0:T(8,128)(2,1)S(1)} %collective-permute-done.8.refs_1_.refs_3_.refs_28_), channel_id=1, source_target_pairs={{0,1},{1,0},{2,3},{3,2},{4,5},{5,4},{6,7},{7,6},{8,9},{9,8},{10,11... | collective-permute-start | bytes 1204232 | tf_op jit(solution)/shard_map/ppermute | solution.py:24
  45.8 3.4 %collective-permute-start.11 = (bf16[144,1792]{1,0:T(8,128)(2,1)S(1)}, bf16[144,1792]{1,0:T(8,128)(2,1)S(1)}, u32[]{:S(2)}, u32[]{:S(2)}) collective-permute-start(bf16[144,1792]{1,0:T(8,128)(2,1)S(1)} %collective-permute-done.7.refs_0_.refs_2_.refs_27_), channel_id=1, source_target_pairs={{0,1},{1,0},{2,3},{3,2},{4,5},{5,4},{6,7},{7,6},{8,9},{9,8},{10,11... | collective-permute-start | bytes 1548296 | tf_op jit(solution)/shard_map/ppermute | solution.py:24
  51.0 1.6 %collective-permute-start.13 = (f32[4,1024]{1,0:T(4,128)S(1)}, f32[4,1024]{1,0:T(4,128)S(1)}, u32[]{:S(2)}, u32[]{:S(2)}) collective-permute-start(f32[4,1024]{1,0:T(4,128)S(1)} %get-tuple-element.110.refs_0_), channel_id=1, source_target_pairs={{0,1},{1,0},{2,3},{3,2},{4,5},{5,4},{6,7},{7,6},{8,9},{9,8},{10,11... | collective-permute-start | bytes 49160 | tf_op jit(solution)/shard_map/ppermute | solution.py:24
  51.0 3.8 %collective-permute-start.14 = (f32[4,1024]{1,0:T(4,128)S(1)}, f32[4,1024]{1,0:T(4,128)S(1)}, u32[]{:S(2)}, u32[]{:S(2)}) collective-permute-start(f32[4,1024]{1,0:T(4,128)S(1)} %get-tuple-element.111.refs_1_), channel_id=1, source_target_pairs={{0,2},{1,3},{2,0},{3,1},{4,6},{5,7},{6,4},{7,5},{8,10},{9,11},{10,... | collective-permute-start | bytes 49160 | tf_op jit(solution)/shard_map/ppermute | solution.py:24
  54.9 6.9 %collective-permute-start.15 = (f32[4,512]{1,0:T(4,128)S(1)}, f32[4,512]{1,0:T(4,128)S(1)}, u32[]{:S(2)}, u32[]{:S(2)}) collective-permute-start(f32[4,512]{1,0:T(4,128)S(1)} %get-tuple-element.113), channel_id=1, source_target_pairs={{0,4},{1,5},{2,6},{3,7},{4,0},{5,1},{6,2},{7,3},{8,12},{9,13},{10,... | collective-permute-start | bytes 24584 | tf_op jit(solution)/shard_map/ppermute | solution.py:24
  55.7 6.2 %collective-permute-start.16 = (f32[4,512]{1,0:T(4,128)S(1)}, f32[4,512]{1,0:T(4,128)S(1)}, u32[]{:S(2)}, u32[]{:S(2)}) collective-permute-start(f32[4,512]{1,0:T(4,128)S(1)} %get-tuple-element.114), channel_id=1, source_target_pairs={{0,8},{1,9},{2,10},{3,11},{4,12},{5,13},{6,14},{7,15},{8,0},{9,1},... | collective-permute-start | bytes 24584 | tf_op jit(solution)/shard_map/ppermute | solution.py:24
  56.0 6.3 %collective-permute-start.17 = (f32[4,512]{1,0:T(4,128)S(1)}, f32[4,512]{1,0:T(4,128)S(1)}, u32[]{:S(2)}, u32[]{:S(2)}) collective-permute-start(f32[4,512]{1,0:T(4,128)S(1)} %get-tuple-element.115), channel_id=1, source_target_pairs={{0,28},{1,29},{2,30},{3,31},{4,8},{5,9},{6,10},{7,11},{8,4},{9,5},... | collective-permute-start | bytes 24584 | tf_op jit(solution)/shard_map/ppermute | solution.py:24
  59.8 5.4 %collective-permute-start.18 = (f32[4,512]{1,0:T(4,128)S(1)}, f32[4,512]{1,0:T(4,128)S(1)}, u32[]{:S(2)}, u32[]{:S(2)}) collective-permute-start(f32[4,512]{1,0:T(4,128)S(1)} %get-tuple-element.116), channel_id=1, source_target_pairs={{0,24},{1,25},{2,26},{3,27},{4,28},{5,29},{6,30},{7,31},{8,16},{9,... | collective-permute-start | bytes 24584 | tf_op jit(solution)/shard_map/ppermute | solution.py:24
  68.0 2.2 %collective-permute-start.20 = (bf16[256,512]{1,0:T(8,128)(2,1)S(1)}, bf16[256,512]{1,0:T(8,128)(2,1)S(1)}, u32[]{:S(2)}, u32[]{:S(2)}) collective-permute-start(bf16[256,512]{1,0:T(8,128)(2,1)S(1)} %get-tuple-element.120), channel_id=1, source_target_pairs={{0,1},{1,0},{2,3},{3,2},{4,5},{5,4},{6,7},{7,6},{8,9},{9,8},{10,11... | collective-permute-start | bytes 786440 | tf_op jit(solution)/shard_map/ppermute | solution.py:24
  68.1 6.4 %collective-permute-start.19 = (bf16[256,256]{1,0:T(8,128)(2,1)S(1)}, bf16[256,256]{1,0:T(8,128)(2,1)S(1)}, u32[]{:S(2)}, u32[]{:S(2)}) collective-permute-start(bf16[256,256]{1,0:T(8,128)(2,1)S(1)} %get-tuple-element.118), channel_id=1, source_target_pairs={{0,2},{1,3},{2,0},{3,1},{4,6},{5,7},{6,4},{7,5},{8,10},{9,11},{10,... | collective-permute-start | bytes 393224 | tf_op jit(solution)/shard_map/ppermute | solution.py:24
  69.1 7.7 %collective-permute-start.22 = (bf16[256,256]{1,0:T(8,128)(2,1)S(1)}, bf16[256,256]{1,0:T(8,128)(2,1)S(1)}, u32[]{:S(2)}, u32[]{:S(2)}) collective-permute-start(bf16[256,256]{1,0:T(8,128)(2,1)S(1)} %get-tuple-element.127), channel_id=1, source_target_pairs={{0,2},{1,3},{2,0},{3,1},{4,6},{5,7},{6,4},{7,5},{8,10},{9,11},{10,... | collective-permute-start | bytes 393224 | tf_op jit(solution)/shard_map/ppermute | solution.py:24
  70.3 14.4 %collective-permute-start.25 = (bf16[256,512]{1,0:T(8,128)(2,1)S(1)}, bf16[256,512]{1,0:T(8,128)(2,1)S(1)}, u32[]{:S(2)}, u32[]{:S(2)}) collective-permute-start(bf16[256,512]{1,0:T(8,128)(2,1)S(1)} %add_convert_fusion), channel_id=1, source_target_pairs={{0,28},{1,29},{2,30},{3,31},{4,0},{5,1},{6,2},{7,3},{8,4},{9,5},{1... | collective-permute-start | bytes 786440 | tf_op jit(solution)/shard_map/ppermute | solution.py:24
  74.5 11.1 %collective-permute-start.21 = (bf16[256,256]{1,0:T(8,128)(2,1)S(1)}, bf16[256,256]{1,0:T(8,128)(2,1)S(1)}, u32[]{:S(2)}, u32[]{:S(2)}) collective-permute-start(bf16[256,256]{1,0:T(8,128)(2,1)S(1)} %add_text.2), channel_id=1, source_target_pairs={{0,8},{1,9},{2,10},{3,11},{4,12},{5,13},{6,14},{7,15},{8,16},{9,17... | collective-permute-start | bytes 393224 | tf_op jit(solution)/shard_map/ppermute | solution.py:24
  76.8 7.9 %collective-permute-start.26 = (bf16[512,256]{1,0:T(8,128)(2,1)S(1)}, bf16[512,256]{1,0:T(8,128)(2,1)S(1)}, u32[]{:S(2)}, u32[]{:S(2)}) collective-permute-start(bf16[512,256]{1,0:T(8,128)(2,1)S(1)} %get-tuple-element.131), channel_id=1, source_target_pairs={{0,2},{1,3},{2,0},{3,1},{4,6},{5,7},{6,4},{7,5},{8,10},{9,11},{10,... | collective-permute-start | bytes 786440 | tf_op jit(solution)/shard_map/ppermute | solution.py:24
  77.8 6.9 %collective-permute-start.24 = (bf16[256,512]{1,0:T(8,128)(2,1)S(1)}, bf16[256,512]{1,0:T(8,128)(2,1)S(1)}, u32[]{:S(2)}, u32[]{:S(2)}) collective-permute-start(bf16[256,512]{1,0:T(8,128)(2,1)S(1)} %get-tuple-element.130), channel_id=1, source_target_pairs={{0,1},{1,0},{2,3},{3,2},{4,5},{5,4},{6,7},{7,6},{8,9},{9,8},{10,11... | collective-permute-start | bytes 786440 | tf_op jit(solution)/shard_map/ppermute | solution.py:24
  77.8 7.8 %collective-permute-start.23 = (bf16[256,256]{1,0:T(8,128)(2,1)S(1)}, bf16[256,256]{1,0:T(8,128)(2,1)S(1)}, u32[]{:S(2)}, u32[]{:S(2)}) collective-permute-start(bf16[256,256]{1,0:T(8,128)(2,1)S(1)} %add_text.3), channel_id=1, source_target_pairs={{0,8},{1,9},{2,10},{3,11},{4,12},{5,13},{6,14},{7,15},{8,16},{9,17... | collective-permute-start | bytes 393224 | tf_op jit(solution)/shard_map/ppermute | solution.py:24
